TPU v7x, 32 devices: a whole 2x2x4 slice. The times are simulated.
32 devices in a mesh: blk: 4 (over y, x), tile: 8 (over z, core).
Axes of the slice: x: 2, y: 2, z: 4, core: 2. Of those that a mesh axis runs over, the one named last changes fastest.
Arguments:
- left_rows: bfloat16 [1024, 49152], P('blk', 'tile'), may hold values from -0.1875 to 0.1875
- right_rows: bfloat16 [1024, 4096], P('blk', 'tile'), may hold values from -6 to 6
- row_weight: float32 [1024], P('blk'), may hold values from 0.25 to 4
- coupling: float32 [1024], P('blk'), may hold values from -6 to 6
- assign: int32 [8], replicated, may hold values from 0 to 3, as said below
- orders: int32 [8], replicated, may hold values from 42 to 214, as said below
- offsets: int32 [8], replicated, may hold values from 0 to 214, as said below
Outputs:
- schur_band: bfloat16 [4096, 49152], P('blk', 'tile')
Inputs may be any that keep to these rules, and one draw needn't show every extreme that they name: `assign`: each blk index names exactly 2 blocks. The orders of the blocks that one blk index names sum to at most 256, and to exactly 256 for some index in every draw. offsets[b] is the sum of the orders of the blocks before b in the list that name the same blk index.
All inputs are finite; a program needn't handle non-finite values.
Results may differ from a plain program's by a relative error of at most 0.013.
Values may be sent and summed in bfloat16 or wider, within the bound.
No kernel may reach another device: no remote copies, remote signals or barrier semaphores. Data moves between devices by JAX's collectives and lax.ppermute only.
A program may use at most 128 MiB of HBM per device.

v0:
```python
import jax
import jax.numpy as jnp
from jax import lax
from jax.sharding import PartitionSpec as P

BAND = 4096


def weigh_rows(right_rows, row_weight, coupling, member, orders):
    right_wide = right_rows.astype(jnp.float32)
    block_sums = jnp.dot(member.T, coupling[:, None] * right_wide, precision=lax.Precision.HIGHEST)
    block_terms = block_sums / jnp.sqrt(orders.astype(jnp.float32))[:, None]
    spread_back = jnp.dot(member, block_terms, precision=lax.Precision.HIGHEST)
    is_live = jnp.sum(member, axis=1, keepdims=True)
    return (is_live * row_weight[:, None] * right_wide + coupling[:, None] * spread_back).astype(
        jnp.bfloat16
    )


def contract(cols_piece, slab_left):
    return lax.dot_general(
        cols_piece, slab_left, (((0,), (0,)), ((), ())), preferred_element_type=jnp.float32
    )


def shards(left_rows, right_rows, row_weight, coupling, assign, orders, offsets):
    height = left_rows.shape[0]
    my_index = lax.axis_index("blk")
    row_ids = lax.broadcasted_iota(jnp.int32, (height, assign.shape[0]), 0)
    member = (
        (assign[None, :] == my_index)
        & (row_ids >= offsets[None, :])
        & (row_ids < offsets[None, :] + orders[None, :])
    ).astype(jnp.float32)
    weighted = weigh_rows(right_rows, row_weight, coupling, member, orders)
    weighted_all = lax.all_gather(weighted, "tile", axis=1, tiled=True)
    blk_count = lax.axis_size("blk")
    my_columns = lax.all_to_all(weighted_all, "blk", split_axis=1, concat_axis=0, tiled=True)
    initial = jnp.zeros((BAND // blk_count, left_rows.shape[1]), jnp.float32)
    running = initial
    slab_left = lax.all_gather(left_rows, "blk", axis=0, tiled=True)
    for which in range(slab_left.shape[0] // height):
        cols_piece = lax.dynamic_slice_in_dim(my_columns, which * height, height, 0)
        slab_term = contract(cols_piece, slab_left[which * height : (which + 1) * height])
        slab_term = lax.optimization_barrier(slab_term.astype(jnp.bfloat16)).astype(jnp.float32)
        running = running + slab_term
    return running.astype(jnp.bfloat16)


def solution(mesh):
    return jax.shard_map(
        shards,
        mesh=mesh,
        in_specs=(P("blk", "tile"), P("blk", "tile"), P("blk"), P("blk"), P(), P(), P()),
        out_specs=P("blk", "tile"),
        check_vma=False,
    )
```

profile of v0, /device:TPU:0, one launch (start us, length us, event | category | flops | bytes accessed | tf_op | source)
XLA Modules:
  0.0 246.9 jit_solution(16281396031844603382)
XLA Ops:
  6.5 0.0 all-gather.3.cloned.1.call-start
  6.5 0.7 convert_sqrt_fusion
  7.2 0.7 add.16
  7.9 0.7 broadcast_compare_fusion
  8.5 0.7 convert_reduce_fusion
  9.3 0.7 mul.26
  10.0 1.3 convolution_divide_fusion
  11.3 2.2 fusion.5
  13.5 0.0 all-gather.3.cloned.1.call-update
  13.5 0.0 all-gather.5.cloned.1.call-start
  13.5 0.7 all-gather.5.cloned.1.call-update
  14.2 31.2 %all-gather.3.cloned.1.call-done = bf16[256,4096]{1,0:T(8,128)(2,1)} async-done(((bf16[256,512]{1,0:T(8,128)(2,1)}), bf16[256,4096]{1,0:T(8,128)(2,1)}) %all-gather.3.cloned.1.call-update) | async-done | bytes 2097168 | tf_op jit(solution)/shard_map/all_gather | solution.py:36
  45.4 1.8 copy.12
  47.2 45.7 %all_to_all.16 = bf16[256,4,1024]{2,0,1:T(8,128)(2,1)S(1)} all-to-all(bf16[256,4,1024]{2,0,1:T(8,128)(2,1)S(1)} %bitcast.22), channel_id=1, replica_groups=mesh['blk'=4,'tile'=8] {'blk'}, dimensions={1} | all-to-all | bytes 4194304 | tf_op jit(solution)/shard_map/all_to_all | solution.py:38
  92.9 90.7 %all-gather.5.cloned.1.call-done = bf16[1024,6144]{1,0:T(8,128)(2,1)} async-done(((bf16[256,6144]{1,0:T(8,128)(2,1)}), bf16[1024,6144]{1,0:T(8,128)(2,1)}) %all-gather.5.cloned.1.call-update) | async-done | bytes 12582928 | tf_op jit(solution)/shard_map/all_gather | solution.py:41
  183.6 8.5 %convolution_convert_fusion = bf16[1024,6144]{1,0:T(8,128)(2,1)} fusion(bf16[1024,6144]{1,0:T(8,128)(2,1)} %all-gather.5.cloned.1.call-done, bf16[4,256,1024]{2,1,0:T(8,128)(2,1)S(1)} %bitcast.18), kind=kOutput, calls=%fused_computation.1 | convolution fusion | flops 3227516928 | bytes 16252928 | tf_op jit(solution)/shard_map/dot_general | solution.py:21
  192.1 8.2 %convolution_convert_fusion.1 = bf16[1024,6144]{1,0:T(8,128)(2,1)} fusion(bf16[1024,6144]{1,0:T(8,128)(2,1)} %all-gather.5.cloned.1.call-done, bf16[4,256,1024]{2,1,0:T(8,128)(2,1)S(1)} %bitcast.19), kind=kOutput, calls=%fused_computation.2 | convolution fusion | flops 3227516928 | bytes 16252928 | tf_op jit(solution)/shard_map/dot_general | solution.py:21
  200.3 8.2 %convolution_convert_fusion.3 = bf16[1024,6144]{1,0:T(8,128)(2,1)} fusion(bf16[1024,6144]{1,0:T(8,128)(2,1)} %all-gather.5.cloned.1.call-done, bf16[4,256,1024]{2,1,0:T(8,128)(2,1)S(1)} %bitcast.20), kind=kOutput, calls=%fused_computation.4 | convolution fusion | flops 3227516928 | bytes 16252928 | tf_op jit(solution)/shard_map/dot_general | solution.py:21
  208.4 8.3 %convolution_convert_fusion.2 = bf16[1024,6144]{1,0:T(8,128)(2,1)} fusion(bf16[1024,6144]{1,0:T(8,128)(2,1)} %all-gather.5.cloned.1.call-done, bf16[4,256,1024]{2,1,0:T(8,128)(2,1)S(1)} %bitcast.21), kind=kOutput, calls=%fused_computation.3 | convolution fusion | flops 3227516928 | bytes 16252928 | tf_op jit(solution)/shard_map/dot_general | solution.py:21
  216.7 23.4 %add_convert_fusion = bf16[1024,6144]{1,0:T(8,128)(2,1)} fusion(bf16[1024,6144]{1,0:T(8,128)(2,1)} %convolution_convert_fusion, bf16[1024,6144]{1,0:T(8,128)(2,1)} %convolution_convert_fusion.1, bf16[1024,6144]{1,0:T(8,128)(2,1)} %convolution_convert_fusion.2, bf16[1024,6144]{1,0:T(8,128)(2,1)} %convolution_convert_fusion.3), kind=kLoop, calls=%fused_computation | loop fusion | flops 50331648 | bytes 62914560 | tf_op jit(solution)/shard_map/convert_element_type | solution.py:47
Async XLA Ops:
  6.5 38.9 %all-gather.3.cloned.1.call-start = ((), (), s32[]{:S(2)}) async-start(), calls=%async_computation.1 | async-start | bytes 2359296 | tf_op jit(solution)/shard_map/all_gather | solution.py:36
  13.5 170.1 %all-gather.5.cloned.1.call-start = ((), (), s32[]{:S(2)}) async-start(), calls=%async_computation.2 | async-start | bytes 15728640 | tf_op jit(solution)/shard_map/all_gather | solution.py:41
Sparse Core Ops, SparseCore 0:
  13.6 31.7 all-gather.2
  47.3 136.2 all-gather.4
where the time goes:
time: 247 us
  waiting for transfers between devices  123 us (50%)
  blocking collectives  45.7 us (19%)
  matrix products  36.6 us (15%)
  other arithmetic  26.8 us (11%)
  between operations  13.4 us (5%)
    all_gather x1, waiting for transfers between devices, shards(): slab_left = lax.all_gather(left_rows, 'blk', axis=0, tiled=True)  90.7 us
    all_to_all x1, blocking collectives, shards(): lax.all_to_all(weighted_all, 'blk', split_axis=1, concat_axis=0, tiled=True)  45.7 us
    dot_general x4, matrix products, contract(): lax.dot_general(cols_piece, slab_left, (((0,), (0,)), ((), ())), preferre...  33.2 us
    all_gather x1, waiting for transfers between devices, shards(): weighted_all = lax.all_gather(weighted, 'tile', axis=1, tiled=True)  31.2 us
    convert_element_type x1, other arithmetic, shards(): return running.astype(jnp.bfloat16)  23.4 us
  transfers between devices with their start and end apart: 2, of which 2 were waited for; matrix products, arithmetic and copies ran while one was open for 1% of the time, Pallas kernels for 0%

commit v1 on v0

v1 whole, which is shorter than its diff:
```python
import jax
import jax.numpy as jnp
from jax import lax
from jax.experimental import pallas as pl
from jax.experimental.pallas import tpu as pltpu
from jax.sharding import PartitionSpec as P

UNITS = 12
CHUNKS = (2, 4, 5, 1)


def weigh_rows(right_rows, row_weight, coupling, member, orders):
    right_wide = right_rows.astype(jnp.float32)
    block_sums = jnp.dot(member.T, coupling[:, None] * right_wide, precision=lax.Precision.HIGHEST)
    block_terms = block_sums / jnp.sqrt(orders.astype(jnp.float32))[:, None]
    spread_back = jnp.dot(member, block_terms, precision=lax.Precision.HIGHEST)
    is_live = jnp.sum(member, axis=1, keepdims=True)
    return (is_live * row_weight[:, None] * right_wide + coupling[:, None] * spread_back).astype(
        jnp.bfloat16
    )


def on_ring(place, count):
    half = count // 2
    return jnp.where(place < half, place, count + half - 1 - place)


def ring_shift(count, by):
    half = count // 2
    ring = list(range(half)) + list(range(count - 1, half - 1, -1))
    return [(ring[p], ring[(p + by) % count]) for p in range(count)]


def exchange_weighted(weighted):
    blks, tiles = lax.axis_size("blk"), lax.axis_size("tile")
    ring_place = on_ring(lax.axis_index("blk"), blks)
    rows = lax.all_to_all(weighted, "tile", split_axis=0, concat_axis=1, tiled=True)
    width = rows.shape[1] // blks
    parts = []
    for step in range(blks):
        target = on_ring(lax.rem(ring_place + step, blks), blks)
        part = lax.dynamic_slice_in_dim(rows, target * width, width, 1)
        parts.append(lax.ppermute(part, "blk", ring_shift(blks, step)) if step else part)
    held = jnp.stack(parts)
    axis, bit = 0, tiles // 2
    while bit:
        other = lax.ppermute(held, "tile", [(t, t ^ bit) for t in range(tiles)])
        upper = (lax.axis_index("tile") & bit) != 0
        held = jnp.stack(
            [jnp.where(upper, other, held), jnp.where(upper, held, other)], axis=axis
        )
        axis, bit = axis + 1, bit // 2
    held = held.reshape((tiles, blks, rows.shape[0], width))
    return held.transpose((3, 1, 0, 2)).reshape((width, blks * weighted.shape[0]))


def gather_left(piece):
    blks = lax.axis_size("blk")
    forth, back = ring_shift(blks, 1), ring_shift(blks, -1)
    low, high = [piece], [piece]
    for _ in range(blks // 2 - 1):
        low.append(lax.ppermute(low[-1], "blk", forth))
        high.append(lax.ppermute(high[-1], "blk", back))
    half = piece.shape[0] // 2
    far = [lax.ppermute(low[-1][:half], "blk", forth), lax.ppermute(high[-1][half:], "blk", back)]
    return low[1:] + far + high[:0:-1]


def band_kernel(*refs):
    weights, pieces, out = refs[0], refs[1:-1], refs[-1]
    stacked = jnp.concatenate([piece[...] for piece in pieces], axis=0)
    out[...] = jnp.dot(weights[...], stacked, preferred_element_type=jnp.float32).astype(out.dtype)


def band_kernel_onto(*refs):
    band_kernel(*refs[1:])


def band_chunk(band, weights, left_rows, others, first, unit):
    height, columns = left_rows.shape
    width = others[0].shape[1]
    rows, depth = weights.shape
    here = lambda j: (0, first + j)
    specs = [pl.BlockSpec((rows, depth), lambda j: (0, 0)), pl.BlockSpec((height, unit), here)]
    specs += [pl.BlockSpec((o.shape[0], unit), lambda j: (0, j)) for o in others]
    operands = [weights, left_rows, *others]
    kernel, aliases = band_kernel, {}
    if band is not None:
        specs.insert(0, pl.BlockSpec(memory_space=pl.ANY))
        operands.insert(0, band)
        kernel, aliases = band_kernel_onto, {0: 0}
    return pl.pallas_call(
        kernel,
        grid=(width // unit,),
        in_specs=specs,
        out_specs=pl.BlockSpec((rows, unit), here),
        out_shape=jax.ShapeDtypeStruct((rows, columns), jnp.bfloat16),
        input_output_aliases=aliases,
        compiler_params=pltpu.CompilerParams(vmem_limit_bytes=32 * 1024 * 1024),
        cost_estimate=pl.CostEstimate(
            flops=2 * rows * depth * width,
            bytes_accessed=2 * (rows * depth + depth * width + rows * width),
            transcendentals=0,
        ),
    )(*operands)


def shards(left_rows, right_rows, row_weight, coupling, assign, orders, offsets):
    height, columns = left_rows.shape
    my_index = lax.axis_index("blk")
    unit = columns // UNITS
    gathered, start = [], 0
    for size in CHUNKS:
        piece = left_rows[:, start * unit : (start + size) * unit]
        gathered.append((start, gather_left(piece)))
        start += size

    row_ids = lax.broadcasted_iota(jnp.int32, (height, assign.shape[0]), 0)
    member = (
        (assign[None, :] == my_index)
        & (row_ids >= offsets[None, :])
        & (row_ids < offsets[None, :] + orders[None, :])
    ).astype(jnp.float32)
    weighted = weigh_rows(right_rows, row_weight, coupling, member, orders)
    weights = exchange_weighted(weighted)

    band = None
    for start, others in gathered:
        band = band_chunk(band, weights, left_rows, others, start, unit)
    return band


def solution(mesh):
    return jax.shard_map(
        shards,
        mesh=mesh,
        in_specs=(P("blk", "tile"), P("blk", "tile"), P("blk"), P("blk"), P(), P(), P()),
        out_specs=P("blk", "tile"),
        check_vma=False,
    )
```

time: 247 us -> 173 us (0.70)
  blocking collectives: 45.7 us -> 0 us
  waiting for transfers between devices: 123 us -> 80.4 us
  matrix products: 36.6 us -> 3.49 us
  starting transfers between devices: 0.04 us -> 28.8 us
  Pallas kernels: 0 us -> 24.3 us
  local copies, waits for them, and re-layouts: 1.76 us -> 25.4 us
  other arithmetic: 26.8 us -> 9.31 us
  between operations: 13.4 us -> 0.15 us
    all_gather x2 -> x0, waiting for transfers between devices: 122 us -> none  [the longest x1 90.7 us: shards(): slab_left = lax.all_gather(left_rows, 'blk', axis=0, tiled=True)]
    ppermute x0 -> x22, waiting for transfers between devices: none -> 70.7 us  [the longest x4 34 us: gather_left(): high.append(lax.ppermute(high[-1], 'blk', back))]
    all_to_all x1 -> x0, blocking collectives: 45.7 us -> none  [shards(): lax.all_to_all(weighted_all, 'blk', split_axis=1, concat_axis=0, tiled=True)]
    dot_general x4 -> x0, matrix products: 33.2 us -> none  [contract(): lax.dot_general(cols_piece, slab_left, (((0,), (0,)), ((), ())), preferre...]
    pallas_call x0 -> x4, Pallas kernels: none -> 24.3 us  [band_chunk(): pl.pallas_call(kernel, grid=(width // unit,), in_specs=specs, out_specs=p...]
    convert_element_type x1 -> x0, other arithmetic: 23.4 us -> none  [shards(): return running.astype(jnp.bfloat16)]
    ppermute x0 -> x22, starting transfers between devices: none -> 22.2 us  [the longest x4 5.87 us: gather_left(): lax.ppermute(low[-1][:half], 'blk', forth)]
    slice x0 -> x12, local copies, waits for them, and re-layouts: none -> 15.8 us  [the longest x4 6.49 us: gather_left(): high[-1][half:]]
  transfers between devices with their start and end apart: 2 -> 23, of which waited for: 2 -> 8; matrix products, arithmetic and copies ran while one was open for 1% -> 15% of each run, Pallas kernels for 0% -> 12%
where the time goes in v1:
time: 173 us; the launch traced here: 172 us
  waiting for transfers between devices  80.4 us (46%)
  starting transfers between devices  28.8 us (17%)
  local copies, waits for them, and re-layouts  25.4 us (15%)
  Pallas kernels  24.3 us (14%)
  other arithmetic  9.31 us (5%)
  matrix products  3.49 us (2%)
    ppermute x4, waiting for transfers between devices, gather_left(): high.append(lax.ppermute(high[-1], 'blk', back))  34 us
    pallas_call x4, Pallas kernels, band_chunk(): pl.pallas_call(kernel, grid=(width // unit,), in_specs=specs, out_specs=p...  24.3 us
    ppermute x4, waiting for transfers between devices, gather_left(): low.append(lax.ppermute(low[-1], 'blk', forth))  18.7 us
    ppermute x3, waiting for transfers between devices, exchange_weighted(): other = lax.ppermute(held, 'tile', [(t, t ^ bit) for t in range(tiles)])  15.1 us
    all_to_all x1, waiting for transfers between devices, exchange_weighted(): lax.all_to_all(weighted, 'tile', split_axis=0, concat_axis=1, tiled=True)  9.74 us
    all_to_all x1, starting transfers between devices, exchange_weighted(): lax.all_to_all(weighted, 'tile', split_axis=0, concat_axis=1, tiled=True)  6.59 us
    slice x4, local copies, waits for them, and re-layouts, gather_left(): high[-1][half:]  6.49 us
    ppermute x4, starting transfers between devices, gather_left(): lax.ppermute(low[-1][:half], 'blk', forth)  5.87 us
  transfers between devices with their start and end apart: 23, of which 8 were waited for; matrix products, arithmetic and copies ran while one was open for 15% of the time, Pallas kernels for 12%

profile of v1, /device:TPU:0, one launch (start us, length us, event | category | flops | bytes accessed | tf_op | source)
XLA Modules:
  0.0 171.9 jit_solution(15898185356137496596)
XLA Ops:
  2.0 0.7 convert_reduce_fusion
  3.4 1.3 convolution_divide_fusion
  4.8 2.2 %fusion.1 = bf16[256,512]{1,0:T(8,128)(2,1)} fusion(f32[8,512]{1,0:T(8,128)S(1)} %convolution_divide_fusion, bf16[256,512]{1,0:T(8,128)(2,1)} %param.8, f32[256]{0:T(256)} %param.10, f32[256]{0:T(256)S(1)} %mul.38, s32[8]{0:T(128)S(1)} %add.28, s32[8]{0:T(128)} %param.13, pred[8]{0:T(512)(128)(4,1)S(1)} %broadcast_compare_fusion), kind=kOutput, calls=%fused_computation.3 | convolution fusion | flops 13246464 | bytes 542792 | tf_op jit(solution)/shard_map/dot_general | solution.py:16
  6.9 6.6 %all-to-all-start = ((bf16[8,32,512]{2,1,0:T(8,128)(2,1)}), bf16[8,32,512]{2,1,0:T(8,128)(2,1)S(1)}, u32[]{:S(2)}, u32[]{:S(2)}) async-start(bf16[8,32,512]{2,1,0:T(8,128)(2,1)} %bitcast.30), calls=%async_computation | async-start | bytes 524288 | tf_op jit(solution)/shard_map/all_to_all | solution.py:37
  13.5 9.7 %all-to-all-done = bf16[8,32,512]{2,1,0:T(8,128)(2,1)S(1)} async-done(((bf16[8,32,512]{2,1,0:T(8,128)(2,1)}), bf16[8,32,512]{2,1,0:T(8,128)(2,1)S(1)}, u32[]{:S(2)}, u32[]{:S(2)}) %all-to-all-start) | async-done | bytes 262176 | tf_op jit(solution)/shard_map/all_to_all | solution.py:37
  23.3 1.5 collective-permute-start
  24.9 1.5 collective-permute-start.1
  26.3 1.5 collective-permute-start.2
  27.8 2.2 %collective-permute-done.1 = bf16[32,1024]{1,0:T(8,128)(2,1)S(1)} collective-permute-done((bf16[32,1024]{1,0:T(8,128)(2,1)S(1)}, bf16[32,1024]{1,0:T(8,128)(2,1)S(1)}, u32[]{:S(2)}, u32[]{:S(2)}) %collective-permute-start.1) | collective-permute-done | bytes 65568 | tf_op jit(solution)/shard_map/ppermute | solution.py:43
  31.2 12.7 %collective-permute-done.3 = bf16[4,32,1024]{2,1,0:T(8,128)(2,1)} collective-permute-done((bf16[4,32,1024]{2,1,0:T(8,128)(2,1)S(1)}, bf16[4,32,1024]{2,1,0:T(8,128)(2,1)}, u32[]{:S(2)}, u32[]{:S(2)}) %collective-permute-start.3) | collective-permute-done | bytes 262176 | tf_op jit(solution)/shard_map/ppermute | solution.py:47
  44.0 1.0 select_bitcast_fusion.5
  45.1 0.9 pad_maximum_fusion.2
  46.0 0.7 slice.45
  46.7 0.8 collective-permute-start.18
  47.5 0.9 slice.36
  48.3 1.5 collective-permute-start.6
  50.4 1.2 slice.42
  51.5 1.5 collective-permute-start.14
  53.0 1.0 slice.39
  54.0 2.1 %collective-permute-done.18.refs_3_ = bf16[256,512]{1,0:T(8,128)(2,1)S(1)} collective-permute-done((bf16[256,512]{1,0:T(8,128)(2,1)}, bf16[256,512]{1,0:T(8,128)(2,1)S(1)}, u32[]{:S(2)}, u32[]{:S(2)}) %collective-permute-start.18) | collective-permute-done | bytes 262176 | tf_op jit(solution)/shard_map/ppermute | solution.py:62
  56.1 1.7 collective-permute-start.16
  57.8 2.4 %collective-permute-done.4 = bf16[2,4,32,1024]{3,2,1,0:T(8,128)(2,1)} collective-permute-done((bf16[2,4,32,1024]{3,2,1,0:T(8,128)(2,1)}, bf16[2,4,32,1024]{3,2,1,0:T(8,128)(2,1)}, u32[]{:S(2)}, u32[]{:S(2)}) %collective-permute-start.4) | collective-permute-done | bytes 524320 | tf_op jit(solution)/shard_map/ppermute | solution.py:47
  60.1 1.7 collective-permute-start.20
  61.8 1.3 select_bitcast_fusion.3
  63.1 34.0 %collective-permute-done.20.refs_6_ = bf16[256,512]{1,0:T(8,128)(2,1)} collective-permute-done((bf16[256,512]{1,0:T(8,128)(2,1)}, bf16[256,512]{1,0:T(8,128)(2,1)}, u32[]{:S(2)}, u32[]{:S(2)}) %collective-permute-start.20) | collective-permute-done | bytes 262176 | tf_op jit(solution)/shard_map/ppermute | solution.py:63
  97.1 1.5 collective-permute-start.10
  99.1 1.1 pad_maximum_fusion.1
  100.9 0.9 slice.55
  101.8 1.0 slice.48
  102.8 1.7 slice.49
  104.4 16.6 %collective-permute-done.10.refs_3_ = bf16[256,2048]{1,0:T(8,128)(2,1)} collective-permute-done((bf16[256,2048]{1,0:T(8,128)(2,1)}, bf16[256,2048]{1,0:T(8,128)(2,1)}, u32[]{:S(2)}, u32[]{:S(2)}) %collective-permute-start.10) | collective-permute-done | bytes 1048608 | tf_op jit(solution)/shard_map/ppermute | solution.py:62
  121.0 1.5 collective-permute-start.7
  122.5 1.9 %slice.50 = bf16[128,2048]{1,0:T(8,128)(2,1)} slice(bf16[256,2048]{1,0:T(8,128)(2,1)} %collective-permute-done.10.refs_3_), slice={[0:128], [0:2048]} | slice | bytes 1048576 | tf_op jit(solution)/shard_map/slice | solution.py:65
  125.0 1.9 %slice.51 = bf16[128,2048]{1,0:T(8,128)(2,1)} slice(bf16[256,2048]{1,0:T(8,128)(2,1)} %collective-permute-done.12.refs_6_), slice={[128:256], [0:2048]} | slice | bytes 1048576 | tf_op jit(solution)/shard_map/slice | solution.py:65
  126.9 1.5 collective-permute-start.11
  128.4 2.0 %slice.52 = bf16[128,2560]{1,0:T(8,128)(2,1)} slice(bf16[256,2560]{1,0:T(8,128)(2,1)} %collective-permute-done.14.refs_3_), slice={[0:128], [0:2560]} | slice | bytes 1310720 | tf_op jit(solution)/shard_map/slice | solution.py:65
  130.9 2.0 %slice.53 = bf16[128,2560]{1,0:T(8,128)(2,1)} slice(bf16[256,2560]{1,0:T(8,128)(2,1)} %collective-permute-done.16.refs_6_), slice={[128:256], [0:2560]} | slice | bytes 1310720 | tf_op jit(solution)/shard_map/slice | solution.py:65
  133.0 1.5 collective-permute-start.15
  134.4 1.4 select_bitcast_fusion.1
  137.6 1.5 copy.45
  139.0 3.9 %copy.46.refs_0_.refs_1_ = bf16[1024,1024]{1,0:T(8,128)(2,1)} copy(bf16[1024,1024]{0,1:T(8,128)(2,1)} %bitcast.27) | data formatting | bytes 4194304 | tf_op jit(solution)/shard_map/reshape | solution.py:54
  143.0 1.5 collective-permute-start.19
  144.5 1.6 copy-done.1
  146.1 0.9 copy-done.3
  147.0 4.6 %shard_map.73.refs_0_ = bf16[1024,6144]{1,0:T(8,128)(2,1)} custom-call(bf16[1024,1024]{1,0:T(8,128)(2,1)S(1)} %copy-done.1, bf16[256,6144]{1,0:T(8,128)(2,1)S(1)} %copy-done, bf16[256,1024]{1,0:T(8,128)(2,1)} %collective-permute-done.6.refs_2_, bf16[128,1024]{1,0:T(8,128)(2,1)S(1)} %copy-done.3, bf16[128,1024]{1,0:T(8,128)(2,1)} %collective-permute-done.9.refs_4_, ...), custom_call_target="tpu_custom_call" | custom-call | flops 2147483648 | bytes 6291456 | tf_op jit(solution)/shard_map/pallas_call | solution.py:92
  152.2 7.5 %shard_map.74.refs_0_ = bf16[1024,6144]{1,0:T(8,128)(2,1)} custom-call(bf16[1024,6144]{1,0:T(8,128)(2,1)} %shard_map.73.refs_0_, bf16[1024,1024]{1,0:T(8,128)(2,1)S(1)} %copy-done.1, bf16[256,6144]{1,0:T(8,128)(2,1)S(1)} %copy-done, bf16[256,2048]{1,0:T(8,128)(2,1)} %collective-permute-done.10.refs_3_, ...), custom_call_target="tpu_custom_call", output_to_operand_aliasing={{}: (0, {})} | custom-call | flops 4294967296 | bytes 10485760 | tf_op jit(solution)/shard_map/pallas_call | solution.py:92
  159.7 9.0 %shard_map.75.refs_0_ = bf16[1024,6144]{1,0:T(8,128)(2,1)} custom-call(bf16[1024,6144]{1,0:T(8,128)(2,1)} %shard_map.74.refs_0_, bf16[1024,1024]{1,0:T(8,128)(2,1)S(1)} %copy-done.1, bf16[256,6144]{1,0:T(8,128)(2,1)S(1)} %copy-done, bf16[256,2560]{1,0:T(8,128)(2,1)} %collective-permute-done.14.refs_3_, ...), custom_call_target="tpu_custom_call", output_to_operand_aliasing={{}: (0, {})} | custom-call | flops 5368709120 | bytes 12582912 | tf_op jit(solution)/shard_map/pallas_call | solution.py:92
  168.7 3.2 %shard_map.76 = bf16[1024,6144]{1,0:T(8,128)(2,1)} custom-call(bf16[1024,6144]{1,0:T(8,128)(2,1)} %shard_map.75.refs_0_, bf16[1024,1024]{1,0:T(8,128)(2,1)S(1)} %copy-done.1, bf16[256,6144]{1,0:T(8,128)(2,1)S(1)} %copy-done, bf16[256,512]{1,0:T(8,128)(2,1)S(1)} %collective-permute-done.18.refs_3_, ...), custom_call_target="tpu_custom_call", output_to_operand_aliasing={{}: (0, {})} | custom-call | flops 1073741824 | bytes 4194304 | tf_op jit(solution)/shard_map/pallas_call | solution.py:92
  (57 shorter events, 9.3 us)
Async XLA Ops:
  6.9 39.1 %copy-start = (bf16[256,6144]{1,0:T(8,128)(2,1)S(1)}, bf16[256,6144]{1,0:T(8,128)(2,1)}, u32[]{:S(2)}) copy-start(bf16[256,6144]{1,0:T(8,128)(2,1)} %refs_2_.5) | copy-start | bytes 9437188
  6.9 16.3 %all-to-all-start = ((bf16[8,32,512]{2,1,0:T(8,128)(2,1)}), bf16[8,32,512]{2,1,0:T(8,128)(2,1)S(1)}, u32[]{:S(2)}, u32[]{:S(2)}) async-start(bf16[8,32,512]{2,1,0:T(8,128)(2,1)} %bitcast.30), calls=%async_computation | async-start | bytes 524288 | tf_op jit(solution)/shard_map/all_to_all | solution.py:37
  23.3 4.5 %collective-permute-start = (bf16[32,1024]{1,0:T(8,128)(2,1)S(1)}, bf16[32,1024]{1,0:T(8,128)(2,1)S(1)}, u32[]{:S(2)}, u32[]{:S(2)}) collective-permute-start(bf16[32,1024]{1,0:T(8,128)(2,1)S(1)} %get-tuple-element.14), channel_id=1, source_target_pairs={{0,8},{8,24},{24,16},{16,0},{1,9},{9,25},{25,17},{17,1},{2,10},{10... | collective-permute-start | bytes 196616 | tf_op jit(solution)/shard_map/ppermute | solution.py:43
  24.9 5.2 %collective-permute-start.1 = (bf16[32,1024]{1,0:T(8,128)(2,1)S(1)}, bf16[32,1024]{1,0:T(8,128)(2,1)S(1)}, u32[]{:S(2)}, u32[]{:S(2)}) collective-permute-start(bf16[32,1024]{1,0:T(8,128)(2,1)S(1)} %get-tuple-element.13), channel_id=1, source_target_pairs={{0,24},{8,16},{24,0},{16,8},{1,25},{9,17},{25,1},{17,9},{2,26},{10... | collective-permute-start | bytes 196616 | tf_op jit(solution)/shard_map/ppermute | solution.py:43
  26.3 4.3 %collective-permute-start.2 = (bf16[32,1024]{1,0:T(8,128)(2,1)S(1)}, bf16[32,1024]{1,0:T(8,128)(2,1)S(1)}, u32[]{:S(2)}, u32[]{:S(2)}) collective-permute-start(bf16[32,1024]{1,0:T(8,128)(2,1)S(1)} %get-tuple-element.12), channel_id=1, source_target_pairs={{0,16},{8,0},{24,8},{16,24},{1,17},{9,1},{25,9},{17,25},{2,18},{10... | collective-permute-start | bytes 196616 | tf_op jit(solution)/shard_map/ppermute | solution.py:43
  30.0 0.6 copy-start.10
  30.6 0.6 copy-start.11
  31.2 12.7 %collective-permute-start.3 = (bf16[4,32,1024]{2,1,0:T(8,128)(2,1)S(1)}, bf16[4,32,1024]{2,1,0:T(8,128)(2,1)}, u32[]{:S(2)}, u32[]{:S(2)}) collective-permute-start(bf16[4,32,1024]{2,1,0:T(8,128)(2,1)S(1)} %pad_maximum_fusion.3), channel_id=1, source_target_pairs={{0,4},{1,5},{2,6},{3,7},{4,0},{5,1},{6,2},{7,3},{8,12},{9,13},{10,... | collective-permute-start | bytes 786440 | tf_op jit(solution)/shard_map/ppermute | solution.py:47
  45.0 1.0 copy-start.8
  45.0 1.7 copy-start.9
  46.0 14.2 %collective-permute-start.4 = (bf16[2,4,32,1024]{3,2,1,0:T(8,128)(2,1)}, bf16[2,4,32,1024]{3,2,1,0:T(8,128)(2,1)}, u32[]{:S(2)}, u32[]{:S(2)}) collective-permute-start(bf16[2,4,32,1024]{3,2,1,0:T(8,128)(2,1)} %pad_maximum_fusion.2), channel_id=1, source_target_pairs={{0,2},{1,3},{2,0},{3,1},{4,6},{5,7},{6,4},{7,5},{8,10},{9,11},{10,... | collective-permute-start | bytes 1572872 | tf_op jit(solution)/shard_map/ppermute | solution.py:47
  46.7 9.4 %collective-permute-start.18 = (bf16[256,512]{1,0:T(8,128)(2,1)}, bf16[256,512]{1,0:T(8,128)(2,1)S(1)}, u32[]{:S(2)}, u32[]{:S(2)}) collective-permute-start(bf16[256,512]{1,0:T(8,128)(2,1)} %slice.45), channel_id=1, source_target_pairs={{0,8},{8,24},{24,16},{16,0},{1,9},{9,25},{25,17},{17,1},{2,10},{10... | collective-permute-start | bytes 786440 | tf_op jit(solution)/shard_map/ppermute | solution.py:62
  48.3 50.2 %collective-permute-start.6 = (bf16[256,1024]{1,0:T(8,128)(2,1)}, bf16[256,1024]{1,0:T(8,128)(2,1)}, u32[]{:S(2)}, u32[]{:S(2)}) collective-permute-start(bf16[256,1024]{1,0:T(8,128)(2,1)} %slice.36), channel_id=1, source_target_pairs={{0,8},{8,24},{24,16},{16,0},{1,9},{9,25},{25,17},{17,1},{2,10},{10... | collective-permute-start | bytes 1572872 | tf_op jit(solution)/shard_map/ppermute | solution.py:62
  49.8 50.4 %collective-permute-start.8 = (bf16[256,1024]{1,0:T(8,128)(2,1)}, bf16[256,1024]{1,0:T(8,128)(2,1)}, u32[]{:S(2)}, u32[]{:S(2)}) collective-permute-start(bf16[256,1024]{1,0:T(8,128)(2,1)} %slice.36), channel_id=1, source_target_pairs={{0,16},{8,0},{24,8},{16,24},{1,17},{9,1},{25,9},{17,25},{2,18},{10... | collective-permute-start | bytes 1572872 | tf_op jit(solution)/shard_map/ppermute | solution.py:63
  51.5 75.4 %collective-permute-start.14 = (bf16[256,2560]{1,0:T(8,128)(2,1)}, bf16[256,2560]{1,0:T(8,128)(2,1)}, u32[]{:S(2)}, u32[]{:S(2)}) collective-permute-start(bf16[256,2560]{1,0:T(8,128)(2,1)} %slice.42), channel_id=1, source_target_pairs={{0,8},{8,24},{24,16},{16,0},{1,9},{9,25},{25,17},{17,1},{2,10},{10... | collective-permute-start | bytes 3932168 | tf_op jit(solution)/shard_map/ppermute | solution.py:62
  56.1 74.3 %collective-permute-start.16 = (bf16[256,2560]{1,0:T(8,128)(2,1)}, bf16[256,2560]{1,0:T(8,128)(2,1)}, u32[]{:S(2)}, u32[]{:S(2)}) collective-permute-start(bf16[256,2560]{1,0:T(8,128)(2,1)} %slice.42), channel_id=1, source_target_pairs={{0,16},{8,0},{24,8},{16,24},{1,17},{9,1},{25,9},{17,25},{2,18},{10... | collective-permute-start | bytes 3932168 | tf_op jit(solution)/shard_map/ppermute | solution.py:63
  60.1 37.0 %collective-permute-start.20 = (bf16[256,512]{1,0:T(8,128)(2,1)}, bf16[256,512]{1,0:T(8,128)(2,1)}, u32[]{:S(2)}, u32[]{:S(2)}) collective-permute-start(bf16[256,512]{1,0:T(8,128)(2,1)} %slice.45), channel_id=1, source_target_pairs={{0,16},{8,0},{24,8},{16,24},{1,17},{9,1},{25,9},{17,25},{2,18},{10... | collective-permute-start | bytes 786440 | tf_op jit(solution)/shard_map/ppermute | solution.py:63
  63.1 36.1 %copy-start.4 = (bf16[2,1,4,32,1024]{4,3,2,0,1:T(8,128)(2,1)}, bf16[2,1,4,32,1024]{4,3,2,0,1:T(8,128)(2,1)S(1)}, u32[]{:S(2)}) copy-start(bf16[2,1,4,32,1024]{4,3,2,0,1:T(8,128)(2,1)S(1)} %get-tuple-element.7) | copy-start | bytes 1572868
  63.1 37.1 %copy-start.6 = (bf16[2,1,4,32,1024]{4,3,2,0,1:T(8,128)(2,1)}, bf16[2,1,4,32,1024]{4,3,2,0,1:T(8,128)(2,1)S(1)}, u32[]{:S(2)}) copy-start(bf16[2,1,4,32,1024]{4,3,2,0,1:T(8,128)(2,1)S(1)} %get-tuple-element.8) | copy-start | bytes 1572868
  97.1 23.9 %collective-permute-start.10 = (bf16[256,2048]{1,0:T(8,128)(2,1)}, bf16[256,2048]{1,0:T(8,128)(2,1)}, u32[]{:S(2)}, u32[]{:S(2)}) collective-permute-start(bf16[256,2048]{1,0:T(8,128)(2,1)} %slice.39), channel_id=1, source_target_pairs={{0,8},{8,24},{24,16},{16,0},{1,9},{9,25},{25,17},{17,1},{2,10},{10... | collective-permute-start | bytes 3145736 | tf_op jit(solution)/shard_map/ppermute | solution.py:62
  98.6 25.9 %collective-permute-start.12 = (bf16[256,2048]{1,0:T(8,128)(2,1)}, bf16[256,2048]{1,0:T(8,128)(2,1)}, u32[]{:S(2)}, u32[]{:S(2)}) collective-permute-start(bf16[256,2048]{1,0:T(8,128)(2,1)} %slice.39), channel_id=1, source_target_pairs={{0,16},{8,0},{24,8},{16,24},{1,17},{9,1},{25,9},{17,25},{2,18},{10... | collective-permute-start | bytes 3145736 | tf_op jit(solution)/shard_map/ppermute | solution.py:63
  100.2 32.8 %collective-permute-start.5 = (bf16[2,2,4,32,1024]{4,3,2,0,1:T(8,128)(2,1)}, bf16[2,2,4,32,1024]{4,3,2,0,1:T(8,128)(2,1)}, u32[]{:S(2)}, u32[]{:S(2)}) collective-permute-start(bf16[2,2,4,32,1024]{4,3,2,0,1:T(8,128)(2,1)} %pad_maximum_fusion.1), channel_id=1, source_target_pairs={{0,1},{1,0},{2,3},{3,2},{4,5},{5,4},{6,7},{7,6},{8,9},{9,8},{10,11... | collective-permute-start | bytes 3145736 | tf_op jit(solution)/shard_map/ppermute | solution.py:47
  121.0 14.8 %collective-permute-start.7 = (bf16[128,1024]{1,0:T(8,128)(2,1)S(1)}, bf16[128,1024]{1,0:T(8,128)(2,1)S(1)}, u32[]{:S(2)}, u32[]{:S(2)}) collective-permute-start(bf16[128,1024]{1,0:T(8,128)(2,1)S(1)} %slice.48), channel_id=1, source_target_pairs={{0,8},{8,24},{24,16},{16,0},{1,9},{9,25},{25,17},{17,1},{2,10},{10... | collective-permute-start | bytes 786440 | tf_op jit(solution)/shard_map/ppermute | solution.py:65
  124.4 10.0 %copy-start.5 = (bf16[2,1,4,32,1024]{4,3,2,0,1:T(8,128)(2,1)S(1)}, bf16[2,1,4,32,1024]{4,3,2,0,1:T(8,128)(2,1)}, u32[]{:S(2)}) copy-start(bf16[2,1,4,32,1024]{4,3,2,0,1:T(8,128)(2,1)} %copy-done.4) | copy-start | bytes 1572868
  124.4 10.0 %copy-start.7 = (bf16[2,1,4,32,1024]{4,3,2,0,1:T(8,128)(2,1)S(1)}, bf16[2,1,4,32,1024]{4,3,2,0,1:T(8,128)(2,1)}, u32[]{:S(2)}) copy-start(bf16[2,1,4,32,1024]{4,3,2,0,1:T(8,128)(2,1)} %copy-done.6) | copy-start | bytes 1572868
  124.4 18.6 %collective-permute-start.9 = (bf16[128,1024]{1,0:T(8,128)(2,1)}, bf16[128,1024]{1,0:T(8,128)(2,1)}, u32[]{:S(2)}, u32[]{:S(2)}) collective-permute-start(bf16[128,1024]{1,0:T(8,128)(2,1)} %slice.49), channel_id=1, source_target_pairs={{0,16},{8,0},{24,8},{16,24},{1,17},{9,1},{25,9},{17,25},{2,18},{10... | collective-permute-start | bytes 786440 | tf_op jit(solution)/shard_map/ppermute | solution.py:65
  126.9 24.7 %collective-permute-start.11 = (bf16[128,2048]{1,0:T(8,128)(2,1)}, bf16[128,2048]{1,0:T(8,128)(2,1)}, u32[]{:S(2)}, u32[]{:S(2)}) collective-permute-start(bf16[128,2048]{1,0:T(8,128)(2,1)} %slice.50), channel_id=1, source_target_pairs={{0,8},{8,24},{24,16},{16,0},{1,9},{9,25},{25,17},{17,1},{2,10},{10... | collective-permute-start | bytes 1572872 | tf_op jit(solution)/shard_map/ppermute | solution.py:65
  130.4 21.8 %collective-permute-start.13 = (bf16[128,2048]{1,0:T(8,128)(2,1)}, bf16[128,2048]{1,0:T(8,128)(2,1)}, u32[]{:S(2)}, u32[]{:S(2)}) collective-permute-start(bf16[128,2048]{1,0:T(8,128)(2,1)} %slice.51), channel_id=1, source_target_pairs={{0,16},{8,0},{24,8},{16,24},{1,17},{9,1},{25,9},{17,25},{2,18},{10... | collective-permute-start | bytes 1572872 | tf_op jit(solution)/shard_map/ppermute | solution.py:65
  133.0 26.7 %collective-permute-start.15 = (bf16[128,2560]{1,0:T(8,128)(2,1)}, bf16[128,2560]{1,0:T(8,128)(2,1)}, u32[]{:S(2)}, u32[]{:S(2)}) collective-permute-start(bf16[128,2560]{1,0:T(8,128)(2,1)} %slice.52), channel_id=1, source_target_pairs={{0,8},{8,24},{24,16},{16,0},{1,9},{9,25},{25,17},{17,1},{2,10},{10... | collective-permute-start | bytes 1966088 | tf_op jit(solution)/shard_map/ppermute | solution.py:65
  135.8 0.7 copy-start.2
  136.5 23.2 %collective-permute-start.17 = (bf16[128,2560]{1,0:T(8,128)(2,1)}, bf16[128,2560]{1,0:T(8,128)(2,1)}, u32[]{:S(2)}, u32[]{:S(2)}) collective-permute-start(bf16[128,2560]{1,0:T(8,128)(2,1)} %slice.53), channel_id=1, source_target_pairs={{0,16},{8,0},{24,8},{16,24},{1,17},{9,1},{25,9},{17,25},{2,18},{10... | collective-permute-start | bytes 1966088 | tf_op jit(solution)/shard_map/ppermute | solution.py:65
  143.0 25.7 %collective-permute-start.19 = (bf16[128,512]{1,0:T(8,128)(2,1)}, bf16[128,512]{1,0:T(8,128)(2,1)S(1)}, u32[]{:S(2)}, u32[]{:S(2)}) collective-permute-start(bf16[128,512]{1,0:T(8,128)(2,1)} %slice.54), channel_id=1, source_target_pairs={{0,8},{8,24},{24,16},{16,0},{1,9},{9,25},{25,17},{17,1},{2,10},{10... | collective-permute-start | bytes 393224 | tf_op jit(solution)/shard_map/ppermute | solution.py:65
  144.5 1.6 copy-start.1
  146.1 0.9 copy-start.3
  151.6 17.1 %collective-permute-start.21 = (bf16[128,512]{1,0:T(8,128)(2,1)S(1)}, bf16[128,512]{1,0:T(8,128)(2,1)S(1)}, u32[]{:S(2)}, u32[]{:S(2)}) collective-permute-start(bf16[128,512]{1,0:T(8,128)(2,1)S(1)} %slice.55), channel_id=1, source_target_pairs={{0,16},{8,0},{24,8},{16,24},{1,17},{9,1},{25,9},{17,25},{2,18},{10... | collective-permute-start | bytes 393224 | tf_op jit(solution)/shard_map/ppermute | solution.py:65

commit v2 on v0

v2 whole, which is shorter than its diff:
```python
import functools

import jax
import jax.numpy as jnp
from jax import lax
from jax.experimental import pallas as pl
from jax.experimental.pallas import tpu as pltpu
from jax.sharding import PartitionSpec as P

UNITS = 24
SENDS = ((8,), (6, 4, 4, 2))
LANES = 128
VMEM_LIMIT = 20 * 1024 * 1024
VMEM_MOST = 60 * 1024 * 1024


def cost(weight):
    return pl.CostEstimate(flops=weight * 10**6, bytes_accessed=0, transcendentals=0)


def on_ring(place, count):
    half = count // 2
    return jnp.where(place < half, place, count + half - 1 - place)


def ring_shift(count, by):
    half = count // 2
    ring = list(range(half)) + list(range(count - 1, half - 1, -1))
    return [(ring[p], ring[(p + by) % count]) for p in range(count)]


def block_width(first, size, unit):
    return 2 * unit if first % (2 * unit) == 0 and size % (2 * unit) == 0 else unit


def swap(count, distance):
    return [(t, t ^ distance) for t in range(count)]


def my_group():
    members = lax.axis_size("tile") // lax.axis_size("blk")
    return lax.axis_index("tile") // members


def token_spec():
    return pl.BlockSpec((16, LANES), lambda i: (0, 0))


def token_shape():
    return jax.ShapeDtypeStruct((16, LANES), jnp.bfloat16)


def as_columns(row, width):
    column = jnp.broadcast_to(row, (LANES, row.shape[1])).T
    return jnp.concatenate([column] * (width // LANES), axis=1)


def weigh_kernel(groups, *refs):
    sources, outs = refs[:6], refs[7 : 7 + groups]
    *held, weighted, sems = refs[7 + groups :]
    copies = [
        pltpu.make_async_copy(source, target, sems.at[i])
        for i, (source, target) in enumerate(zip(sources, held))
    ]
    for copy in copies:
        copy.start()
    for copy in copies:
        copy.wait()
    assign, orders, offsets, right, row_weight, coupling = held
    height, width = right.shape
    me = lax.axis_index("blk")
    right_wide = right[...].astype(jnp.float32)
    coupled = as_columns(coupling[...], width)
    scaled = coupled * right_wide
    row_ids = lax.broadcasted_iota(jnp.int32, (height, width), 0)
    live = jnp.zeros((height, width), jnp.float32)
    spread = jnp.zeros((height, width), jnp.float32)
    for b in range(assign.shape[0]):
        mine = assign[b] == me
        first = jnp.where(mine, offsets[b], 0)
        last = jnp.where(mine, offsets[b] + orders[b], 0)
        member = ((row_ids >= first) & (row_ids < last)).astype(jnp.float32)
        block_sum = jnp.sum(member * scaled, axis=0, keepdims=True)
        root = jnp.sqrt(jnp.full((1, width), orders[b], jnp.int32).astype(jnp.float32))
        spread += member * (block_sum / root)
        live += member
    result = live * as_columns(row_weight[...], width) * right_wide + coupled * spread
    weighted[...] = result.astype(jnp.bfloat16)
    group, rows = my_group(), outs[0].shape[0]
    for distance, out in enumerate(outs):
        start = pl.multiple_of(jnp.bitwise_xor(group, distance) * rows, rows)
        out[...] = weighted[pl.ds(start, rows), :]


def weigh_rows(right_rows, row_weight, coupling, assign, orders, offsets, after):
    height, width = right_rows.shape
    groups = lax.axis_size("blk")
    row_weight, coupling = row_weight.reshape(1, height), coupling.reshape(1, height)
    operands = (assign, orders, offsets, right_rows, row_weight, coupling)
    spaces = [pltpu.SMEM] * 3 + [pltpu.VMEM] * 3
    return pl.pallas_call(
        functools.partial(weigh_kernel, groups),
        grid=(1,),
        in_specs=[pl.BlockSpec(memory_space=pl.ANY)] * 6 + [token_spec()],
        out_specs=[pl.BlockSpec((height // groups, width), lambda i: (0, 0))] * groups,
        out_shape=[jax.ShapeDtypeStruct((height // groups, width), jnp.bfloat16)] * groups,
        scratch_shapes=[space(a.shape, a.dtype) for space, a in zip(spaces, operands)]
        + [pltpu.VMEM((height, width), jnp.bfloat16), pltpu.SemaphoreType.DMA((6,))],
        compiler_params=pltpu.CompilerParams(vmem_limit_bytes=VMEM_MOST),
        cost_estimate=cost(100000),
    )(*operands, after)


def pick_kernel(*refs):
    count = (len(refs) - 2) // 2
    pieces, outs, token, held = refs[:count], refs[count:-2], refs[-2], refs[-1]
    token[...] = jnp.zeros_like(token)
    for distance, piece in enumerate(pieces):
        held[distance] = piece[...]
    place = on_ring(lax.axis_index("blk"), count)
    group = my_group()
    for step, out in enumerate(outs):
        target = on_ring(lax.rem(place + step, count), count)
        out[...] = held[jnp.bitwise_xor(group, target)]


def pick_columns(pieces):
    count = len(pieces)
    return pl.pallas_call(
        pick_kernel,
        out_shape=[jax.ShapeDtypeStruct(pieces[0].shape, pieces[0].dtype)] * count
        + [token_shape()],
        scratch_shapes=[pltpu.VMEM((count, *pieces[0].shape), pieces[0].dtype)],
        compiler_params=pltpu.CompilerParams(vmem_limit_bytes=VMEM_LIMIT),
        cost_estimate=cost(1),
    )(*pieces)


def stack_kernel(*refs):
    parts, (_, out, token) = refs[:-3], refs[-3:]
    token[...] = jnp.zeros_like(token)
    for step, part in enumerate(parts):
        out[step] = part[...]


def whole_spec(shape):
    return pl.BlockSpec(tuple(shape), lambda i: (0,) * len(shape))


def stack_parts(parts, after, weight=1):
    shape = (len(parts), *parts[0].shape)
    return pl.pallas_call(
        stack_kernel,
        grid=(1,),
        in_specs=[whole_spec(part.shape) for part in parts] + [token_spec()],
        out_specs=[whole_spec(shape), token_spec()],
        out_shape=[jax.ShapeDtypeStruct(shape, parts[0].dtype), token_shape()],
        compiler_params=pltpu.CompilerParams(vmem_limit_bytes=VMEM_LIMIT),
        cost_estimate=cost(weight),
    )(*parts, after)


def arrange_kernel(far_groups, *refs):
    pieces, (_, out, token, held) = refs[:-4], refs[-4:]
    token[...] = jnp.zeros_like(token)
    _, slabs, rows, width = pieces[0].shape
    height = held.shape[0] // slabs
    group, member = my_group(), lax.rem(lax.axis_index("tile"), len(pieces))
    for far_member, piece in enumerate(pieces):
        column = pl.multiple_of(jnp.bitwise_xor(member, far_member) * width, width)
        for index, far_group in enumerate(far_groups):
            row = pl.multiple_of(jnp.bitwise_xor(group, far_group) * rows, rows)
            for slab in range(slabs):
                held[pl.ds(slab * height + row, rows), pl.ds(column, width)] = piece[index, slab]
    for slab in range(slabs):
        part = pl.ds(slab * height, height)
        out[:, part] = held[part, :].T


def arrange(pieces, far_groups, height, after):
    _, slabs, _, width = pieces[0].shape
    shape = (len(pieces) * width, slabs * height)
    return pl.pallas_call(
        functools.partial(arrange_kernel, far_groups),
        grid=(1,),
        in_specs=[whole_spec(piece.shape) for piece in pieces] + [token_spec()],
        out_specs=[whole_spec(shape), token_spec()],
        out_shape=[jax.ShapeDtypeStruct(shape, jnp.bfloat16), token_shape()],
        scratch_shapes=[pltpu.VMEM(shape[::-1], jnp.bfloat16)],
        compiler_params=pltpu.CompilerParams(vmem_limit_bytes=VMEM_LIMIT),
        cost_estimate=cost(1),
    )(*pieces, after)


def slice_kernel(left, *refs):
    out, token = refs[-2:]
    out[...] = left[...]
    token[...] = jnp.zeros_like(token)


def slice_columns(left_rows, first, size, unit, after):
    unit = block_width(first, size, unit)
    height, begin = left_rows.shape[0], first // unit
    return pl.pallas_call(
        slice_kernel,
        grid=(size // unit,),
        in_specs=[pl.BlockSpec((height, unit), lambda j: (0, begin + j))]
        + [token_spec()] * len(after),
        out_specs=[pl.BlockSpec((height, unit), lambda j: (0, j)), token_spec()],
        out_shape=[jax.ShapeDtypeStruct((height, size), left_rows.dtype), token_shape()],
        compiler_params=pltpu.CompilerParams(vmem_limit_bytes=VMEM_LIMIT),
        cost_estimate=cost(1),
    )(left_rows, *after)


def send_slab(piece):
    blks = lax.axis_size("blk")
    forth, back = ring_shift(blks, 1), ring_shift(blks, -1)
    ahead, behind = [], []
    for _ in range(blks // 2 - 1):
        ahead.append(lax.ppermute(ahead[-1] if ahead else piece, "blk", forth))
        behind.append(lax.ppermute(behind[-1] if behind else piece, "blk", back))
    return ahead, behind


def cut_kernel(ahead, behind, *refs):
    low, high, token = refs[-3:]
    low[...] = ahead[...]
    high[...] = behind[...]
    token[...] = jnp.zeros_like(token)


def cut_far(ahead, behind, first, size, unit, after):
    half = ahead[-1].shape[0] // 2
    unit = size if first % size == 0 else block_width(first, size, unit)
    begin = first // unit
    out_spec = pl.BlockSpec((half, unit), lambda j: (0, j))
    return pl.pallas_call(
        cut_kernel,
        grid=(size // unit,),
        in_specs=[
            pl.BlockSpec((half, unit), lambda j: (0, begin + j)),
            pl.BlockSpec((half, unit), lambda j: (1, begin + j)),
        ]
        + [token_spec()] * len(after),
        out_specs=[out_spec] * 2 + [token_spec()],
        out_shape=[jax.ShapeDtypeStruct((half, size), ahead[-1].dtype)] * 2 + [token_shape()],
        compiler_params=pltpu.CompilerParams(vmem_limit_bytes=VMEM_LIMIT),
        cost_estimate=cost(1),
    )(ahead[-1], behind[-1], *after)


def send_far(cuts):
    blks = lax.axis_size("blk")
    return [lax.ppermute(cut, "blk", ring_shift(blks, by)) for cut, by in zip(cuts, (1, -1))]


def band_kernel(*refs):
    weights, pieces, (_, out, token) = refs[0], refs[1:-3], refs[-3:]
    token[...] = jnp.zeros_like(token)
    stacked = jnp.concatenate([piece[...] for piece in pieces], axis=0)
    out[...] = jnp.dot(weights[...], stacked, preferred_element_type=jnp.float32).astype(out.dtype)


def band_kernel_onto(*refs):
    band_kernel(*refs[1:])


def band_chunk(band, weights, pieces, width, columns, unit, after):
    rows, depth = weights.shape

    def spec(array, first):
        return pl.BlockSpec((array.shape[0], unit), lambda j: (0, first // unit + j))

    specs = [pl.BlockSpec((rows, depth), lambda j: (0, 0))]
    specs += [spec(array, first) for array, first in pieces]
    specs.append(token_spec())
    operands = [weights] + [array for array, _ in pieces] + [after]
    kernel, aliases = band_kernel, {}
    if band is not None:
        specs.insert(0, pl.BlockSpec(memory_space=pl.ANY))
        operands.insert(0, band)
        kernel, aliases = band_kernel_onto, {0: 0}
    begin = pieces[0][1] // unit
    return pl.pallas_call(
        kernel,
        grid=(width // unit,),
        in_specs=specs,
        out_specs=[pl.BlockSpec((rows, unit), lambda j: (0, begin + j)), token_spec()],
        out_shape=[
            jax.ShapeDtypeStruct((rows, columns), jnp.bfloat16),
            token_shape(),
        ],
        input_output_aliases=aliases,
        compiler_params=pltpu.CompilerParams(vmem_limit_bytes=VMEM_LIMIT),
        cost_estimate=cost(1),
    )(*operands)


def shards(left_rows, right_rows, row_weight, coupling, assign, orders, offsets):
    height, columns = left_rows.shape
    blks, tiles = lax.axis_size("blk"), lax.axis_size("tile")
    members = tiles // blks
    unit = columns // UNITS

    starts = [sum(map(sum, SENDS[:i])) * unit for i in range(len(SENDS))]
    widths = [sum(sizes) * unit for sizes in SENDS]
    head = left_rows[:, : widths[0]]
    streams = [send_slab(head)]

    blocks = weigh_rows(right_rows, row_weight, coupling, assign, orders, offsets, head)
    pieces = [blocks[0]]
    for distance in range(1, blks):
        pieces.append(lax.ppermute(blocks[distance], "tile", swap(tiles, distance * members)))
    *parts, token = pick_columns(pieces)
    for step in range(1, blks):
        parts[step] = lax.ppermute(parts[step], "blk", ring_shift(blks, step))

    chunks = []

    def send_chunk(which, place, token, after=()):
        (ahead, behind), width = streams[which], SENDS[which][place] * unit
        offset = sum(SENDS[which][:place]) * unit
        *cuts, token = cut_far(ahead, behind, offset, width, unit, [token, *after])
        chunks.append((starts[which] + offset, offset, width, ahead, behind, send_far(cuts)))
        return token

    def send_slice(which, token, after=()):
        slab, token = slice_columns(left_rows, starts[which], widths[which], unit, [token, *after])
        streams.append(send_slab(slab))
        return token

    def multiply(band, index, token):
        begin, offset, width, ahead, behind, far = chunks[index]
        pieces = (
            [(left_rows, begin)]
            + [(array, offset) for array in ahead]
            + [(array, 0) for array in far]
            + [(array, offset) for array in behind[::-1]]
        )
        block = block_width(begin, width, unit)
        return band_chunk(band, weights, pieces, width, columns, block, token)

    token = send_slice(1, token)
    token = send_chunk(0, 0, token)
    held, token = stack_parts(parts, token, 100000)
    held, far_groups = held[None], [0]
    bit = blks // 2
    while bit:
        moved = lax.ppermute(held, "tile", swap(tiles, bit * members))
        held, token = stack_parts([held, moved], token)
        held = held.reshape((-1, *held.shape[2:]))
        far_groups = far_groups + [group ^ bit for group in far_groups]
        bit //= 2
    by_member = {0: held}
    bit = members // 2
    while bit:
        for member, piece in list(by_member.items()):
            by_member[member ^ bit] = lax.ppermute(piece, "tile", swap(tiles, bit))
        bit //= 2
    pieces = [by_member[member] for member in range(members)]
    weights, token = arrange(pieces, far_groups, height, token)

    band = None
    token = send_chunk(1, 0, token)
    for index in range(len(SENDS[1]) + 1):
        if index + 1 < len(SENDS[1]):
            token = send_chunk(1, index + 1, token, chunks[index][-1])
        band, token = multiply(band, index, token)
    return band


def solution(mesh):
    return jax.shard_map(
        shards,
        mesh=mesh,
        in_specs=(P("blk", "tile"), P("blk", "tile"), P("blk"), P("blk"), P(), P(), P()),
        out_specs=P("blk", "tile"),
        check_vma=False,
    )
```

time: 247 us -> 121 us (0.49)
  waiting for transfers between devices: 123 us -> 60.4 us
  blocking collectives: 45.7 us -> 0 us
  matrix products: 36.6 us -> 0 us
  Pallas kernels: 0 us -> 28.8 us
  starting transfers between devices: 0.04 us -> 28.7 us
  other arithmetic: 26.8 us -> 0 us
  between operations: 13.4 us -> 0.14 us
    all_gather x2 -> x0, waiting for transfers between devices: 122 us -> none  [the longest x1 90.7 us: shards(): slab_left = lax.all_gather(left_rows, 'blk', axis=0, tiled=True)]
    ppermute x0 -> x23, waiting for transfers between devices: none -> 60.4 us  [the longest x2 21.5 us: shards(): moved = lax.ppermute(held, 'tile', swap(tiles, bit * members))]
    all_to_all x1 -> x0, blocking collectives: 45.7 us -> none  [shards(): lax.all_to_all(weighted_all, 'blk', split_axis=1, concat_axis=0, tiled=True)]
    dot_general x6 -> x0, matrix products: 36.6 us -> none  [the longest x4 33.2 us: contract(): lax.dot_general(cols_piece, slab_left, (((0,), (0,)), ((), ())), preferre...]
    pallas_call x0 -> x17, Pallas kernels: none -> 28.8 us  [the longest x5 21.8 us: band_chunk(): pl.pallas_call(kernel, grid=(width // unit,), in_specs=specs, out_specs=[...]
    ppermute x0 -> x23, starting transfers between devices: none -> 28.7 us  [the longest x10 10.4 us: send_far(): lax.ppermute(cut, 'blk', ring_shift(blks, by))]
    convert_element_type x1 -> x0, other arithmetic: 23.4 us -> none  [shards(): return running.astype(jnp.bfloat16)]
  transfers between devices with their start and end apart: 2 -> 23, of which waited for: 2 -> 10; matrix products, arithmetic and copies ran while one was open for 1% -> 0% of each run, Pallas kernels for 0% -> 22%
where the time goes in v2:
time: 121 us
  waiting for transfers between devices  60.4 us (50%)
  Pallas kernels  28.8 us (24%)
  starting transfers between devices  28.7 us (24%)
  local copies, waits for them, and re-layouts  3.15 us (3%)
    pallas_call x5, Pallas kernels, band_chunk(): pl.pallas_call(kernel, grid=(width // unit,), in_specs=specs, out_specs=[...  21.8 us
    ppermute x2, waiting for transfers between devices, shards(): moved = lax.ppermute(held, 'tile', swap(tiles, bit * members))  21.5 us
    ppermute x2, waiting for transfers between devices, send_slab(): behind.append(lax.ppermute(behind[-1] if behind else piece, 'blk', back))  19.6 us
    ppermute x10, starting transfers between devices, send_far(): lax.ppermute(cut, 'blk', ring_shift(blks, by))  10.4 us
    ppermute x10, waiting for transfers between devices, send_far(): lax.ppermute(cut, 'blk', ring_shift(blks, by))  9.12 us
    ppermute x3, waiting for transfers between devices, shards(): lax.ppermute(blocks[distance], 'tile', swap(tiles, distance * members))  6.27 us
    ppermute x2, starting transfers between devices, send_slab(): behind.append(lax.ppermute(behind[-1] if behind else piece, 'blk', back))  5.59 us
    ppermute x3, starting transfers between devices, shards(): lax.ppermute(blocks[distance], 'tile', swap(tiles, distance * members))  4.73 us
  transfers between devices with their start and end apart: 23, of which 10 were waited for; matrix products, arithmetic and copies ran while one was open for 0% of the time, Pallas kernels for 22%

profile of v2, /device:TPU:0, one launch (start us, length us, event | category | flops | bytes accessed | tf_op | source)
XLA Modules:
  0.0 121.2 jit_solution(10290392651658288643)
XLA Ops:
  0.0 2.3 %slice.3.refs_6_ = bf16[256,2048]{1,0:T(8,128)(2,1)} slice(bf16[256,6144]{1,0:T(8,128)(2,1)} %refs_2_.9), slice={[0:256], [0:2048]} | slice | bytes 2097152 | tf_op jit(solution)/shard_map/slice | solution.py:308
  2.3 3.0 %collective-permute-start.7 = (bf16[256,2048]{1,0:T(8,128)(2,1)}, bf16[256,2048]{1,0:T(8,128)(2,1)}, u32[]{:S(2)}, u32[]{:S(2)}) collective-permute-start(bf16[256,2048]{1,0:T(8,128)(2,1)} %slice.3.refs_6_), channel_id=1, source_target_pairs={{0,16},{8,0},{24,8},{16,24},{1,17},{9,1},{25,9},{17,25},{2,18},{10... | collective-permute-start | bytes 3145736 | tf_op jit(solution)/shard_map/ppermute | solution.py:222
  5.3 3.7 %shard_map.73 = (bf16[64,512]{1,0:T(8,128)(2,1)}, bf16[64,512]{1,0:T(8,128)(2,1)}, bf16[64,512]{1,0:T(8,128)(2,1)}, bf16[64,512]{1,0:T(8,128)(2,1)}) custom-call(s32[8]{0:T(128)} %refs_0_.1, s32[8]{0:T(128)} %refs_1_.2, s32[8]{0:T(128)} %refs_2_.5, bf16[256,512]{1,0:T(8,128)(2,1)} %refs_3_.1, f32[1,256]{1,0:T(1,128)} %bitcast.11, f32[1,256]{1,0:T(1,128)} %bitcast.12, ...), custom_call_target="tpu_custom_call" | custom-call | flops 99999997952 | tf_op jit(solution)/shard_map/pallas_call | solution.py:101
  9.0 2.1 %collective-permute-start = (bf16[64,512]{1,0:T(8,128)(2,1)}, bf16[64,512]{1,0:T(8,128)(2,1)S(1)}, u32[]{:S(2)}, u32[]{:S(2)}) collective-permute-start(bf16[64,512]{1,0:T(8,128)(2,1)} %get-tuple-element.49), channel_id=1, source_target_pairs={{0,2},{1,3},{2,0},{3,1},{4,6},{5,7},{6,4},{7,5},{8,10},{9,11},{10,... | collective-permute-start | bytes 196616 | tf_op jit(solution)/shard_map/ppermute | solution.py:314
  11.2 2.6 %collective-permute-start.1 = (bf16[64,512]{1,0:T(8,128)(2,1)}, bf16[64,512]{1,0:T(8,128)(2,1)S(1)}, u32[]{:S(2)}, u32[]{:S(2)}) collective-permute-start(bf16[64,512]{1,0:T(8,128)(2,1)} %get-tuple-element.50), channel_id=1, source_target_pairs={{0,4},{1,5},{2,6},{3,7},{4,0},{5,1},{6,2},{7,3},{8,12},{9,13},{10,... | collective-permute-start | bytes 196616 | tf_op jit(solution)/shard_map/ppermute | solution.py:314
  13.8 0.0 collective-permute-done.refs_1_
  13.8 4.3 %collective-permute-done.1.refs_2_ = bf16[64,512]{1,0:T(8,128)(2,1)S(1)} collective-permute-done((bf16[64,512]{1,0:T(8,128)(2,1)}, bf16[64,512]{1,0:T(8,128)(2,1)S(1)}, u32[]{:S(2)}, u32[]{:S(2)}) %collective-permute-start.1) | collective-permute-done | bytes 65568 | tf_op jit(solution)/shard_map/ppermute | solution.py:314
  18.1 2.0 %collective-permute-done.2.refs_3_ = bf16[64,512]{1,0:T(8,128)(2,1)S(1)} collective-permute-done((bf16[64,512]{1,0:T(8,128)(2,1)}, bf16[64,512]{1,0:T(8,128)(2,1)S(1)}, u32[]{:S(2)}, u32[]{:S(2)}) %collective-permute-start.2) | collective-permute-done | bytes 65568 | tf_op jit(solution)/shard_map/ppermute | solution.py:314
  20.0 0.8 copy-done.1
  20.9 1.5 %collective-permute-start.3 = (bf16[64,512]{1,0:T(8,128)(2,1)S(1)}, bf16[64,512]{1,0:T(8,128)(2,1)S(1)}, u32[]{:S(2)}, u32[]{:S(2)}) collective-permute-start(bf16[64,512]{1,0:T(8,128)(2,1)S(1)} %get-tuple-element.53), channel_id=1, source_target_pairs={{0,8},{8,24},{24,16},{16,0},{1,9},{9,25},{25,17},{17,1},{2,10},{10... | collective-permute-start | bytes 196616 | tf_op jit(solution)/shard_map/ppermute | solution.py:317
  22.5 1.5 %collective-permute-start.4 = (bf16[64,512]{1,0:T(8,128)(2,1)S(1)}, bf16[64,512]{1,0:T(8,128)(2,1)S(1)}, u32[]{:S(2)}, u32[]{:S(2)}) collective-permute-start(bf16[64,512]{1,0:T(8,128)(2,1)S(1)} %get-tuple-element.54), channel_id=1, source_target_pairs={{0,24},{8,16},{24,0},{16,8},{1,25},{9,17},{25,1},{17,9},{2,26},{10... | collective-permute-start | bytes 196616 | tf_op jit(solution)/shard_map/ppermute | solution.py:317
  24.0 1.5 %collective-permute-start.5 = (bf16[64,512]{1,0:T(8,128)(2,1)S(1)}, bf16[64,512]{1,0:T(8,128)(2,1)S(1)}, u32[]{:S(2)}, u32[]{:S(2)}) collective-permute-start(bf16[64,512]{1,0:T(8,128)(2,1)S(1)} %get-tuple-element.55), channel_id=1, source_target_pairs={{0,16},{8,0},{24,8},{16,24},{1,17},{9,1},{25,9},{17,25},{2,18},{10... | collective-permute-start | bytes 196616 | tf_op jit(solution)/shard_map/ppermute | solution.py:317
  25.4 0.6 shard_map.75
  26.0 4.2 %collective-permute-done.7.behind.refs_5_ = bf16[256,2048]{1,0:T(8,128)(2,1)} collective-permute-done((bf16[256,2048]{1,0:T(8,128)(2,1)}, bf16[256,2048]{1,0:T(8,128)(2,1)}, u32[]{:S(2)}, u32[]{:S(2)}) %collective-permute-start.7) | collective-permute-done | bytes 1048608 | tf_op jit(solution)/shard_map/ppermute | solution.py:222
  30.2 2.6 %collective-permute-start.14 = (bf16[256,4096]{1,0:T(8,128)(2,1)S(1)}, bf16[256,4096]{1,0:T(8,128)(2,1)S(1)}, u32[]{:S(2)}, u32[]{:S(2)}) collective-permute-start(bf16[256,4096]{1,0:T(8,128)(2,1)S(1)} %get-tuple-element.68), channel_id=1, source_target_pairs={{0,16},{8,0},{24,8},{16,24},{1,17},{9,1},{25,9},{17,25},{2,18},{10... | collective-permute-start | bytes 6291464 | tf_op jit(solution)/shard_map/ppermute | solution.py:222
  32.8 1.3 %shard_map.76 = (bf16[128,2048]{1,0:T(8,128)(2,1)S(1)}, bf16[128,2048]{1,0:T(8,128)(2,1)S(1)}, bf16[16,128]{1,0:T(8,128)(2,1)S(1)}) custom-call(bf16[256,2048]{1,0:T(8,128)(2,1)} %collective-permute-done.6.ahead.refs_2_, bf16[256,2048]{1,0:T(8,128)(2,1)} %collective-permute-done.7.behind.refs_5_, bf16[16,128]{1,0:T(8,128)(2,1)S(1)} %get-tuple-element.57.refs_0_), custom_call_target="tpu_custom_call" | custom-call | flops 1000000 | tf_op jit(solution)/shard_map/pallas_call | solution.py:238
  34.1 0.0 collective-permute-done.3.refs_1_
  34.1 0.8 collective-permute-done.4.refs_2_
  34.9 2.7 %collective-permute-start.8 = (bf16[1,4,64,512]{3,2,1,0:T(8,128)(2,1)S(1)}, bf16[1,4,64,512]{3,2,1,0:T(8,128)(2,1)S(1)}, u32[]{:S(2)}, u32[]{:S(2)}) collective-permute-start(bf16[1,4,64,512]{3,2,1,0:T(8,128)(2,1)S(1)} %bitcast.9), channel_id=1, source_target_pairs={{0,4},{1,5},{2,6},{3,7},{4,0},{5,1},{6,2},{7,3},{8,12},{9,13},{10,... | collective-permute-start | bytes 786440 | tf_op jit(solution)/shard_map/ppermute | solution.py:350
  37.6 9.4 %collective-permute-done.8.refs_1_ = bf16[1,4,64,512]{3,2,1,0:T(8,128)(2,1)S(1)} collective-permute-done((bf16[1,4,64,512]{3,2,1,0:T(8,128)(2,1)S(1)}, bf16[1,4,64,512]{3,2,1,0:T(8,128)(2,1)S(1)}, u32[]{:S(2)}, u32[]{:S(2)}) %collective-permute-start.8) | collective-permute-done | bytes 262176 | tf_op jit(solution)/shard_map/ppermute | solution.py:350
  47.1 0.7 collective-permute-start.9
  47.8 12.1 %collective-permute-done.9.refs_1_ = bf16[2,4,64,512]{3,2,1,0:T(8,128)(2,1)S(1)} collective-permute-done((bf16[2,4,64,512]{3,2,1,0:T(8,128)(2,1)S(1)}, bf16[2,4,64,512]{3,2,1,0:T(8,128)(2,1)S(1)}, u32[]{:S(2)}, u32[]{:S(2)}) %collective-permute-start.9) | collective-permute-done | bytes 524320 | tf_op jit(solution)/shard_map/ppermute | solution.py:350
  59.9 0.1 shard_map.79
  60.0 0.1 collective-permute-start.10
  60.0 0.1 collective-permute-start.11
  60.1 2.0 %collective-permute-start.12 = (bf16[128,2048]{1,0:T(8,128)(2,1)S(1)}, bf16[128,2048]{1,0:T(8,128)(2,1)S(1)}, u32[]{:S(2)}, u32[]{:S(2)}) collective-permute-start(bf16[128,2048]{1,0:T(8,128)(2,1)S(1)} %get-tuple-element.67), channel_id=1, source_target_pairs={{0,16},{8,0},{24,8},{16,24},{1,17},{9,1},{25,9},{17,25},{2,18},{10... | collective-permute-start | bytes 1572872 | tf_op jit(solution)/shard_map/ppermute | solution.py:255
  62.1 0.6 collective-permute-done.10.refs_1_
  62.7 0.8 shard_map.80
  63.5 15.4 %collective-permute-done.14.behind.refs_6_ = bf16[256,4096]{1,0:T(8,128)(2,1)S(1)} collective-permute-done((bf16[256,4096]{1,0:T(8,128)(2,1)S(1)}, bf16[256,4096]{1,0:T(8,128)(2,1)S(1)}, u32[]{:S(2)}, u32[]{:S(2)}) %collective-permute-start.14) | collective-permute-done | bytes 2097184 | tf_op jit(solution)/shard_map/ppermute | solution.py:222
  78.9 2.5 %collective-permute-done.13.ahead.refs_3_ = bf16[256,4096]{1,0:T(8,128)(2,1)S(1)} collective-permute-done((bf16[256,4096]{1,0:T(8,128)(2,1)S(1)}, bf16[256,4096]{1,0:T(8,128)(2,1)S(1)}, u32[]{:S(2)}, u32[]{:S(2)}) %collective-permute-start.13) | collective-permute-done | bytes 2097184 | tf_op jit(solution)/shard_map/ppermute | solution.py:221
  81.4 0.1 shard_map.81
  81.5 0.1 collective-permute-start.15
  81.5 2.0 %collective-permute-start.16 = (bf16[128,1536]{1,0:T(8,128)(2,1)S(1)}, bf16[128,1536]{1,0:T(8,128)(2,1)S(1)}, u32[]{:S(2)}, u32[]{:S(2)}) collective-permute-start(bf16[128,1536]{1,0:T(8,128)(2,1)S(1)} %get-tuple-element.74), channel_id=1, source_target_pairs={{0,16},{8,0},{24,8},{16,24},{1,17},{9,1},{25,9},{17,25},{2,18},{10... | collective-permute-start | bytes 1179656 | tf_op jit(solution)/shard_map/ppermute | solution.py:255
  83.5 9.1 %collective-permute-done.11.refs_1_.refs_3_ = bf16[128,2048]{1,0:T(8,128)(2,1)S(1)} collective-permute-done((bf16[128,2048]{1,0:T(8,128)(2,1)S(1)}, bf16[128,2048]{1,0:T(8,128)(2,1)S(1)}, u32[]{:S(2)}, u32[]{:S(2)}) %collective-permute-start.11) | collective-permute-done | bytes 524320 | tf_op jit(solution)/shard_map/ppermute | solution.py:255
  92.6 0.0 collective-permute-done.12.refs_2_.refs_4_
  92.6 0.2 shard_map.82
  92.8 0.1 collective-permute-start.17
  92.9 2.0 %collective-permute-start.18 = (bf16[128,1024]{1,0:T(8,128)(2,1)S(1)}, bf16[128,1024]{1,0:T(8,128)(2,1)S(1)}, u32[]{:S(2)}, u32[]{:S(2)}) collective-permute-start(bf16[128,1024]{1,0:T(8,128)(2,1)S(1)} %get-tuple-element.79), channel_id=1, source_target_pairs={{0,16},{8,0},{24,8},{16,24},{1,17},{9,1},{25,9},{17,25},{2,18},{10... | collective-permute-start | bytes 786440 | tf_op jit(solution)/shard_map/ppermute | solution.py:255
  94.9 7.3 %shard_map.83 = (bf16[1024,6144]{1,0:T(8,128)(2,1)}, bf16[16,128]{1,0:T(8,128)(2,1)S(1)}) custom-call(bf16[1024,1024]{1,0:T(8,128)(2,1)S(1)} %get-tuple-element.65.refs_0_.refs_1_, bf16[256,6144]{1,0:T(8,128)(2,1)S(1)} %copy-done, bf16[256,2048]{1,0:T(8,128)(2,1)} %collective-permute-done.6.ahead.refs_2_, ...), custom_call_target="tpu_custom_call" | custom-call | flops 1000000 | tf_op jit(solution)/shard_map/pallas_call | solution.py:285
  102.2 0.2 shard_map.84
  102.4 0.1 collective-permute-start.19
  102.5 2.0 %collective-permute-start.20 = (bf16[128,1024]{1,0:T(8,128)(2,1)S(1)}, bf16[128,1024]{1,0:T(8,128)(2,1)S(1)}, u32[]{:S(2)}, u32[]{:S(2)}) collective-permute-start(bf16[128,1024]{1,0:T(8,128)(2,1)S(1)} %get-tuple-element.84), channel_id=1, source_target_pairs={{0,16},{8,0},{24,8},{16,24},{1,17},{9,1},{25,9},{17,25},{2,18},{10... | collective-permute-start | bytes 786440 | tf_op jit(solution)/shard_map/ppermute | solution.py:255
  104.5 5.0 %shard_map.85 = (bf16[1024,6144]{1,0:T(8,128)(2,1)}, bf16[16,128]{1,0:T(8,128)(2,1)S(1)}) custom-call(bf16[1024,6144]{1,0:T(8,128)(2,1)} %get-tuple-element.72.refs_0_, bf16[1024,1024]{1,0:T(8,128)(2,1)S(1)} %get-tuple-element.65.refs_0_.refs_1_, bf16[256,6144]{1,0:T(8,128)(2,1)S(1)} %copy-done, ...), custom_call_target="tpu_custom_call", output_to_operand_aliasing={{0}: (0, {})} | custom-call | flops 1000000 | tf_op jit(solution)/shard_map/pallas_call | solution.py:285
  109.5 0.1 collective-permute-start.21
  109.6 2.0 %collective-permute-start.22 = (bf16[128,512]{1,0:T(8,128)(2,1)S(1)}, bf16[128,512]{1,0:T(8,128)(2,1)S(1)}, u32[]{:S(2)}, u32[]{:S(2)}) collective-permute-start(bf16[128,512]{1,0:T(8,128)(2,1)S(1)} %get-tuple-element.88), channel_id=1, source_target_pairs={{0,16},{8,0},{24,8},{16,24},{1,17},{9,1},{25,9},{17,25},{2,18},{10... | collective-permute-start | bytes 393224 | tf_op jit(solution)/shard_map/ppermute | solution.py:255
  111.6 3.7 %shard_map.87 = (bf16[1024,6144]{1,0:T(8,128)(2,1)}, bf16[16,128]{1,0:T(8,128)(2,1)S(1)}) custom-call(bf16[1024,6144]{1,0:T(8,128)(2,1)} %get-tuple-element.77.refs_0_, bf16[1024,1024]{1,0:T(8,128)(2,1)S(1)} %get-tuple-element.65.refs_0_.refs_1_, bf16[256,6144]{1,0:T(8,128)(2,1)S(1)} %copy-done, ...), custom_call_target="tpu_custom_call", output_to_operand_aliasing={{0}: (0, {})} | custom-call | flops 1000000 | tf_op jit(solution)/shard_map/pallas_call | solution.py:285
  115.3 3.7 %shard_map.88 = (bf16[1024,6144]{1,0:T(8,128)(2,1)}, bf16[16,128]{1,0:T(8,128)(2,1)S(1)}) custom-call(bf16[1024,6144]{1,0:T(8,128)(2,1)} %get-tuple-element.82.refs_0_, bf16[1024,1024]{1,0:T(8,128)(2,1)S(1)} %get-tuple-element.65.refs_0_.refs_1_, bf16[256,6144]{1,0:T(8,128)(2,1)S(1)} %copy-done, ...), custom_call_target="tpu_custom_call", output_to_operand_aliasing={{0}: (0, {})} | custom-call | flops 1000000 | tf_op jit(solution)/shard_map/pallas_call | solution.py:285
  118.9 2.2 %shard_map.89 = (bf16[1024,6144]{1,0:T(8,128)(2,1)}, bf16[16,128]{1,0:T(8,128)(2,1)}) custom-call(bf16[1024,6144]{1,0:T(8,128)(2,1)} %get-tuple-element.86.refs_0_, bf16[1024,1024]{1,0:T(8,128)(2,1)S(1)} %get-tuple-element.65.refs_0_.refs_1_, bf16[256,6144]{1,0:T(8,128)(2,1)S(1)} %copy-done, ...), custom_call_target="tpu_custom_call", output_to_operand_aliasing={{0}: (0, {})} | custom-call | flops 1000000 | tf_op jit(solution)/shard_map/pallas_call | solution.py:285
  (20 shorter events, 0.1 us)
Async XLA Ops:
  2.3 27.9 %collective-permute-start.7 = (bf16[256,2048]{1,0:T(8,128)(2,1)}, bf16[256,2048]{1,0:T(8,128)(2,1)}, u32[]{:S(2)}, u32[]{:S(2)}) collective-permute-start(bf16[256,2048]{1,0:T(8,128)(2,1)} %slice.3.refs_6_), channel_id=1, source_target_pairs={{0,16},{8,0},{24,8},{16,24},{1,17},{9,1},{25,9},{17,25},{2,18},{10... | collective-permute-start | bytes 3145736 | tf_op jit(solution)/shard_map/ppermute | solution.py:222
  5.3 27.6 %collective-permute-start.6 = (bf16[256,2048]{1,0:T(8,128)(2,1)}, bf16[256,2048]{1,0:T(8,128)(2,1)}, u32[]{:S(2)}, u32[]{:S(2)}) collective-permute-start(bf16[256,2048]{1,0:T(8,128)(2,1)} %slice.3.refs_6_), channel_id=1, source_target_pairs={{0,8},{8,24},{24,16},{16,0},{1,9},{9,25},{25,17},{17,1},{2,10},{10... | collective-permute-start | bytes 3145736 | tf_op jit(solution)/shard_map/ppermute | solution.py:221
  5.3 20.2 %copy-start = (bf16[256,6144]{1,0:T(8,128)(2,1)S(1)}, bf16[256,6144]{1,0:T(8,128)(2,1)}, u32[]{:S(2)}) copy-start(bf16[256,6144]{1,0:T(8,128)(2,1)} %refs_2_.9) | copy-start | bytes 9437188
  9.0 4.7 %collective-permute-start = (bf16[64,512]{1,0:T(8,128)(2,1)}, bf16[64,512]{1,0:T(8,128)(2,1)S(1)}, u32[]{:S(2)}, u32[]{:S(2)}) collective-permute-start(bf16[64,512]{1,0:T(8,128)(2,1)} %get-tuple-element.49), channel_id=1, source_target_pairs={{0,2},{1,3},{2,0},{3,1},{4,6},{5,7},{6,4},{7,5},{8,10},{9,11},{10,... | collective-permute-start | bytes 196616 | tf_op jit(solution)/shard_map/ppermute | solution.py:314
  11.2 6.9 %collective-permute-start.1 = (bf16[64,512]{1,0:T(8,128)(2,1)}, bf16[64,512]{1,0:T(8,128)(2,1)S(1)}, u32[]{:S(2)}, u32[]{:S(2)}) collective-permute-start(bf16[64,512]{1,0:T(8,128)(2,1)} %get-tuple-element.50), channel_id=1, source_target_pairs={{0,4},{1,5},{2,6},{3,7},{4,0},{5,1},{6,2},{7,3},{8,12},{9,13},{10,... | collective-permute-start | bytes 196616 | tf_op jit(solution)/shard_map/ppermute | solution.py:314
  13.8 6.3 %collective-permute-start.2 = (bf16[64,512]{1,0:T(8,128)(2,1)}, bf16[64,512]{1,0:T(8,128)(2,1)S(1)}, u32[]{:S(2)}, u32[]{:S(2)}) collective-permute-start(bf16[64,512]{1,0:T(8,128)(2,1)} %get-tuple-element.51), channel_id=1, source_target_pairs={{0,6},{1,7},{2,4},{3,5},{4,2},{5,3},{6,0},{7,1},{8,14},{9,15},{10,... | collective-permute-start | bytes 196616 | tf_op jit(solution)/shard_map/ppermute | solution.py:314
  20.0 0.8 copy-start.1
  20.9 13.2 %collective-permute-start.3 = (bf16[64,512]{1,0:T(8,128)(2,1)S(1)}, bf16[64,512]{1,0:T(8,128)(2,1)S(1)}, u32[]{:S(2)}, u32[]{:S(2)}) collective-permute-start(bf16[64,512]{1,0:T(8,128)(2,1)S(1)} %get-tuple-element.53), channel_id=1, source_target_pairs={{0,8},{8,24},{24,16},{16,0},{1,9},{9,25},{25,17},{17,1},{2,10},{10... | collective-permute-start | bytes 196616 | tf_op jit(solution)/shard_map/ppermute | solution.py:317
  22.5 12.5 %collective-permute-start.4 = (bf16[64,512]{1,0:T(8,128)(2,1)S(1)}, bf16[64,512]{1,0:T(8,128)(2,1)S(1)}, u32[]{:S(2)}, u32[]{:S(2)}) collective-permute-start(bf16[64,512]{1,0:T(8,128)(2,1)S(1)} %get-tuple-element.54), channel_id=1, source_target_pairs={{0,24},{8,16},{24,0},{16,8},{1,25},{9,17},{25,1},{17,9},{2,26},{10... | collective-permute-start | bytes 196616 | tf_op jit(solution)/shard_map/ppermute | solution.py:317
  24.0 11.0 %collective-permute-start.5 = (bf16[64,512]{1,0:T(8,128)(2,1)S(1)}, bf16[64,512]{1,0:T(8,128)(2,1)S(1)}, u32[]{:S(2)}, u32[]{:S(2)}) collective-permute-start(bf16[64,512]{1,0:T(8,128)(2,1)S(1)} %get-tuple-element.55), channel_id=1, source_target_pairs={{0,16},{8,0},{24,8},{16,24},{1,17},{9,1},{25,9},{17,25},{2,18},{10... | collective-permute-start | bytes 196616 | tf_op jit(solution)/shard_map/ppermute | solution.py:317
  30.2 48.7 %collective-permute-start.14 = (bf16[256,4096]{1,0:T(8,128)(2,1)S(1)}, bf16[256,4096]{1,0:T(8,128)(2,1)S(1)}, u32[]{:S(2)}, u32[]{:S(2)}) collective-permute-start(bf16[256,4096]{1,0:T(8,128)(2,1)S(1)} %get-tuple-element.68), channel_id=1, source_target_pairs={{0,16},{8,0},{24,8},{16,24},{1,17},{9,1},{25,9},{17,25},{2,18},{10... | collective-permute-start | bytes 6291464 | tf_op jit(solution)/shard_map/ppermute | solution.py:222
  32.8 48.6 %collective-permute-start.13 = (bf16[256,4096]{1,0:T(8,128)(2,1)S(1)}, bf16[256,4096]{1,0:T(8,128)(2,1)S(1)}, u32[]{:S(2)}, u32[]{:S(2)}) collective-permute-start(bf16[256,4096]{1,0:T(8,128)(2,1)S(1)} %get-tuple-element.68), channel_id=1, source_target_pairs={{0,8},{8,24},{24,16},{16,0},{1,9},{9,25},{25,17},{17,1},{2,10},{10... | collective-permute-start | bytes 6291464 | tf_op jit(solution)/shard_map/ppermute | solution.py:221
  34.9 12.1 %collective-permute-start.8 = (bf16[1,4,64,512]{3,2,1,0:T(8,128)(2,1)S(1)}, bf16[1,4,64,512]{3,2,1,0:T(8,128)(2,1)S(1)}, u32[]{:S(2)}, u32[]{:S(2)}) collective-permute-start(bf16[1,4,64,512]{3,2,1,0:T(8,128)(2,1)S(1)} %bitcast.9), channel_id=1, source_target_pairs={{0,4},{1,5},{2,6},{3,7},{4,0},{5,1},{6,2},{7,3},{8,12},{9,13},{10,... | collective-permute-start | bytes 786440 | tf_op jit(solution)/shard_map/ppermute | solution.py:350
  47.1 12.8 %collective-permute-start.9 = (bf16[2,4,64,512]{3,2,1,0:T(8,128)(2,1)S(1)}, bf16[2,4,64,512]{3,2,1,0:T(8,128)(2,1)S(1)}, u32[]{:S(2)}, u32[]{:S(2)}) collective-permute-start(bf16[2,4,64,512]{3,2,1,0:T(8,128)(2,1)S(1)} %bitcast.7), channel_id=1, source_target_pairs={{0,2},{1,3},{2,0},{3,1},{4,6},{5,7},{6,4},{7,5},{8,10},{9,11},{10,... | collective-permute-start | bytes 1572872 | tf_op jit(solution)/shard_map/ppermute | solution.py:350
  60.0 2.7 %collective-permute-start.10 = (bf16[4,4,64,512]{3,2,1,0:T(8,128)(2,1)S(1)}, bf16[4,4,64,512]{3,2,1,0:T(8,128)(2,1)S(1)}, u32[]{:S(2)}, u32[]{:S(2)}) collective-permute-start(bf16[4,4,64,512]{3,2,1,0:T(8,128)(2,1)S(1)} %bitcast.5), channel_id=1, source_target_pairs={{0,1},{1,0},{2,3},{3,2},{4,5},{5,4},{6,7},{7,6},{8,9},{9,8},{10,11... | collective-permute-start | bytes 3145736 | tf_op jit(solution)/shard_map/ppermute | solution.py:359
  60.0 32.6 %collective-permute-start.11 = (bf16[128,2048]{1,0:T(8,128)(2,1)S(1)}, bf16[128,2048]{1,0:T(8,128)(2,1)S(1)}, u32[]{:S(2)}, u32[]{:S(2)}) collective-permute-start(bf16[128,2048]{1,0:T(8,128)(2,1)S(1)} %get-tuple-element.66), channel_id=1, source_target_pairs={{0,8},{8,24},{24,16},{16,0},{1,9},{9,25},{25,17},{17,1},{2,10},{10... | collective-permute-start | bytes 1572872 | tf_op jit(solution)/shard_map/ppermute | solution.py:255
  60.1 32.5 %collective-permute-start.12 = (bf16[128,2048]{1,0:T(8,128)(2,1)S(1)}, bf16[128,2048]{1,0:T(8,128)(2,1)S(1)}, u32[]{:S(2)}, u32[]{:S(2)}) collective-permute-start(bf16[128,2048]{1,0:T(8,128)(2,1)S(1)} %get-tuple-element.67), channel_id=1, source_target_pairs={{0,16},{8,0},{24,8},{16,24},{1,17},{9,1},{25,9},{17,25},{2,18},{10... | collective-permute-start | bytes 1572872 | tf_op jit(solution)/shard_map/ppermute | solution.py:255
  81.5 20.7 %collective-permute-start.15 = (bf16[128,1536]{1,0:T(8,128)(2,1)S(1)}, bf16[128,1536]{1,0:T(8,128)(2,1)S(1)}, u32[]{:S(2)}, u32[]{:S(2)}) collective-permute-start(bf16[128,1536]{1,0:T(8,128)(2,1)S(1)} %get-tuple-element.73), channel_id=1, source_target_pairs={{0,8},{8,24},{24,16},{16,0},{1,9},{9,25},{25,17},{17,1},{2,10},{10... | collective-permute-start | bytes 1179656 | tf_op jit(solution)/shard_map/ppermute | solution.py:255
  81.5 20.7 %collective-permute-start.16 = (bf16[128,1536]{1,0:T(8,128)(2,1)S(1)}, bf16[128,1536]{1,0:T(8,128)(2,1)S(1)}, u32[]{:S(2)}, u32[]{:S(2)}) collective-permute-start(bf16[128,1536]{1,0:T(8,128)(2,1)S(1)} %get-tuple-element.74), channel_id=1, source_target_pairs={{0,16},{8,0},{24,8},{16,24},{1,17},{9,1},{25,9},{17,25},{2,18},{10... | collective-permute-start | bytes 1179656 | tf_op jit(solution)/shard_map/ppermute | solution.py:255
  92.8 16.7 %collective-permute-start.17 = (bf16[128,1024]{1,0:T(8,128)(2,1)S(1)}, bf16[128,1024]{1,0:T(8,128)(2,1)S(1)}, u32[]{:S(2)}, u32[]{:S(2)}) collective-permute-start(bf16[128,1024]{1,0:T(8,128)(2,1)S(1)} %get-tuple-element.78), channel_id=1, source_target_pairs={{0,8},{8,24},{24,16},{16,0},{1,9},{9,25},{25,17},{17,1},{2,10},{10... | collective-permute-start | bytes 786440 | tf_op jit(solution)/shard_map/ppermute | solution.py:255
  92.9 16.6 %collective-permute-start.18 = (bf16[128,1024]{1,0:T(8,128)(2,1)S(1)}, bf16[128,1024]{1,0:T(8,128)(2,1)S(1)}, u32[]{:S(2)}, u32[]{:S(2)}) collective-permute-start(bf16[128,1024]{1,0:T(8,128)(2,1)S(1)} %get-tuple-element.79), channel_id=1, source_target_pairs={{0,16},{8,0},{24,8},{16,24},{1,17},{9,1},{25,9},{17,25},{2,18},{10... | collective-permute-start | bytes 786440 | tf_op jit(solution)/shard_map/ppermute | solution.py:255
  102.4 12.8 %collective-permute-start.19 = (bf16[128,1024]{1,0:T(8,128)(2,1)S(1)}, bf16[128,1024]{1,0:T(8,128)(2,1)S(1)}, u32[]{:S(2)}, u32[]{:S(2)}) collective-permute-start(bf16[128,1024]{1,0:T(8,128)(2,1)S(1)} %get-tuple-element.83), channel_id=1, source_target_pairs={{0,8},{8,24},{24,16},{16,0},{1,9},{9,25},{25,17},{17,1},{2,10},{10... | collective-permute-start | bytes 786440 | tf_op jit(solution)/shard_map/ppermute | solution.py:255
  102.5 12.7 %collective-permute-start.20 = (bf16[128,1024]{1,0:T(8,128)(2,1)S(1)}, bf16[128,1024]{1,0:T(8,128)(2,1)S(1)}, u32[]{:S(2)}, u32[]{:S(2)}) collective-permute-start(bf16[128,1024]{1,0:T(8,128)(2,1)S(1)} %get-tuple-element.84), channel_id=1, source_target_pairs={{0,16},{8,0},{24,8},{16,24},{1,17},{9,1},{25,9},{17,25},{2,18},{10... | collective-permute-start | bytes 786440 | tf_op jit(solution)/shard_map/ppermute | solution.py:255
  109.5 9.4 %collective-permute-start.21 = (bf16[128,512]{1,0:T(8,128)(2,1)S(1)}, bf16[128,512]{1,0:T(8,128)(2,1)S(1)}, u32[]{:S(2)}, u32[]{:S(2)}) collective-permute-start(bf16[128,512]{1,0:T(8,128)(2,1)S(1)} %get-tuple-element.87), channel_id=1, source_target_pairs={{0,8},{8,24},{24,16},{16,0},{1,9},{9,25},{25,17},{17,1},{2,10},{10... | collective-permute-start | bytes 393224 | tf_op jit(solution)/shard_map/ppermute | solution.py:255
  109.6 9.3 %collective-permute-start.22 = (bf16[128,512]{1,0:T(8,128)(2,1)S(1)}, bf16[128,512]{1,0:T(8,128)(2,1)S(1)}, u32[]{:S(2)}, u32[]{:S(2)}) collective-permute-start(bf16[128,512]{1,0:T(8,128)(2,1)S(1)} %get-tuple-element.88), channel_id=1, source_target_pairs={{0,16},{8,0},{24,8},{16,24},{1,17},{9,1},{25,9},{17,25},{2,18},{10... | collective-permute-start | bytes 393224 | tf_op jit(solution)/shard_map/ppermute | solution.py:255

commit v3 on v2

--- a/solution.py
+++ b/solution.py
@@ -8,10 +8,10 @@
 from jax.sharding import PartitionSpec as P
 
 UNITS = 24
-SENDS = ((8,), (6, 4, 4, 2))
+SENDS = ((8,), (6, 7), (3,))
+SHIFT = (0, 16, 0, 0)
 LANES = 128
 VMEM_LIMIT = 20 * 1024 * 1024
-VMEM_MOST = 60 * 1024 * 1024
 
 
 def cost(weight):
@@ -101,12 +101,12 @@
     return pl.pallas_call(
         functools.partial(weigh_kernel, groups),
         grid=(1,),
-        in_specs=[pl.BlockSpec(memory_space=pl.ANY)] * 6 + [token_spec()],
+        in_specs=[pl.BlockSpec(memory_space=pltpu.HBM)] * 6 + [token_spec()],
         out_specs=[pl.BlockSpec((height // groups, width), lambda i: (0, 0))] * groups,
         out_shape=[jax.ShapeDtypeStruct((height // groups, width), jnp.bfloat16)] * groups,
         scratch_shapes=[space(a.shape, a.dtype) for space, a in zip(spaces, operands)]
         + [pltpu.VMEM((height, width), jnp.bfloat16), pltpu.SemaphoreType.DMA((6,))],
-        compiler_params=pltpu.CompilerParams(vmem_limit_bytes=VMEM_MOST),
+        compiler_params=pltpu.CompilerParams(vmem_limit_bytes=VMEM_LIMIT),
         cost_estimate=cost(100000),
     )(*operands, after)
 
@@ -160,28 +160,27 @@
     )(*parts, after)
 
 
-def arrange_kernel(far_groups, *refs):
+def arrange_kernel(places, members, *refs):
     pieces, (_, out, token, held) = refs[:-4], refs[-4:]
     token[...] = jnp.zeros_like(token)
     _, slabs, rows, width = pieces[0].shape
     height = held.shape[0] // slabs
-    group, member = my_group(), lax.rem(lax.axis_index("tile"), len(pieces))
-    for far_member, piece in enumerate(pieces):
+    group, member = my_group(), lax.rem(lax.axis_index("tile"), members)
+    for (far_member, far_groups), piece in zip(places, pieces):
         column = pl.multiple_of(jnp.bitwise_xor(member, far_member) * width, width)
         for index, far_group in enumerate(far_groups):
             row = pl.multiple_of(jnp.bitwise_xor(group, far_group) * rows, rows)
             for slab in range(slabs):
                 held[pl.ds(slab * height + row, rows), pl.ds(column, width)] = piece[index, slab]
-    for slab in range(slabs):
-        part = pl.ds(slab * height, height)
-        out[:, part] = held[part, :].T
-
-
-def arrange(pieces, far_groups, height, after):
+    for place, slab in enumerate(sorted(range(slabs), key=lambda s: (s == slabs // 2, s))):
+        out[:, pl.ds(place * height, height)] = held[pl.ds(slab * height, height), :].T
+
+
+def arrange(places, pieces, members, height, after):
     _, slabs, _, width = pieces[0].shape
-    shape = (len(pieces) * width, slabs * height)
-    return pl.pallas_call(
-        functools.partial(arrange_kernel, far_groups),
+    shape = (members * width, slabs * height)
+    return pl.pallas_call(
+        functools.partial(arrange_kernel, places, members),
         grid=(1,),
         in_specs=[whole_spec(piece.shape) for piece in pieces] + [token_spec()],
         out_specs=[whole_spec(shape), token_spec()],
@@ -225,26 +224,30 @@
 
 def cut_kernel(ahead, behind, *refs):
     low, high, token = refs[-3:]
-    low[...] = ahead[...]
-    high[...] = behind[...]
-    token[...] = jnp.zeros_like(token)
-
-
-def cut_far(ahead, behind, first, size, unit, after):
-    half = ahead[-1].shape[0] // 2
+    low[...] = ahead[: low.shape[0], :]
+    high[...] = behind[low.shape[0] :, :]
+    token[...] = jnp.zeros_like(token)
+
+
+def cut_far(ahead, behind, first, size, unit, shift, after):
     unit = size if first % size == 0 else block_width(first, size, unit)
-    begin = first // unit
-    out_spec = pl.BlockSpec((half, unit), lambda j: (0, j))
+    height, begin = ahead[-1].shape[0], first // unit
+    low, high = height // 2 - shift, height // 2 + shift
     return pl.pallas_call(
         cut_kernel,
         grid=(size // unit,),
-        in_specs=[
-            pl.BlockSpec((half, unit), lambda j: (0, begin + j)),
-            pl.BlockSpec((half, unit), lambda j: (1, begin + j)),
-        ]
+        in_specs=[pl.BlockSpec((height, unit), lambda j: (0, begin + j))] * 2
         + [token_spec()] * len(after),
-        out_specs=[out_spec] * 2 + [token_spec()],
-        out_shape=[jax.ShapeDtypeStruct((half, size), ahead[-1].dtype)] * 2 + [token_shape()],
+        out_specs=[
+            pl.BlockSpec((low, unit), lambda j: (0, j)),
+            pl.BlockSpec((high, unit), lambda j: (0, j)),
+            token_spec(),
+        ],
+        out_shape=[
+            jax.ShapeDtypeStruct((low, size), ahead[-1].dtype),
+            jax.ShapeDtypeStruct((high, size), ahead[-1].dtype),
+            token_shape(),
+        ],
         compiler_params=pltpu.CompilerParams(vmem_limit_bytes=VMEM_LIMIT),
         cost_estimate=cost(1),
     )(ahead[-1], behind[-1], *after)
@@ -255,46 +258,86 @@
     return [lax.ppermute(cut, "blk", ring_shift(blks, by)) for cut, by in zip(cuts, (1, -1))]
 
 
-def band_kernel(*refs):
+def stacked_dot(weights, pieces):
+    stacked = jnp.concatenate([piece[...] for piece in pieces], axis=0)
+    return jnp.dot(weights, stacked, preferred_element_type=jnp.float32)
+
+
+def near_kernel(*refs):
     weights, pieces, (_, out, token) = refs[0], refs[1:-3], refs[-3:]
     token[...] = jnp.zeros_like(token)
-    stacked = jnp.concatenate([piece[...] for piece in pieces], axis=0)
-    out[...] = jnp.dot(weights[...], stacked, preferred_element_type=jnp.float32).astype(out.dtype)
-
-
-def band_kernel_onto(*refs):
-    band_kernel(*refs[1:])
-
-
-def band_chunk(band, weights, pieces, width, columns, unit, after):
+    depth = sum(piece.shape[0] for piece in pieces)
+    out[...] = stacked_dot(weights[:, :depth], pieces)
+
+
+def far_kernel_onto(_, *refs):
+    far_kernel(*refs)
+
+
+def far_kernel(near, weights, *refs):
+    pieces, (_, out, token) = refs[:-3], refs[-3:]
+    token[...] = jnp.zeros_like(token)
+    rows, width = out.shape
+    step = pl.program_id(0)
+    if rows < near.shape[0]:
+        here = near[pl.ds(pl.multiple_of(step * rows, rows), rows), :]
+    else:
+        here = near[:, pl.ds(pl.multiple_of(step * width, width), width)]
+    out[...] = (here + stacked_dot(weights[...], pieces)).astype(out.dtype)
+
+
+def piece_specs(pieces, unit):
+    return [
+        pl.BlockSpec((array.shape[0], unit), lambda j, begin=first // unit: (0, begin + j))
+        for array, first in pieces
+    ]
+
+
+def near_chunk(weights, pieces, width, unit, after):
     rows, depth = weights.shape
-
-    def spec(array, first):
-        return pl.BlockSpec((array.shape[0], unit), lambda j: (0, first // unit + j))
-
-    specs = [pl.BlockSpec((rows, depth), lambda j: (0, 0))]
-    specs += [spec(array, first) for array, first in pieces]
-    specs.append(token_spec())
-    operands = [weights] + [array for array, _ in pieces] + [after]
-    kernel, aliases = band_kernel, {}
+    return pl.pallas_call(
+        near_kernel,
+        grid=(width // unit,),
+        in_specs=[pl.BlockSpec((rows, depth), lambda j: (0, 0))]
+        + piece_specs(pieces, unit)
+        + [token_spec()],
+        out_specs=[pl.BlockSpec((rows, unit), lambda j: (0, j)), token_spec()],
+        out_shape=[jax.ShapeDtypeStruct((rows, width), jnp.float32), token_shape()],
+        compiler_params=pltpu.CompilerParams(vmem_limit_bytes=VMEM_LIMIT),
+        cost_estimate=cost(1),
+    )(weights, *[array for array, _ in pieces], after)
+
+
+def band_chunk(band, near, weights, pieces, begin, columns, unit, after):
+    rows, width = near.shape
+    slab = sum(piece.shape[0] for piece in pieces)
+    last = weights.shape[1] // slab - 1
+    kernel, operands, specs, aliases = far_kernel, [], [], {}
     if band is not None:
-        specs.insert(0, pl.BlockSpec(memory_space=pl.ANY))
-        operands.insert(0, band)
-        kernel, aliases = band_kernel_onto, {0: 0}
-    begin = pieces[0][1] // unit
+        kernel, operands, aliases = far_kernel_onto, [band], {0: 0}
+        specs = [pl.BlockSpec(memory_space=pl.ANY)]
+    specs.append(pl.BlockSpec(memory_space=pltpu.VMEM))
+    if begin % width == 0:
+        steps, place = 2, begin // width
+        specs.append(pl.BlockSpec((rows // steps, slab), lambda i: (i, last)))
+        specs += [whole_spec(piece.shape) for piece in pieces]
+        out_spec = pl.BlockSpec((rows // steps, width), lambda i: (i, place))
+    else:
+        block = block_width(begin, width, unit)
+        steps, place = width // block, begin // block
+        specs.append(pl.BlockSpec((rows, slab), lambda i: (0, last)))
+        specs += piece_specs([(piece, 0) for piece in pieces], block)
+        out_spec = pl.BlockSpec((rows, block), lambda i: (0, place + i))
     return pl.pallas_call(
         kernel,
-        grid=(width // unit,),
-        in_specs=specs,
-        out_specs=[pl.BlockSpec((rows, unit), lambda j: (0, begin + j)), token_spec()],
-        out_shape=[
-            jax.ShapeDtypeStruct((rows, columns), jnp.bfloat16),
-            token_shape(),
-        ],
+        grid=(steps,),
+        in_specs=specs + [token_spec()],
+        out_specs=[out_spec, token_spec()],
+        out_shape=[jax.ShapeDtypeStruct((rows, columns), jnp.bfloat16), token_shape()],
         input_output_aliases=aliases,
         compiler_params=pltpu.CompilerParams(vmem_limit_bytes=VMEM_LIMIT),
         cost_estimate=cost(1),
-    )(*operands)
+    )(*operands, near, weights, *pieces, after)
 
 
 def shards(left_rows, right_rows, row_weight, coupling, assign, orders, offsets):
@@ -321,8 +364,10 @@
     def send_chunk(which, place, token, after=()):
         (ahead, behind), width = streams[which], SENDS[which][place] * unit
         offset = sum(SENDS[which][:place]) * unit
-        *cuts, token = cut_far(ahead, behind, offset, width, unit, [token, *after])
-        chunks.append((starts[which] + offset, offset, width, ahead, behind, send_far(cuts)))
+        *cuts, token = cut_far(
+            ahead, behind, offset, width, unit, SHIFT[len(chunks)], [token, *after]
+        )
+        chunks.append((starts[which] + offset, send_far(cuts)))
         return token
 
     def send_slice(which, token, after=()):
@@ -330,43 +375,50 @@
         streams.append(send_slab(slab))
         return token
 
-    def multiply(band, index, token):
-        begin, offset, width, ahead, behind, far = chunks[index]
-        pieces = (
-            [(left_rows, begin)]
-            + [(array, offset) for array in ahead]
-            + [(array, 0) for array in far]
-            + [(array, offset) for array in behind[::-1]]
-        )
-        block = block_width(begin, width, unit)
-        return band_chunk(band, weights, pieces, width, columns, block, token)
+    def multiply_near(which, place, token):
+        (ahead, behind), offset = streams[which], sum(SENDS[which][:place]) * unit
+        width, begin = SENDS[which][place] * unit, starts[which] + offset
+        pieces = [(left_rows, begin)] + [(array, offset) for array in ahead + behind[::-1]]
+        return near_chunk(weights, pieces, width, block_width(begin, width, unit), token)
+
+    def multiply(band, near, index, token):
+        begin, far = chunks[index]
+        return band_chunk(band, near, weights, far, begin, columns, unit, token)
 
     token = send_slice(1, token)
     token = send_chunk(0, 0, token)
     held, token = stack_parts(parts, token, 100000)
     held, far_groups = held[None], [0]
     bit = blks // 2
-    while bit:
+    while bit > 1:
         moved = lax.ppermute(held, "tile", swap(tiles, bit * members))
         held, token = stack_parts([held, moved], token)
         held = held.reshape((-1, *held.shape[2:]))
         far_groups = far_groups + [group ^ bit for group in far_groups]
         bit //= 2
-    by_member = {0: held}
+    moved = lax.ppermute(held, "tile", swap(tiles, members))
+    arrived = {(0, tuple(far_groups)): held, (0, tuple(g ^ 1 for g in far_groups)): moved}
     bit = members // 2
     while bit:
-        for member, piece in list(by_member.items()):
-            by_member[member ^ bit] = lax.ppermute(piece, "tile", swap(tiles, bit))
+        for (member, groups), piece in list(arrived.items()):
+            arrived[member ^ bit, groups] = lax.ppermute(piece, "tile", swap(tiles, bit))
         bit //= 2
-    pieces = [by_member[member] for member in range(members)]
-    weights, token = arrange(pieces, far_groups, height, token)
-
-    band = None
-    token = send_chunk(1, 0, token)
-    for index in range(len(SENDS[1]) + 1):
-        if index + 1 < len(SENDS[1]):
-            token = send_chunk(1, index + 1, token, chunks[index][-1])
-        band, token = multiply(band, index, token)
+    weights, token = arrange(
+        list(arrived.keys()), list(arrived.values()), members, height, token
+    )
+
+    nears = [None] * sum(map(len, SENDS))
+    nears[0], token = multiply_near(0, 0, token)
+    token = send_slice(2, token, [streams[1][0][-1], streams[1][1][-1]])
+    nears[1], token = multiply_near(1, 0, token)
+    nears[2], token = multiply_near(1, 1, token)
+    token = send_chunk(1, 0, token, chunks[0][-1])
+    band, token = multiply(None, nears[0], 0, token)
+    token = send_chunk(1, 1, token, [streams[2][0][-1], streams[2][1][-1]])
+    nears[3], token = multiply_near(2, 0, token)
+    token = send_chunk(2, 0, token, chunks[1][-1])
+    for index in range(1, len(chunks)):
+        band, token = multiply(band, nears[index], index, token)
     return band
 
 

time: 121 us -> 112 us (0.926)
  waiting for transfers between devices: 60.4 us -> 48.1 us
  local copies, waits for them, and re-layouts: 3.15 us -> 5.58 us
    ppermute x2 -> x3, waiting for transfers between devices: 19.6 us -> 6.58 us  [send_slab(): behind.append(lax.ppermute(behind[-1] if behind else piece, 'blk', back))]
    ppermute x2 -> x1, waiting for transfers between devices: 21.5 us -> 9.31 us  [shards(): moved = lax.ppermute(held, 'tile', swap(tiles, bit * members))]
    ppermute x1 -> x3, waiting for transfers between devices: 0.57 us -> 12.1 us  [the longest x1 12.1 us: shards(): moved = lax.ppermute(held, 'tile', swap(tiles, members))]
    pallas_call x6 -> x9, Pallas kernels: 22.6 us -> 26.5 us  [the longest x4 15.3 us: near_chunk(): pl.pallas_call(near_kernel, grid=(width // unit,), in_specs=[pl.BlockSpec...]
    unnamed x4 -> x20, local copies, waits for them, and re-layouts: 0.84 us -> 4.29 us
    ppermute x2 -> x3, waiting for transfers between devices: 2.49 us -> 4.98 us  [send_slab(): ahead.append(lax.ppermute(ahead[-1] if ahead else piece, 'blk', forth))]
    ppermute x10 -> x8, waiting for transfers between devices: 9.12 us -> 6.95 us  [send_far(): lax.ppermute(cut, 'blk', ring_shift(blks, by))]
    pallas_call x1, Pallas kernels: 3.74 us -> 1.57 us  [weigh_rows(): pl.pallas_call(functools.partial(weigh_kernel, groups), grid=(1,), in_spe...]
  transfers between devices with their start and end apart: 23 -> 24, of which waited for: 10 -> 14; matrix products, arithmetic and copies ran while one was open for 0% -> 0% of each run, Pallas kernels for 22% -> 25%
where the time goes in v3:
time: 112 us
  waiting for transfers between devices  48.1 us (43%)
  Pallas kernels  29.6 us (26%)
  starting transfers between devices  28.8 us (26%)
  local copies, waits for them, and re-layouts  5.58 us (5%)
    pallas_call x4, Pallas kernels, near_chunk(): pl.pallas_call(near_kernel, grid=(width // unit,), in_specs=[pl.BlockSpec...  15.3 us
    ppermute x1, waiting for transfers between devices, shards(): moved = lax.ppermute(held, 'tile', swap(tiles, members))  12.1 us
    pallas_call x4, Pallas kernels, band_chunk(): pl.pallas_call(kernel, grid=(steps,), in_specs=specs + [token_spec()], ou...  10.3 us
    ppermute x1, waiting for transfers between devices, shards(): moved = lax.ppermute(held, 'tile', swap(tiles, bit * members))  9.31 us
    ppermute x8, starting transfers between devices, send_far(): lax.ppermute(cut, 'blk', ring_shift(blks, by))  8.39 us
    ppermute x8, waiting for transfers between devices, send_far(): lax.ppermute(cut, 'blk', ring_shift(blks, by))  6.95 us
    ppermute x3, waiting for transfers between devices, send_slab(): behind.append(lax.ppermute(behind[-1] if behind else piece, 'blk', back))  6.58 us
    ppermute x3, waiting for transfers between devices, shards(): lax.ppermute(blocks[distance], 'tile', swap(tiles, distance * members))  6.06 us
  transfers between devices with their start and end apart: 24, of which 14 were waited for; matrix products, arithmetic and copies ran while one was open for 0% of the time, Pallas kernels for 25%

profile of v3, /device:TPU:0, one launch (start us, length us, event | category | flops | bytes accessed | tf_op | source)
XLA Modules:
  0.0 112.3 jit_solution(4029847771959036481)
XLA Ops:
  0.0 1.3 %slice.3.refs_6_ = bf16[256,2048]{1,0:T(8,128)(2,1)S(1)} slice(bf16[256,6144]{1,0:T(8,128)(2,1)} %refs_1_.9), slice={[0:256], [0:2048]} | slice | bytes 2097152 | tf_op jit(solution)/shard_map/slice | solution.py:351
  1.3 3.0 %collective-permute-start.7 = (bf16[256,2048]{1,0:T(8,128)(2,1)S(1)}, bf16[256,2048]{1,0:T(8,128)(2,1)S(1)}, u32[]{:S(2)}, u32[]{:S(2)}) collective-permute-start(bf16[256,2048]{1,0:T(8,128)(2,1)S(1)} %slice.3.refs_6_), channel_id=1, source_target_pairs={{0,16},{8,0},{24,8},{16,24},{1,17},{9,1},{25,9},{17,25},{2,18},{10... | collective-permute-start | bytes 3145736 | tf_op jit(solution)/shard_map/ppermute | solution.py:221
  4.4 0.9 copy-done.2
  5.3 0.7 copy-done.3
  6.0 0.7 copy-done.4
  6.7 0.7 copy-done.5
  7.3 0.7 copy-done.6
  8.0 0.7 copy-done.7
  8.6 1.6 %shard_map.73 = (bf16[64,512]{1,0:T(8,128)(2,1)S(1)}, bf16[64,512]{1,0:T(8,128)(2,1)S(1)}, bf16[64,512]{1,0:T(8,128)(2,1)S(1)}, bf16[64,512]{1,0:T(8,128)(2,1)S(1)}) custom-call(s32[8]{0:T(128)S(1)} %copy-done.5, s32[8]{0:T(128)S(1)} %copy-done.6, s32[8]{0:T(128)S(1)} %copy-done.7, bf16[256,512]{1,0:T(8,128)(2,1)S(1)} %copy-done.2, f32[1,256]{1,0:T(1,128)S(1)} %bitcast.11, ...), custom_call_target="tpu_custom_call" | custom-call | flops 99999997952 | tf_op jit(solution)/shard_map/pallas_call | solution.py:101
  10.2 2.1 %collective-permute-start = (bf16[64,512]{1,0:T(8,128)(2,1)S(1)}, bf16[64,512]{1,0:T(8,128)(2,1)S(1)}, u32[]{:S(2)}, u32[]{:S(2)}) collective-permute-start(bf16[64,512]{1,0:T(8,128)(2,1)S(1)} %get-tuple-element.52), channel_id=1, source_target_pairs={{0,2},{1,3},{2,0},{3,1},{4,6},{5,7},{6,4},{7,5},{8,10},{9,11},{10,... | collective-permute-start | bytes 196616 | tf_op jit(solution)/shard_map/ppermute | solution.py:357
  12.3 2.6 %collective-permute-start.1 = (bf16[64,512]{1,0:T(8,128)(2,1)S(1)}, bf16[64,512]{1,0:T(8,128)(2,1)S(1)}, u32[]{:S(2)}, u32[]{:S(2)}) collective-permute-start(bf16[64,512]{1,0:T(8,128)(2,1)S(1)} %get-tuple-element.53), channel_id=1, source_target_pairs={{0,4},{1,5},{2,6},{3,7},{4,0},{5,1},{6,2},{7,3},{8,12},{9,13},{10,... | collective-permute-start | bytes 196616 | tf_op jit(solution)/shard_map/ppermute | solution.py:357
  14.9 4.1 %collective-permute-done.1.refs_2_ = bf16[64,512]{1,0:T(8,128)(2,1)S(1)} collective-permute-done((bf16[64,512]{1,0:T(8,128)(2,1)S(1)}, bf16[64,512]{1,0:T(8,128)(2,1)S(1)}, u32[]{:S(2)}, u32[]{:S(2)}) %collective-permute-start.1) | collective-permute-done | bytes 65568 | tf_op jit(solution)/shard_map/ppermute | solution.py:357
  19.0 2.0 %collective-permute-done.2.refs_3_ = bf16[64,512]{1,0:T(8,128)(2,1)S(1)} collective-permute-done((bf16[64,512]{1,0:T(8,128)(2,1)S(1)}, bf16[64,512]{1,0:T(8,128)(2,1)S(1)}, u32[]{:S(2)}, u32[]{:S(2)}) %collective-permute-start.2) | collective-permute-done | bytes 65568 | tf_op jit(solution)/shard_map/ppermute | solution.py:357
  21.0 1.5 %collective-permute-start.3 = (bf16[64,512]{1,0:T(8,128)(2,1)S(1)}, bf16[64,512]{1,0:T(8,128)(2,1)S(1)}, u32[]{:S(2)}, u32[]{:S(2)}) collective-permute-start(bf16[64,512]{1,0:T(8,128)(2,1)S(1)} %get-tuple-element.56), channel_id=1, source_target_pairs={{0,8},{8,24},{24,16},{16,0},{1,9},{9,25},{25,17},{17,1},{2,10},{10... | collective-permute-start | bytes 196616 | tf_op jit(solution)/shard_map/ppermute | solution.py:360
  22.6 1.5 %collective-permute-start.4 = (bf16[64,512]{1,0:T(8,128)(2,1)S(1)}, bf16[64,512]{1,0:T(8,128)(2,1)S(1)}, u32[]{:S(2)}, u32[]{:S(2)}) collective-permute-start(bf16[64,512]{1,0:T(8,128)(2,1)S(1)} %get-tuple-element.57), channel_id=1, source_target_pairs={{0,24},{8,16},{24,0},{16,8},{1,25},{9,17},{25,1},{17,9},{2,26},{10... | collective-permute-start | bytes 196616 | tf_op jit(solution)/shard_map/ppermute | solution.py:360
  24.1 1.5 %collective-permute-start.5 = (bf16[64,512]{1,0:T(8,128)(2,1)S(1)}, bf16[64,512]{1,0:T(8,128)(2,1)S(1)}, u32[]{:S(2)}, u32[]{:S(2)}) collective-permute-start(bf16[64,512]{1,0:T(8,128)(2,1)S(1)} %get-tuple-element.58), channel_id=1, source_target_pairs={{0,16},{8,0},{24,8},{16,24},{1,17},{9,1},{25,9},{17,25},{2,18},{10... | collective-permute-start | bytes 196616 | tf_op jit(solution)/shard_map/ppermute | solution.py:360
  25.5 0.7 shard_map.75
  26.3 2.7 %collective-permute-done.7.behind.refs_3_ = bf16[256,2048]{1,0:T(8,128)(2,1)S(1)} collective-permute-done((bf16[256,2048]{1,0:T(8,128)(2,1)S(1)}, bf16[256,2048]{1,0:T(8,128)(2,1)S(1)}, u32[]{:S(2)}, u32[]{:S(2)}) %collective-permute-start.7) | collective-permute-done | bytes 1048608 | tf_op jit(solution)/shard_map/ppermute | solution.py:221
  29.0 2.6 %collective-permute-start.15 = (bf16[256,3328]{1,0:T(8,128)(2,1)S(1)}, bf16[256,3328]{1,0:T(8,128)(2,1)S(1)}, u32[]{:S(2)}, u32[]{:S(2)}) collective-permute-start(bf16[256,3328]{1,0:T(8,128)(2,1)S(1)} %get-tuple-element.71), channel_id=1, source_target_pairs={{0,16},{8,0},{24,8},{16,24},{1,17},{9,1},{25,9},{17,25},{2,18},{10... | collective-permute-start | bytes 5111816 | tf_op jit(solution)/shard_map/ppermute | solution.py:221
  31.7 2.1 %collective-permute-done.4.refs_2_ = bf16[64,512]{1,0:T(8,128)(2,1)S(1)} collective-permute-done((bf16[64,512]{1,0:T(8,128)(2,1)S(1)}, bf16[64,512]{1,0:T(8,128)(2,1)S(1)}, u32[]{:S(2)}, u32[]{:S(2)}) %collective-permute-start.4) | collective-permute-done | bytes 65568 | tf_op jit(solution)/shard_map/ppermute | solution.py:360
  33.9 2.7 %collective-permute-start.8 = (bf16[1,4,64,512]{3,2,1,0:T(8,128)(2,1)S(1)}, bf16[1,4,64,512]{3,2,1,0:T(8,128)(2,1)S(1)}, u32[]{:S(2)}, u32[]{:S(2)}) collective-permute-start(bf16[1,4,64,512]{3,2,1,0:T(8,128)(2,1)S(1)} %bitcast.9), channel_id=1, source_target_pairs={{0,4},{1,5},{2,6},{3,7},{4,0},{5,1},{6,2},{7,3},{8,12},{9,13},{10,... | collective-permute-start | bytes 786440 | tf_op jit(solution)/shard_map/ppermute | solution.py:394
  36.5 9.3 %collective-permute-done.8.refs_1_ = bf16[1,4,64,512]{3,2,1,0:T(8,128)(2,1)S(1)} collective-permute-done((bf16[1,4,64,512]{3,2,1,0:T(8,128)(2,1)S(1)}, bf16[1,4,64,512]{3,2,1,0:T(8,128)(2,1)S(1)}, u32[]{:S(2)}, u32[]{:S(2)}) %collective-permute-start.8) | collective-permute-done | bytes 262176 | tf_op jit(solution)/shard_map/ppermute | solution.py:394
  45.9 0.7 collective-permute-start.9
  46.6 12.1 %collective-permute-done.9.refs_1_ = bf16[2,4,64,512]{3,2,1,0:T(8,128)(2,1)S(1)} collective-permute-done((bf16[2,4,64,512]{3,2,1,0:T(8,128)(2,1)S(1)}, bf16[2,4,64,512]{3,2,1,0:T(8,128)(2,1)S(1)}, u32[]{:S(2)}, u32[]{:S(2)}) %collective-permute-start.9) | collective-permute-done | bytes 524320 | tf_op jit(solution)/shard_map/ppermute | solution.py:399
  58.7 2.0 %collective-permute-start.13 = (bf16[128,2048]{1,0:T(8,128)(2,1)S(1)}, bf16[128,2048]{1,0:T(8,128)(2,1)S(1)}, u32[]{:S(2)}, u32[]{:S(2)}) collective-permute-start(bf16[128,2048]{1,0:T(8,128)(2,1)S(1)} %get-tuple-element.70), channel_id=1, source_target_pairs={{0,16},{8,0},{24,8},{16,24},{1,17},{9,1},{25,9},{17,25},{2,18},{10... | collective-permute-start | bytes 1572872 | tf_op jit(solution)/shard_map/ppermute | solution.py:258
  60.8 0.8 shard_map.79
  61.6 4.7 %shard_map.80 = (f32[1024,2048]{1,0:T(8,128)S(1)}, bf16[16,128]{1,0:T(8,128)(2,1)S(1)}) custom-call(bf16[1024,1024]{1,0:T(8,128)(2,1)S(1)} %get-tuple-element.66.refs_0_.weights.refs_1_, bf16[256,6144]{1,0:T(8,128)(2,1)S(1)} %copy-done, bf16[256,2048]{1,0:T(8,128)(2,1)S(1)} %collective-permute-done.6.ahead.refs_2_, ...), custom_call_target="tpu_custom_call" | custom-call | flops 1000000 | tf_op jit(solution)/shard_map/pallas_call | solution.py:298
  66.3 3.0 %collective-permute-done.15.refs_2_.refs_3_.behind = bf16[256,3328]{1,0:T(8,128)(2,1)S(1)} collective-permute-done((bf16[256,3328]{1,0:T(8,128)(2,1)S(1)}, bf16[256,3328]{1,0:T(8,128)(2,1)S(1)}, u32[]{:S(2)}, u32[]{:S(2)}) %collective-permute-start.15) | collective-permute-done | bytes 1703968 | tf_op jit(solution)/shard_map/ppermute | solution.py:221
  69.3 2.5 %collective-permute-done.14.refs_1_.refs_2_.ahead = bf16[256,3328]{1,0:T(8,128)(2,1)S(1)} collective-permute-done((bf16[256,3328]{1,0:T(8,128)(2,1)S(1)}, bf16[256,3328]{1,0:T(8,128)(2,1)S(1)}, u32[]{:S(2)}, u32[]{:S(2)}) %collective-permute-start.14) | collective-permute-done | bytes 1703968 | tf_op jit(solution)/shard_map/ppermute | solution.py:220
  72.3 1.8 %collective-permute-start.18 = (bf16[256,768]{1,0:T(8,128)(2,1)S(1)}, bf16[256,768]{1,0:T(8,128)(2,1)S(1)}, u32[]{:S(2)}, u32[]{:S(2)}) collective-permute-start(bf16[256,768]{1,0:T(8,128)(2,1)S(1)} %get-tuple-element.81), channel_id=1, source_target_pairs={{0,8},{8,24},{24,16},{16,0},{1,9},{9,25},{25,17},{17,1},{2,10},{10... | collective-permute-start | bytes 1179656 | tf_op jit(solution)/shard_map/ppermute | solution.py:220
  74.1 3.7 %shard_map.82 = (f32[1024,1536]{1,0:T(8,128)S(1)}, bf16[16,128]{1,0:T(8,128)(2,1)S(1)}) custom-call(bf16[1024,1024]{1,0:T(8,128)(2,1)S(1)} %get-tuple-element.66.refs_0_.weights.refs_1_, bf16[256,6144]{1,0:T(8,128)(2,1)S(1)} %copy-done, bf16[256,3328]{1,0:T(8,128)(2,1)S(1)} %collective-permute-done.14.refs_1_.refs_2_.ahead, ...), custom_call_target="tpu_custom_call" | custom-call | flops 1000000 | tf_op jit(solution)/shard_map/pallas_call | solution.py:298
  77.8 4.9 %shard_map.83 = (f32[1024,1792]{1,0:T(8,128)S(1)}, bf16[16,128]{1,0:T(8,128)(2,1)S(1)}) custom-call(bf16[1024,1024]{1,0:T(8,128)(2,1)S(1)} %get-tuple-element.66.refs_0_.weights.refs_1_, bf16[256,6144]{1,0:T(8,128)(2,1)S(1)} %copy-done, bf16[256,3328]{1,0:T(8,128)(2,1)S(1)} %collective-permute-done.14.refs_1_.refs_2_.ahead, ...), custom_call_target="tpu_custom_call" | custom-call | flops 1000000 | tf_op jit(solution)/shard_map/pallas_call | solution.py:298
  82.6 0.4 collective-permute-done.12.refs_1_.refs_0_
  83.4 1.8 %collective-permute-start.16 = (bf16[112,1536]{1,0:T(8,128)(2,1)S(1)}, bf16[112,1536]{1,0:T(8,128)(2,1)S(1)}, u32[]{:S(2)}, u32[]{:S(2)}) collective-permute-start(bf16[112,1536]{1,0:T(8,128)(2,1)S(1)} %get-tuple-element.79), channel_id=1, source_target_pairs={{0,8},{8,24},{24,16},{16,0},{1,9},{9,25},{25,17},{17,1},{2,10},{10... | collective-permute-start | bytes 1032200 | tf_op jit(solution)/shard_map/ppermute | solution.py:258
  85.1 2.9 %shard_map.85 = (bf16[1024,6144]{1,0:T(8,128)(2,1)}, bf16[16,128]{1,0:T(8,128)(2,1)S(1)}) custom-call(f32[1024,2048]{1,0:T(8,128)S(1)} %get-tuple-element.68.near, bf16[1024,1024]{1,0:T(8,128)(2,1)S(1)} %get-tuple-element.66.refs_0_.weights.refs_1_, bf16[128,2048]{1,0:T(8,128)(2,1)S(1)} %collective-permute-done.12.refs_1_.refs_0_, ...), custom_call_target="tpu_custom_call" | custom-call | flops 1000000 | tf_op jit(solution)/shard_map/pallas_call | solution.py:331
  88.1 0.8 collective-permute-done.19.refs_2_.refs_3_.behind
  88.9 2.5 %collective-permute-done.18.refs_1_.refs_2_.ahead = bf16[256,768]{1,0:T(8,128)(2,1)S(1)} collective-permute-done((bf16[256,768]{1,0:T(8,128)(2,1)S(1)}, bf16[256,768]{1,0:T(8,128)(2,1)S(1)}, u32[]{:S(2)}, u32[]{:S(2)}) %collective-permute-start.18) | collective-permute-done | bytes 393248 | tf_op jit(solution)/shard_map/ppermute | solution.py:220
  91.4 0.4 shard_map.86
  91.9 2.0 %collective-permute-start.21 = (bf16[128,1792]{1,0:T(8,128)(2,1)S(1)}, bf16[128,1792]{1,0:T(8,128)(2,1)S(1)}, u32[]{:S(2)}, u32[]{:S(2)}) collective-permute-start(bf16[128,1792]{1,0:T(8,128)(2,1)S(1)} %get-tuple-element.89), channel_id=1, source_target_pairs={{0,16},{8,0},{24,8},{16,24},{1,17},{9,1},{25,9},{17,25},{2,18},{10... | collective-permute-start | bytes 1376264 | tf_op jit(solution)/shard_map/ppermute | solution.py:258
  94.0 2.1 %shard_map.87 = (f32[1024,768]{1,0:T(8,128)S(1)}, bf16[16,128]{1,0:T(8,128)(2,1)S(1)}) custom-call(bf16[1024,1024]{1,0:T(8,128)(2,1)S(1)} %get-tuple-element.66.refs_0_.weights.refs_1_, bf16[256,6144]{1,0:T(8,128)(2,1)S(1)} %copy-done, bf16[256,768]{1,0:T(8,128)(2,1)S(1)} %collective-permute-done.18.refs_1_.refs_2_.ahead, ...), custom_call_target="tpu_custom_call" | custom-call | flops 1000000 | tf_op jit(solution)/shard_map/pallas_call | solution.py:298
  96.0 2.8 %collective-permute-done.16.refs_1_.refs_2_ = bf16[112,1536]{1,0:T(8,128)(2,1)S(1)} collective-permute-done((bf16[112,1536]{1,0:T(8,128)(2,1)S(1)}, bf16[112,1536]{1,0:T(8,128)(2,1)S(1)}, u32[]{:S(2)}, u32[]{:S(2)}) %collective-permute-start.16) | collective-permute-done | bytes 344096 | tf_op jit(solution)/shard_map/ppermute | solution.py:258
  98.8 1.1 collective-permute-start.22
  100.0 1.1 collective-permute-start.23
  101.1 3.0 %shard_map.89 = (bf16[1024,6144]{1,0:T(8,128)(2,1)}, bf16[16,128]{1,0:T(8,128)(2,1)S(1)}) custom-call(bf16[1024,6144]{1,0:T(8,128)(2,1)} %get-tuple-element.77._, f32[1024,1536]{1,0:T(8,128)S(1)} %bitcast.5, bf16[1024,1024]{1,0:T(8,128)(2,1)S(1)} %get-tuple-element.66.refs_0_.weights.refs_1_, ...), custom_call_target="tpu_custom_call", output_to_operand_aliasing={{0}: (0, {})} | custom-call | flops 1000000 | tf_op jit(solution)/shard_map/pallas_call | solution.py:331
  104.0 3.2 %collective-permute-done.20.refs_2_ = bf16[128,1792]{1,0:T(8,128)(2,1)S(1)} collective-permute-done((bf16[128,1792]{1,0:T(8,128)(2,1)S(1)}, bf16[128,1792]{1,0:T(8,128)(2,1)S(1)}, u32[]{:S(2)}, u32[]{:S(2)}) %collective-permute-start.20) | collective-permute-done | bytes 458784 | tf_op jit(solution)/shard_map/ppermute | solution.py:258
  107.2 0.6 collective-permute-done.21.refs_3_
  107.8 2.7 %shard_map.90 = (bf16[1024,6144]{1,0:T(8,128)(2,1)}, bf16[16,128]{1,0:T(8,128)(2,1)S(1)}) custom-call(bf16[1024,6144]{1,0:T(8,128)(2,1)} %get-tuple-element.86._, f32[1024,1792]{1,0:T(8,128)S(1)} %get-tuple-element.87.refs_0_, bf16[1024,1024]{1,0:T(8,128)(2,1)S(1)} %get-tuple-element.66.refs_0_.weights.refs_1_, ...), custom_call_target="tpu_custom_call", output_to_operand_aliasing={{0}: (0, {})} | custom-call | flops 1000000 | tf_op jit(solution)/shard_map/pallas_call | solution.py:331
  110.5 1.7 %shard_map.91 = (bf16[1024,6144]{1,0:T(8,128)(2,1)}, bf16[16,128]{1,0:T(8,128)(2,1)}) custom-call(bf16[1024,6144]{1,0:T(8,128)(2,1)} %get-tuple-element.91._, f32[1024,768]{1,0:T(8,128)S(1)} %get-tuple-element.92.refs_0_, bf16[1024,1024]{1,0:T(8,128)(2,1)S(1)} %get-tuple-element.66.refs_0_.weights.refs_1_, ...), custom_call_target="tpu_custom_call", output_to_operand_aliasing={{0}: (0, {})} | custom-call | flops 1000000 | tf_op jit(solution)/shard_map/pallas_call | solution.py:331
  (41 shorter events, 1.2 us)
Async XLA Ops:
  1.3 27.7 %collective-permute-start.7 = (bf16[256,2048]{1,0:T(8,128)(2,1)S(1)}, bf16[256,2048]{1,0:T(8,128)(2,1)S(1)}, u32[]{:S(2)}, u32[]{:S(2)}) collective-permute-start(bf16[256,2048]{1,0:T(8,128)(2,1)S(1)} %slice.3.refs_6_), channel_id=1, source_target_pairs={{0,16},{8,0},{24,8},{16,24},{1,17},{9,1},{25,9},{17,25},{2,18},{10... | collective-permute-start | bytes 3145736 | tf_op jit(solution)/shard_map/ppermute | solution.py:221
  4.3 27.3 %collective-permute-start.6 = (bf16[256,2048]{1,0:T(8,128)(2,1)S(1)}, bf16[256,2048]{1,0:T(8,128)(2,1)S(1)}, u32[]{:S(2)}, u32[]{:S(2)}) collective-permute-start(bf16[256,2048]{1,0:T(8,128)(2,1)S(1)} %slice.3.refs_6_), channel_id=1, source_target_pairs={{0,8},{8,24},{24,16},{16,0},{1,9},{9,25},{25,17},{17,1},{2,10},{10... | collective-permute-start | bytes 3145736 | tf_op jit(solution)/shard_map/ppermute | solution.py:220
  4.4 0.9 copy-start.2
  5.3 0.7 copy-start.3
  6.0 0.7 copy-start.4
  6.7 0.7 copy-start.5
  7.3 0.7 copy-start.6
  8.0 0.7 copy-start.7
  8.6 16.9 %copy-start = (bf16[256,6144]{1,0:T(8,128)(2,1)S(1)}, bf16[256,6144]{1,0:T(8,128)(2,1)}, u32[]{:S(2)}) copy-start(bf16[256,6144]{1,0:T(8,128)(2,1)} %refs_1_.9) | copy-start | bytes 9437188
  10.2 4.7 %collective-permute-start = (bf16[64,512]{1,0:T(8,128)(2,1)S(1)}, bf16[64,512]{1,0:T(8,128)(2,1)S(1)}, u32[]{:S(2)}, u32[]{:S(2)}) collective-permute-start(bf16[64,512]{1,0:T(8,128)(2,1)S(1)} %get-tuple-element.52), channel_id=1, source_target_pairs={{0,2},{1,3},{2,0},{3,1},{4,6},{5,7},{6,4},{7,5},{8,10},{9,11},{10,... | collective-permute-start | bytes 196616 | tf_op jit(solution)/shard_map/ppermute | solution.py:357
  12.3 6.7 %collective-permute-start.1 = (bf16[64,512]{1,0:T(8,128)(2,1)S(1)}, bf16[64,512]{1,0:T(8,128)(2,1)S(1)}, u32[]{:S(2)}, u32[]{:S(2)}) collective-permute-start(bf16[64,512]{1,0:T(8,128)(2,1)S(1)} %get-tuple-element.53), channel_id=1, source_target_pairs={{0,4},{1,5},{2,6},{3,7},{4,0},{5,1},{6,2},{7,3},{8,12},{9,13},{10,... | collective-permute-start | bytes 196616 | tf_op jit(solution)/shard_map/ppermute | solution.py:357
  14.9 6.1 %collective-permute-start.2 = (bf16[64,512]{1,0:T(8,128)(2,1)S(1)}, bf16[64,512]{1,0:T(8,128)(2,1)S(1)}, u32[]{:S(2)}, u32[]{:S(2)}) collective-permute-start(bf16[64,512]{1,0:T(8,128)(2,1)S(1)} %get-tuple-element.54), channel_id=1, source_target_pairs={{0,6},{1,7},{2,4},{3,5},{4,2},{5,3},{6,0},{7,1},{8,14},{9,15},{10,... | collective-permute-start | bytes 196616 | tf_op jit(solution)/shard_map/ppermute | solution.py:357
  21.0 10.7 %collective-permute-start.3 = (bf16[64,512]{1,0:T(8,128)(2,1)S(1)}, bf16[64,512]{1,0:T(8,128)(2,1)S(1)}, u32[]{:S(2)}, u32[]{:S(2)}) collective-permute-start(bf16[64,512]{1,0:T(8,128)(2,1)S(1)} %get-tuple-element.56), channel_id=1, source_target_pairs={{0,8},{8,24},{24,16},{16,0},{1,9},{9,25},{25,17},{17,1},{2,10},{10... | collective-permute-start | bytes 196616 | tf_op jit(solution)/shard_map/ppermute | solution.py:360
  22.6 11.3 %collective-permute-start.4 = (bf16[64,512]{1,0:T(8,128)(2,1)S(1)}, bf16[64,512]{1,0:T(8,128)(2,1)S(1)}, u32[]{:S(2)}, u32[]{:S(2)}) collective-permute-start(bf16[64,512]{1,0:T(8,128)(2,1)S(1)} %get-tuple-element.57), channel_id=1, source_target_pairs={{0,24},{8,16},{24,0},{16,8},{1,25},{9,17},{25,1},{17,9},{2,26},{10... | collective-permute-start | bytes 196616 | tf_op jit(solution)/shard_map/ppermute | solution.py:360
  24.1 9.8 %collective-permute-start.5 = (bf16[64,512]{1,0:T(8,128)(2,1)S(1)}, bf16[64,512]{1,0:T(8,128)(2,1)S(1)}, u32[]{:S(2)}, u32[]{:S(2)}) collective-permute-start(bf16[64,512]{1,0:T(8,128)(2,1)S(1)} %get-tuple-element.58), channel_id=1, source_target_pairs={{0,16},{8,0},{24,8},{16,24},{1,17},{9,1},{25,9},{17,25},{2,18},{10... | collective-permute-start | bytes 196616 | tf_op jit(solution)/shard_map/ppermute | solution.py:360
  29.0 40.3 %collective-permute-start.15 = (bf16[256,3328]{1,0:T(8,128)(2,1)S(1)}, bf16[256,3328]{1,0:T(8,128)(2,1)S(1)}, u32[]{:S(2)}, u32[]{:S(2)}) collective-permute-start(bf16[256,3328]{1,0:T(8,128)(2,1)S(1)} %get-tuple-element.71), channel_id=1, source_target_pairs={{0,16},{8,0},{24,8},{16,24},{1,17},{9,1},{25,9},{17,25},{2,18},{10... | collective-permute-start | bytes 5111816 | tf_op jit(solution)/shard_map/ppermute | solution.py:221
  31.6 40.1 %collective-permute-start.14 = (bf16[256,3328]{1,0:T(8,128)(2,1)S(1)}, bf16[256,3328]{1,0:T(8,128)(2,1)S(1)}, u32[]{:S(2)}, u32[]{:S(2)}) collective-permute-start(bf16[256,3328]{1,0:T(8,128)(2,1)S(1)} %get-tuple-element.71), channel_id=1, source_target_pairs={{0,8},{8,24},{24,16},{16,0},{1,9},{9,25},{25,17},{17,1},{2,10},{10... | collective-permute-start | bytes 5111816 | tf_op jit(solution)/shard_map/ppermute | solution.py:220
  33.9 12.0 %collective-permute-start.8 = (bf16[1,4,64,512]{3,2,1,0:T(8,128)(2,1)S(1)}, bf16[1,4,64,512]{3,2,1,0:T(8,128)(2,1)S(1)}, u32[]{:S(2)}, u32[]{:S(2)}) collective-permute-start(bf16[1,4,64,512]{3,2,1,0:T(8,128)(2,1)S(1)} %bitcast.9), channel_id=1, source_target_pairs={{0,4},{1,5},{2,6},{3,7},{4,0},{5,1},{6,2},{7,3},{8,12},{9,13},{10,... | collective-permute-start | bytes 786440 | tf_op jit(solution)/shard_map/ppermute | solution.py:394
  45.9 12.8 %collective-permute-start.9 = (bf16[2,4,64,512]{3,2,1,0:T(8,128)(2,1)S(1)}, bf16[2,4,64,512]{3,2,1,0:T(8,128)(2,1)S(1)}, u32[]{:S(2)}, u32[]{:S(2)}) collective-permute-start(bf16[2,4,64,512]{3,2,1,0:T(8,128)(2,1)S(1)} %bitcast.6), channel_id=1, source_target_pairs={{0,2},{1,3},{2,0},{3,1},{4,6},{5,7},{6,4},{7,5},{8,10},{9,11},{10,... | collective-permute-start | bytes 1572872 | tf_op jit(solution)/shard_map/ppermute | solution.py:399
  46.6 12.1 %collective-permute-start.10 = (bf16[2,4,64,512]{3,2,1,0:T(8,128)(2,1)S(1)}, bf16[2,4,64,512]{3,2,1,0:T(8,128)(2,1)S(1)}, u32[]{:S(2)}, u32[]{:S(2)}) collective-permute-start(bf16[2,4,64,512]{3,2,1,0:T(8,128)(2,1)S(1)} %bitcast.7), channel_id=1, source_target_pairs={{0,1},{1,0},{2,3},{3,2},{4,5},{5,4},{6,7},{7,6},{8,9},{9,8},{10,11... | collective-permute-start | bytes 1572872 | tf_op jit(solution)/shard_map/ppermute | solution.py:404
  58.7 2.0 %collective-permute-start.11 = (bf16[2,4,64,512]{3,2,1,0:T(8,128)(2,1)S(1)}, bf16[2,4,64,512]{3,2,1,0:T(8,128)(2,1)S(1)}, u32[]{:S(2)}, u32[]{:S(2)}) collective-permute-start(bf16[2,4,64,512]{3,2,1,0:T(8,128)(2,1)S(1)} %collective-permute-done.9.refs_1_), channel_id=1, source_target_pairs={{0,1},{1,0},{2,3},{3,2},{4,5},{5,4},{6,7},{7,6},{8,9},{9,8},{10,11... | collective-permute-start | bytes 1572872 | tf_op jit(solution)/shard_map/ppermute | solution.py:404
  58.7 24.3 %collective-permute-start.12 = (bf16[128,2048]{1,0:T(8,128)(2,1)S(1)}, bf16[128,2048]{1,0:T(8,128)(2,1)S(1)}, u32[]{:S(2)}, u32[]{:S(2)}) collective-permute-start(bf16[128,2048]{1,0:T(8,128)(2,1)S(1)} %get-tuple-element.69), channel_id=1, source_target_pairs={{0,8},{8,24},{24,16},{16,0},{1,9},{9,25},{25,17},{17,1},{2,10},{10... | collective-permute-start | bytes 1572872 | tf_op jit(solution)/shard_map/ppermute | solution.py:258
  58.7 24.3 %collective-permute-start.13 = (bf16[128,2048]{1,0:T(8,128)(2,1)S(1)}, bf16[128,2048]{1,0:T(8,128)(2,1)S(1)}, u32[]{:S(2)}, u32[]{:S(2)}) collective-permute-start(bf16[128,2048]{1,0:T(8,128)(2,1)S(1)} %get-tuple-element.70), channel_id=1, source_target_pairs={{0,16},{8,0},{24,8},{16,24},{1,17},{9,1},{25,9},{17,25},{2,18},{10... | collective-permute-start | bytes 1572872 | tf_op jit(solution)/shard_map/ppermute | solution.py:258
  72.0 17.0 %collective-permute-start.19 = (bf16[256,768]{1,0:T(8,128)(2,1)S(1)}, bf16[256,768]{1,0:T(8,128)(2,1)S(1)}, u32[]{:S(2)}, u32[]{:S(2)}) collective-permute-start(bf16[256,768]{1,0:T(8,128)(2,1)S(1)} %get-tuple-element.81), channel_id=1, source_target_pairs={{0,16},{8,0},{24,8},{16,24},{1,17},{9,1},{25,9},{17,25},{2,18},{10... | collective-permute-start | bytes 1179656 | tf_op jit(solution)/shard_map/ppermute | solution.py:221
  72.3 19.2 %collective-permute-start.18 = (bf16[256,768]{1,0:T(8,128)(2,1)S(1)}, bf16[256,768]{1,0:T(8,128)(2,1)S(1)}, u32[]{:S(2)}, u32[]{:S(2)}) collective-permute-start(bf16[256,768]{1,0:T(8,128)(2,1)S(1)} %get-tuple-element.81), channel_id=1, source_target_pairs={{0,8},{8,24},{24,16},{16,0},{1,9},{9,25},{25,17},{17,1},{2,10},{10... | collective-permute-start | bytes 1179656 | tf_op jit(solution)/shard_map/ppermute | solution.py:220
  77.7 5.3 %copy-start.1 = (f32[1024,1536]{1,0:T(8,128)}, f32[1024,1536]{1,0:T(8,128)S(1)}, u32[]{:S(2)}) copy-start(f32[1024,1536]{1,0:T(8,128)S(1)} %get-tuple-element.78.refs_0_) | copy-start | bytes 18874372
  83.1 15.7 %collective-permute-start.17 = (bf16[144,1536]{1,0:T(8,128)(2,1)S(1)}, bf16[144,1536]{1,0:T(8,128)(2,1)S(1)}, u32[]{:S(2)}, u32[]{:S(2)}) collective-permute-start(bf16[144,1536]{1,0:T(8,128)(2,1)S(1)} %get-tuple-element.80), channel_id=1, source_target_pairs={{0,16},{8,0},{24,8},{16,24},{1,17},{9,1},{25,9},{17,25},{2,18},{10... | collective-permute-start | bytes 1327112 | tf_op jit(solution)/shard_map/ppermute | solution.py:258
  83.4 15.4 %collective-permute-start.16 = (bf16[112,1536]{1,0:T(8,128)(2,1)S(1)}, bf16[112,1536]{1,0:T(8,128)(2,1)S(1)}, u32[]{:S(2)}, u32[]{:S(2)}) collective-permute-start(bf16[112,1536]{1,0:T(8,128)(2,1)S(1)} %get-tuple-element.79), channel_id=1, source_target_pairs={{0,8},{8,24},{24,16},{16,0},{1,9},{9,25},{25,17},{17,1},{2,10},{10... | collective-permute-start | bytes 1032200 | tf_op jit(solution)/shard_map/ppermute | solution.py:258
  88.1 13.0 %slice-start = ((s8[6291456]{0:T(1024)(128)(4,1)}), s8[4194304]{0:T(1024)(128)(4,1)S(1)}, s32[]{:S(2)}) async-start(s8[6291456]{0:T(1024)(128)(4,1)} %bitcast.4), calls=%async_computation | async-start | bytes 8388608
  91.9 15.4 %collective-permute-start.20 = (bf16[128,1792]{1,0:T(8,128)(2,1)S(1)}, bf16[128,1792]{1,0:T(8,128)(2,1)S(1)}, u32[]{:S(2)}, u32[]{:S(2)}) collective-permute-start(bf16[128,1792]{1,0:T(8,128)(2,1)S(1)} %get-tuple-element.88), channel_id=1, source_target_pairs={{0,8},{8,24},{24,16},{16,0},{1,9},{9,25},{25,17},{17,1},{2,10},{10... | collective-permute-start | bytes 1376264 | tf_op jit(solution)/shard_map/ppermute | solution.py:258
  91.9 15.9 %collective-permute-start.21 = (bf16[128,1792]{1,0:T(8,128)(2,1)S(1)}, bf16[128,1792]{1,0:T(8,128)(2,1)S(1)}, u32[]{:S(2)}, u32[]{:S(2)}) collective-permute-start(bf16[128,1792]{1,0:T(8,128)(2,1)S(1)} %get-tuple-element.89), channel_id=1, source_target_pairs={{0,16},{8,0},{24,8},{16,24},{1,17},{9,1},{25,9},{17,25},{2,18},{10... | collective-permute-start | bytes 1376264 | tf_op jit(solution)/shard_map/ppermute | solution.py:258
  94.0 7.1 %slice-start.1 = ((s8[6291456]{0:T(1024)(128)(4,1)}), s8[2097152]{0:T(1024)(128)(4,1)S(1)}, s32[]{:S(2)}) async-start(s8[6291456]{0:T(1024)(128)(4,1)} %bitcast.4), calls=%async_computation.1 | async-start | bytes 4194304
  98.8 11.7 %collective-permute-start.22 = (bf16[128,768]{1,0:T(8,128)(2,1)S(1)}, bf16[128,768]{1,0:T(8,128)(2,1)S(1)}, u32[]{:S(2)}, u32[]{:S(2)}) collective-permute-start(bf16[128,768]{1,0:T(8,128)(2,1)S(1)} %get-tuple-element.93), channel_id=1, source_target_pairs={{0,8},{8,24},{24,16},{16,0},{1,9},{9,25},{25,17},{17,1},{2,10},{10... | collective-permute-start | bytes 589832 | tf_op jit(solution)/shard_map/ppermute | solution.py:258
  100.0 10.6 %collective-permute-start.23 = (bf16[128,768]{1,0:T(8,128)(2,1)S(1)}, bf16[128,768]{1,0:T(8,128)(2,1)S(1)}, u32[]{:S(2)}, u32[]{:S(2)}) collective-permute-start(bf16[128,768]{1,0:T(8,128)(2,1)S(1)} %get-tuple-element.94), channel_id=1, source_target_pairs={{0,16},{8,0},{24,8},{16,24},{1,17},{9,1},{25,9},{17,25},{2,18},{10... | collective-permute-start | bytes 589832 | tf_op jit(solution)/shard_map/ppermute | solution.py:258

commit v4 on v3

--- a/solution.py
+++ b/solution.py
@@ -8,10 +8,10 @@
 from jax.sharding import PartitionSpec as P
 
 UNITS = 24
-SENDS = ((8,), (6, 7), (3,))
+SENDS = ((8,), (6, 6), (4,))
 SHIFT = (0, 16, 0, 0)
 LANES = 128
-VMEM_LIMIT = 20 * 1024 * 1024
+VMEM_LIMIT = 16 * 1024 * 1024
 
 
 def cost(weight):
@@ -279,11 +279,14 @@
     token[...] = jnp.zeros_like(token)
     rows, width = out.shape
     step = pl.program_id(0)
+    stacked = jnp.concatenate([piece[...] for piece in pieces], axis=0)
+    last = pl.ds(weights.shape[1] - stacked.shape[0], stacked.shape[0])
     if rows < near.shape[0]:
-        here = near[pl.ds(pl.multiple_of(step * rows, rows), rows), :]
+        down, across = pl.ds(pl.multiple_of(step * rows, rows), rows), slice(None)
     else:
-        here = near[:, pl.ds(pl.multiple_of(step * width, width), width)]
-    out[...] = (here + stacked_dot(weights[...], pieces)).astype(out.dtype)
+        down, across = slice(None), pl.ds(pl.multiple_of(step * width, width), width)
+    added = jnp.dot(weights[down, last], stacked, preferred_element_type=jnp.float32)
+    out[...] = (near[down, across] + added).astype(out.dtype)
 
 
 def piece_specs(pieces, unit):
@@ -310,22 +313,18 @@
 
 def band_chunk(band, near, weights, pieces, begin, columns, unit, after):
     rows, width = near.shape
-    slab = sum(piece.shape[0] for piece in pieces)
-    last = weights.shape[1] // slab - 1
     kernel, operands, specs, aliases = far_kernel, [], [], {}
     if band is not None:
         kernel, operands, aliases = far_kernel_onto, [band], {0: 0}
         specs = [pl.BlockSpec(memory_space=pl.ANY)]
-    specs.append(pl.BlockSpec(memory_space=pltpu.VMEM))
+    specs += [pl.BlockSpec(memory_space=pltpu.VMEM)] * 2
     if begin % width == 0:
         steps, place = 2, begin // width
-        specs.append(pl.BlockSpec((rows // steps, slab), lambda i: (i, last)))
-        specs += [whole_spec(piece.shape) for piece in pieces]
+        specs += [pl.BlockSpec(memory_space=pltpu.VMEM)] * len(pieces)
         out_spec = pl.BlockSpec((rows // steps, width), lambda i: (i, place))
     else:
         block = block_width(begin, width, unit)
         steps, place = width // block, begin // block
-        specs.append(pl.BlockSpec((rows, slab), lambda i: (0, last)))
         specs += piece_specs([(piece, 0) for piece in pieces], block)
         out_spec = pl.BlockSpec((rows, block), lambda i: (0, place + i))
     return pl.pallas_call(

time: 112 us -> 112 us (level)
  Pallas kernels: 29.6 us -> 27.8 us
  waiting for transfers between devices: 48.1 us -> 49.6 us
    pallas_call x4, Pallas kernels: 15.3 us -> 14.1 us  [near_chunk(): pl.pallas_call(near_kernel, grid=(width // unit,), in_specs=[pl.BlockSpec...]
    unnamed x20 -> x14, local copies, waits for them, and re-layouts: 4.29 us -> 4.27 us
  transfers between devices with their start and end apart: 24 -> 24, of which waited for: 14 -> 13; matrix products, arithmetic and copies ran while one was open for 0% -> 0% of each run, Pallas kernels for 25% -> 23%
where the time goes in v4:
time: 112 us
  waiting for transfers between devices  49.6 us (44%)
  starting transfers between devices  28.6 us (26%)
  Pallas kernels  27.8 us (25%)
  local copies, waits for them, and re-layouts  5.57 us (5%)
    pallas_call x4, Pallas kernels, near_chunk(): pl.pallas_call(near_kernel, grid=(width // unit,), in_specs=[pl.BlockSpec...  14.1 us
    ppermute x1, waiting for transfers between devices, shards(): moved = lax.ppermute(held, 'tile', swap(tiles, members))  12.1 us
    pallas_call x4, Pallas kernels, band_chunk(): pl.pallas_call(kernel, grid=(steps,), in_specs=specs + [token_spec()], ou...  10.4 us
    ppermute x1, waiting for transfers between devices, shards(): moved = lax.ppermute(held, 'tile', swap(tiles, bit * members))  9.31 us
    ppermute x8, starting transfers between devices, send_far(): lax.ppermute(cut, 'blk', ring_shift(blks, by))  8.25 us
    ppermute x8, waiting for transfers between devices, send_far(): lax.ppermute(cut, 'blk', ring_shift(blks, by))  8.05 us
    ppermute x3, waiting for transfers between devices, send_slab(): behind.append(lax.ppermute(behind[-1] if behind else piece, 'blk', back))  6.36 us
    ppermute x3, waiting for transfers between devices, shards(): lax.ppermute(blocks[distance], 'tile', swap(tiles, distance * members))  6.06 us
  transfers between devices with their start and end apart: 24, of which 13 were waited for; matrix products, arithmetic and copies ran while one was open for 0% of the time, Pallas kernels for 23%

profile of v4, /device:TPU:0, one launch (start us, length us, event | category | flops | bytes accessed | tf_op | source)
XLA Modules:
  0.0 111.8 jit_solution(8476645529150058808)
XLA Ops:
  0.0 1.3 %slice.3.refs_6_ = bf16[256,2048]{1,0:T(8,128)(2,1)S(1)} slice(bf16[256,6144]{1,0:T(8,128)(2,1)} %refs_1_.9), slice={[0:256], [0:2048]} | slice | bytes 2097152 | tf_op jit(solution)/shard_map/slice | solution.py:350
  1.3 3.0 %collective-permute-start.7 = (bf16[256,2048]{1,0:T(8,128)(2,1)S(1)}, bf16[256,2048]{1,0:T(8,128)(2,1)S(1)}, u32[]{:S(2)}, u32[]{:S(2)}) collective-permute-start(bf16[256,2048]{1,0:T(8,128)(2,1)S(1)} %slice.3.refs_6_), channel_id=1, source_target_pairs={{0,16},{8,0},{24,8},{16,24},{1,17},{9,1},{25,9},{17,25},{2,18},{10... | collective-permute-start | bytes 3145736 | tf_op jit(solution)/shard_map/ppermute | solution.py:221
  4.4 0.9 copy-done.1
  5.3 0.7 copy-done.2
  6.0 0.7 copy-done.3
  6.7 0.7 copy-done.4
  7.3 0.7 copy-done.5
  8.0 0.7 copy-done.6
  8.6 1.6 %shard_map.73 = (bf16[64,512]{1,0:T(8,128)(2,1)S(1)}, bf16[64,512]{1,0:T(8,128)(2,1)S(1)}, bf16[64,512]{1,0:T(8,128)(2,1)S(1)}, bf16[64,512]{1,0:T(8,128)(2,1)S(1)}) custom-call(s32[8]{0:T(128)S(1)} %copy-done.4, s32[8]{0:T(128)S(1)} %copy-done.5, s32[8]{0:T(128)S(1)} %copy-done.6, bf16[256,512]{1,0:T(8,128)(2,1)S(1)} %copy-done.1, f32[1,256]{1,0:T(1,128)S(1)} %bitcast.9, ...), custom_call_target="tpu_custom_call" | custom-call | flops 99999997952 | tf_op jit(solution)/shard_map/pallas_call | solution.py:101
  10.2 2.1 %collective-permute-start = (bf16[64,512]{1,0:T(8,128)(2,1)S(1)}, bf16[64,512]{1,0:T(8,128)(2,1)S(1)}, u32[]{:S(2)}, u32[]{:S(2)}) collective-permute-start(bf16[64,512]{1,0:T(8,128)(2,1)S(1)} %get-tuple-element.52), channel_id=1, source_target_pairs={{0,2},{1,3},{2,0},{3,1},{4,6},{5,7},{6,4},{7,5},{8,10},{9,11},{10,... | collective-permute-start | bytes 196616 | tf_op jit(solution)/shard_map/ppermute | solution.py:356
  12.3 2.6 %collective-permute-start.1 = (bf16[64,512]{1,0:T(8,128)(2,1)S(1)}, bf16[64,512]{1,0:T(8,128)(2,1)S(1)}, u32[]{:S(2)}, u32[]{:S(2)}) collective-permute-start(bf16[64,512]{1,0:T(8,128)(2,1)S(1)} %get-tuple-element.53), channel_id=1, source_target_pairs={{0,4},{1,5},{2,6},{3,7},{4,0},{5,1},{6,2},{7,3},{8,12},{9,13},{10,... | collective-permute-start | bytes 196616 | tf_op jit(solution)/shard_map/ppermute | solution.py:356
  14.9 4.1 %collective-permute-done.1.refs_2_ = bf16[64,512]{1,0:T(8,128)(2,1)S(1)} collective-permute-done((bf16[64,512]{1,0:T(8,128)(2,1)S(1)}, bf16[64,512]{1,0:T(8,128)(2,1)S(1)}, u32[]{:S(2)}, u32[]{:S(2)}) %collective-permute-start.1) | collective-permute-done | bytes 65568 | tf_op jit(solution)/shard_map/ppermute | solution.py:356
  19.0 2.0 %collective-permute-done.2.refs_3_ = bf16[64,512]{1,0:T(8,128)(2,1)S(1)} collective-permute-done((bf16[64,512]{1,0:T(8,128)(2,1)S(1)}, bf16[64,512]{1,0:T(8,128)(2,1)S(1)}, u32[]{:S(2)}, u32[]{:S(2)}) %collective-permute-start.2) | collective-permute-done | bytes 65568 | tf_op jit(solution)/shard_map/ppermute | solution.py:356
  21.0 1.5 %collective-permute-start.3 = (bf16[64,512]{1,0:T(8,128)(2,1)S(1)}, bf16[64,512]{1,0:T(8,128)(2,1)S(1)}, u32[]{:S(2)}, u32[]{:S(2)}) collective-permute-start(bf16[64,512]{1,0:T(8,128)(2,1)S(1)} %get-tuple-element.56), channel_id=1, source_target_pairs={{0,8},{8,24},{24,16},{16,0},{1,9},{9,25},{25,17},{17,1},{2,10},{10... | collective-permute-start | bytes 196616 | tf_op jit(solution)/shard_map/ppermute | solution.py:359
  22.6 1.5 %collective-permute-start.4 = (bf16[64,512]{1,0:T(8,128)(2,1)S(1)}, bf16[64,512]{1,0:T(8,128)(2,1)S(1)}, u32[]{:S(2)}, u32[]{:S(2)}) collective-permute-start(bf16[64,512]{1,0:T(8,128)(2,1)S(1)} %get-tuple-element.57), channel_id=1, source_target_pairs={{0,24},{8,16},{24,0},{16,8},{1,25},{9,17},{25,1},{17,9},{2,26},{10... | collective-permute-start | bytes 196616 | tf_op jit(solution)/shard_map/ppermute | solution.py:359
  24.1 1.5 %collective-permute-start.5 = (bf16[64,512]{1,0:T(8,128)(2,1)S(1)}, bf16[64,512]{1,0:T(8,128)(2,1)S(1)}, u32[]{:S(2)}, u32[]{:S(2)}) collective-permute-start(bf16[64,512]{1,0:T(8,128)(2,1)S(1)} %get-tuple-element.58), channel_id=1, source_target_pairs={{0,16},{8,0},{24,8},{16,24},{1,17},{9,1},{25,9},{17,25},{2,18},{10... | collective-permute-start | bytes 196616 | tf_op jit(solution)/shard_map/ppermute | solution.py:359
  25.5 0.4 shard_map.75
  26.0 3.0 %collective-permute-done.7.behind.refs_3_ = bf16[256,2048]{1,0:T(8,128)(2,1)S(1)} collective-permute-done((bf16[256,2048]{1,0:T(8,128)(2,1)S(1)}, bf16[256,2048]{1,0:T(8,128)(2,1)S(1)}, u32[]{:S(2)}, u32[]{:S(2)}) %collective-permute-start.7) | collective-permute-done | bytes 1048608 | tf_op jit(solution)/shard_map/ppermute | solution.py:221
  29.0 2.6 %collective-permute-start.15 = (bf16[256,3072]{1,0:T(8,128)(2,1)S(1)}, bf16[256,3072]{1,0:T(8,128)(2,1)S(1)}, u32[]{:S(2)}, u32[]{:S(2)}) collective-permute-start(bf16[256,3072]{1,0:T(8,128)(2,1)S(1)} %get-tuple-element.71), channel_id=1, source_target_pairs={{0,16},{8,0},{24,8},{16,24},{1,17},{9,1},{25,9},{17,25},{2,18},{10... | collective-permute-start | bytes 4718600 | tf_op jit(solution)/shard_map/ppermute | solution.py:221
  31.7 2.1 %collective-permute-done.4.refs_2_ = bf16[64,512]{1,0:T(8,128)(2,1)S(1)} collective-permute-done((bf16[64,512]{1,0:T(8,128)(2,1)S(1)}, bf16[64,512]{1,0:T(8,128)(2,1)S(1)}, u32[]{:S(2)}, u32[]{:S(2)}) %collective-permute-start.4) | collective-permute-done | bytes 65568 | tf_op jit(solution)/shard_map/ppermute | solution.py:359
  33.9 2.7 %collective-permute-start.8 = (bf16[1,4,64,512]{3,2,1,0:T(8,128)(2,1)S(1)}, bf16[1,4,64,512]{3,2,1,0:T(8,128)(2,1)S(1)}, u32[]{:S(2)}, u32[]{:S(2)}) collective-permute-start(bf16[1,4,64,512]{3,2,1,0:T(8,128)(2,1)S(1)} %bitcast.7), channel_id=1, source_target_pairs={{0,4},{1,5},{2,6},{3,7},{4,0},{5,1},{6,2},{7,3},{8,12},{9,13},{10,... | collective-permute-start | bytes 786440 | tf_op jit(solution)/shard_map/ppermute | solution.py:393
  36.5 9.3 %collective-permute-done.8.refs_1_ = bf16[1,4,64,512]{3,2,1,0:T(8,128)(2,1)S(1)} collective-permute-done((bf16[1,4,64,512]{3,2,1,0:T(8,128)(2,1)S(1)}, bf16[1,4,64,512]{3,2,1,0:T(8,128)(2,1)S(1)}, u32[]{:S(2)}, u32[]{:S(2)}) %collective-permute-start.8) | collective-permute-done | bytes 262176 | tf_op jit(solution)/shard_map/ppermute | solution.py:393
  45.9 0.7 collective-permute-start.9
  46.6 12.1 %collective-permute-done.9.refs_1_ = bf16[2,4,64,512]{3,2,1,0:T(8,128)(2,1)S(1)} collective-permute-done((bf16[2,4,64,512]{3,2,1,0:T(8,128)(2,1)S(1)}, bf16[2,4,64,512]{3,2,1,0:T(8,128)(2,1)S(1)}, u32[]{:S(2)}, u32[]{:S(2)}) %collective-permute-start.9) | collective-permute-done | bytes 524320 | tf_op jit(solution)/shard_map/ppermute | solution.py:398
  58.7 2.0 %collective-permute-start.13 = (bf16[128,2048]{1,0:T(8,128)(2,1)S(1)}, bf16[128,2048]{1,0:T(8,128)(2,1)S(1)}, u32[]{:S(2)}, u32[]{:S(2)}) collective-permute-start(bf16[128,2048]{1,0:T(8,128)(2,1)S(1)} %get-tuple-element.70), channel_id=1, source_target_pairs={{0,16},{8,0},{24,8},{16,24},{1,17},{9,1},{25,9},{17,25},{2,18},{10... | collective-permute-start | bytes 1572872 | tf_op jit(solution)/shard_map/ppermute | solution.py:258
  60.8 0.8 shard_map.79
  61.6 4.7 %shard_map.80 = (f32[1024,2048]{1,0:T(8,128)S(1)}, bf16[16,128]{1,0:T(8,128)(2,1)S(1)}) custom-call(bf16[1024,1024]{1,0:T(8,128)(2,1)S(1)} %get-tuple-element.66.refs_0_.weights.refs_1_, bf16[256,6144]{1,0:T(8,128)(2,1)S(1)} %copy-done, bf16[256,2048]{1,0:T(8,128)(2,1)S(1)} %collective-permute-done.6.ahead.refs_2_, ...), custom_call_target="tpu_custom_call" | custom-call | flops 1000000 | tf_op jit(solution)/shard_map/pallas_call | solution.py:301
  66.3 2.7 %collective-permute-done.14.refs_1_.refs_2_.ahead = bf16[256,3072]{1,0:T(8,128)(2,1)S(1)} collective-permute-done((bf16[256,3072]{1,0:T(8,128)(2,1)S(1)}, bf16[256,3072]{1,0:T(8,128)(2,1)S(1)}, u32[]{:S(2)}, u32[]{:S(2)}) %collective-permute-start.14) | collective-permute-done | bytes 1572896 | tf_op jit(solution)/shard_map/ppermute | solution.py:220
  69.1 0.3 collective-permute-start.19
  69.4 1.8 %collective-permute-start.18 = (bf16[256,1024]{1,0:T(8,128)(2,1)S(1)}, bf16[256,1024]{1,0:T(8,128)(2,1)S(1)}, u32[]{:S(2)}, u32[]{:S(2)}) collective-permute-start(bf16[256,1024]{1,0:T(8,128)(2,1)S(1)} %get-tuple-element.81), channel_id=1, source_target_pairs={{0,8},{8,24},{24,16},{16,0},{1,9},{9,25},{25,17},{17,1},{2,10},{10... | collective-permute-start | bytes 1572872 | tf_op jit(solution)/shard_map/ppermute | solution.py:220
  71.2 3.5 %shard_map.82 = (f32[1024,1536]{1,0:T(8,128)S(1)}, bf16[16,128]{1,0:T(8,128)(2,1)S(1)}) custom-call(bf16[1024,1024]{1,0:T(8,128)(2,1)S(1)} %get-tuple-element.66.refs_0_.weights.refs_1_, bf16[256,6144]{1,0:T(8,128)(2,1)S(1)} %copy-done, bf16[256,3072]{1,0:T(8,128)(2,1)S(1)} %collective-permute-done.14.refs_1_.refs_2_.ahead, ...), custom_call_target="tpu_custom_call" | custom-call | flops 1000000 | tf_op jit(solution)/shard_map/pallas_call | solution.py:301
  74.8 3.5 %shard_map.83 = (f32[1024,1536]{1,0:T(8,128)S(1)}, bf16[16,128]{1,0:T(8,128)(2,1)S(1)}) custom-call(bf16[1024,1024]{1,0:T(8,128)(2,1)S(1)} %get-tuple-element.66.refs_0_.weights.refs_1_, bf16[256,6144]{1,0:T(8,128)(2,1)S(1)} %copy-done, bf16[256,3072]{1,0:T(8,128)(2,1)S(1)} %collective-permute-done.14.refs_1_.refs_2_.ahead, ...), custom_call_target="tpu_custom_call" | custom-call | flops 1000000 | tf_op jit(solution)/shard_map/pallas_call | solution.py:301
  78.3 1.9 %collective-permute-done.12.refs_1_.refs_0_ = bf16[128,2048]{1,0:T(8,128)(2,1)S(1)} collective-permute-done((bf16[128,2048]{1,0:T(8,128)(2,1)S(1)}, bf16[128,2048]{1,0:T(8,128)(2,1)S(1)}, u32[]{:S(2)}, u32[]{:S(2)}) %collective-permute-start.12) | collective-permute-done | bytes 524320 | tf_op jit(solution)/shard_map/ppermute | solution.py:258
  80.3 0.3 collective-permute-start.17
  80.5 1.8 %collective-permute-start.16 = (bf16[112,1536]{1,0:T(8,128)(2,1)S(1)}, bf16[112,1536]{1,0:T(8,128)(2,1)S(1)}, u32[]{:S(2)}, u32[]{:S(2)}) collective-permute-start(bf16[112,1536]{1,0:T(8,128)(2,1)S(1)} %get-tuple-element.79), channel_id=1, source_target_pairs={{0,8},{8,24},{24,16},{16,0},{1,9},{9,25},{25,17},{17,1},{2,10},{10... | collective-permute-start | bytes 1032200 | tf_op jit(solution)/shard_map/ppermute | solution.py:258
  82.3 2.8 %shard_map.85 = (bf16[1024,6144]{1,0:T(8,128)(2,1)}, bf16[16,128]{1,0:T(8,128)(2,1)S(1)}) custom-call(f32[1024,2048]{1,0:T(8,128)S(1)} %get-tuple-element.68.near, bf16[1024,1024]{1,0:T(8,128)(2,1)S(1)} %get-tuple-element.66.refs_0_.weights.refs_1_, bf16[128,2048]{1,0:T(8,128)(2,1)S(1)} %collective-permute-done.12.refs_1_.refs_0_, ...), custom_call_target="tpu_custom_call" | custom-call | flops 1000000 | tf_op jit(solution)/shard_map/pallas_call | solution.py:330
  85.1 3.4 %collective-permute-done.19.refs_2_.refs_3_.behind = bf16[256,1024]{1,0:T(8,128)(2,1)S(1)} collective-permute-done((bf16[256,1024]{1,0:T(8,128)(2,1)S(1)}, bf16[256,1024]{1,0:T(8,128)(2,1)S(1)}, u32[]{:S(2)}, u32[]{:S(2)}) %collective-permute-start.19) | collective-permute-done | bytes 524320 | tf_op jit(solution)/shard_map/ppermute | solution.py:221
  88.5 2.9 %collective-permute-done.18.refs_1_.refs_2_.ahead = bf16[256,1024]{1,0:T(8,128)(2,1)S(1)} collective-permute-done((bf16[256,1024]{1,0:T(8,128)(2,1)S(1)}, bf16[256,1024]{1,0:T(8,128)(2,1)S(1)}, u32[]{:S(2)}, u32[]{:S(2)}) %collective-permute-start.18) | collective-permute-done | bytes 524320 | tf_op jit(solution)/shard_map/ppermute | solution.py:220
  91.5 2.0 %collective-permute-start.21 = (bf16[128,1536]{1,0:T(8,128)(2,1)S(1)}, bf16[128,1536]{1,0:T(8,128)(2,1)S(1)}, u32[]{:S(2)}, u32[]{:S(2)}) collective-permute-start(bf16[128,1536]{1,0:T(8,128)(2,1)S(1)} %get-tuple-element.89), channel_id=1, source_target_pairs={{0,16},{8,0},{24,8},{16,24},{1,17},{9,1},{25,9},{17,25},{2,18},{10... | collective-permute-start | bytes 1179656 | tf_op jit(solution)/shard_map/ppermute | solution.py:258
  93.6 2.4 %shard_map.87 = (f32[1024,1024]{1,0:T(8,128)S(1)}, bf16[16,128]{1,0:T(8,128)(2,1)S(1)}) custom-call(bf16[1024,1024]{1,0:T(8,128)(2,1)S(1)} %get-tuple-element.66.refs_0_.weights.refs_1_, bf16[256,6144]{1,0:T(8,128)(2,1)S(1)} %copy-done, bf16[256,1024]{1,0:T(8,128)(2,1)S(1)} %collective-permute-done.18.refs_1_.refs_2_.ahead, ...), custom_call_target="tpu_custom_call" | custom-call | flops 1000000 | tf_op jit(solution)/shard_map/pallas_call | solution.py:301
  95.9 2.9 %collective-permute-done.16.refs_1_.refs_2_ = bf16[112,1536]{1,0:T(8,128)(2,1)S(1)} collective-permute-done((bf16[112,1536]{1,0:T(8,128)(2,1)S(1)}, bf16[112,1536]{1,0:T(8,128)(2,1)S(1)}, u32[]{:S(2)}, u32[]{:S(2)}) %collective-permute-start.16) | collective-permute-done | bytes 344096 | tf_op jit(solution)/shard_map/ppermute | solution.py:258
  98.8 1.1 %collective-permute-start.22 = (bf16[128,1024]{1,0:T(8,128)(2,1)S(1)}, bf16[128,1024]{1,0:T(8,128)(2,1)S(1)}, u32[]{:S(2)}, u32[]{:S(2)}) collective-permute-start(bf16[128,1024]{1,0:T(8,128)(2,1)S(1)} %get-tuple-element.93), channel_id=1, source_target_pairs={{0,8},{8,24},{24,16},{16,0},{1,9},{9,25},{25,17},{17,1},{2,10},{10... | collective-permute-start | bytes 786440 | tf_op jit(solution)/shard_map/ppermute | solution.py:258
  100.0 1.0 collective-permute-start.23
  100.9 2.9 %shard_map.89 = (bf16[1024,6144]{1,0:T(8,128)(2,1)}, bf16[16,128]{1,0:T(8,128)(2,1)S(1)}) custom-call(bf16[1024,6144]{1,0:T(8,128)(2,1)} %get-tuple-element.77._, f32[1024,1536]{1,0:T(8,128)S(1)} %get-tuple-element.78.refs_0_, bf16[1024,1024]{1,0:T(8,128)(2,1)S(1)} %get-tuple-element.66.refs_0_.weights.refs_1_, ...), custom_call_target="tpu_custom_call", output_to_operand_aliasing={{0}: (0, {})} | custom-call | flops 1000000 | tf_op jit(solution)/shard_map/pallas_call | solution.py:330
  103.8 2.7 %collective-permute-done.20.refs_2_ = bf16[128,1536]{1,0:T(8,128)(2,1)S(1)} collective-permute-done((bf16[128,1536]{1,0:T(8,128)(2,1)S(1)}, bf16[128,1536]{1,0:T(8,128)(2,1)S(1)}, u32[]{:S(2)}, u32[]{:S(2)}) %collective-permute-start.20) | collective-permute-done | bytes 393248 | tf_op jit(solution)/shard_map/ppermute | solution.py:258
  106.5 2.9 %shard_map.90 = (bf16[1024,6144]{1,0:T(8,128)(2,1)}, bf16[16,128]{1,0:T(8,128)(2,1)S(1)}) custom-call(bf16[1024,6144]{1,0:T(8,128)(2,1)} %get-tuple-element.86._, f32[1024,1536]{1,0:T(8,128)S(1)} %get-tuple-element.87.refs_0_, bf16[1024,1024]{1,0:T(8,128)(2,1)S(1)} %get-tuple-element.66.refs_0_.weights.refs_1_, ...), custom_call_target="tpu_custom_call", output_to_operand_aliasing={{0}: (0, {})} | custom-call | flops 1000000 | tf_op jit(solution)/shard_map/pallas_call | solution.py:330
  109.4 0.6 collective-permute-done.23.refs_3_
  110.0 1.9 %shard_map.91 = (bf16[1024,6144]{1,0:T(8,128)(2,1)}, bf16[16,128]{1,0:T(8,128)(2,1)}) custom-call(bf16[1024,6144]{1,0:T(8,128)(2,1)} %get-tuple-element.91._, f32[1024,1024]{1,0:T(8,128)S(1)} %get-tuple-element.92.refs_0_, bf16[1024,1024]{1,0:T(8,128)(2,1)S(1)} %get-tuple-element.66.refs_0_.weights.refs_1_, ...), custom_call_target="tpu_custom_call", output_to_operand_aliasing={{0}: (0, {})} | custom-call | flops 1000000 | tf_op jit(solution)/shard_map/pallas_call | solution.py:330
  (34 shorter events, 0.6 us)
Async XLA Ops:
  1.3 27.7 %collective-permute-start.7 = (bf16[256,2048]{1,0:T(8,128)(2,1)S(1)}, bf16[256,2048]{1,0:T(8,128)(2,1)S(1)}, u32[]{:S(2)}, u32[]{:S(2)}) collective-permute-start(bf16[256,2048]{1,0:T(8,128)(2,1)S(1)} %slice.3.refs_6_), channel_id=1, source_target_pairs={{0,16},{8,0},{24,8},{16,24},{1,17},{9,1},{25,9},{17,25},{2,18},{10... | collective-permute-start | bytes 3145736 | tf_op jit(solution)/shard_map/ppermute | solution.py:221
  4.3 27.3 %collective-permute-start.6 = (bf16[256,2048]{1,0:T(8,128)(2,1)S(1)}, bf16[256,2048]{1,0:T(8,128)(2,1)S(1)}, u32[]{:S(2)}, u32[]{:S(2)}) collective-permute-start(bf16[256,2048]{1,0:T(8,128)(2,1)S(1)} %slice.3.refs_6_), channel_id=1, source_target_pairs={{0,8},{8,24},{24,16},{16,0},{1,9},{9,25},{25,17},{17,1},{2,10},{10... | collective-permute-start | bytes 3145736 | tf_op jit(solution)/shard_map/ppermute | solution.py:220
  4.4 0.9 copy-start.1
  5.3 0.7 copy-start.2
  6.0 0.7 copy-start.3
  6.7 0.7 copy-start.4
  7.3 0.7 copy-start.5
  8.0 0.7 copy-start.6
  8.6 16.9 %copy-start = (bf16[256,6144]{1,0:T(8,128)(2,1)S(1)}, bf16[256,6144]{1,0:T(8,128)(2,1)}, u32[]{:S(2)}) copy-start(bf16[256,6144]{1,0:T(8,128)(2,1)} %refs_1_.9) | copy-start | bytes 9437188
  10.2 4.7 %collective-permute-start = (bf16[64,512]{1,0:T(8,128)(2,1)S(1)}, bf16[64,512]{1,0:T(8,128)(2,1)S(1)}, u32[]{:S(2)}, u32[]{:S(2)}) collective-permute-start(bf16[64,512]{1,0:T(8,128)(2,1)S(1)} %get-tuple-element.52), channel_id=1, source_target_pairs={{0,2},{1,3},{2,0},{3,1},{4,6},{5,7},{6,4},{7,5},{8,10},{9,11},{10,... | collective-permute-start | bytes 196616 | tf_op jit(solution)/shard_map/ppermute | solution.py:356
  12.3 6.7 %collective-permute-start.1 = (bf16[64,512]{1,0:T(8,128)(2,1)S(1)}, bf16[64,512]{1,0:T(8,128)(2,1)S(1)}, u32[]{:S(2)}, u32[]{:S(2)}) collective-permute-start(bf16[64,512]{1,0:T(8,128)(2,1)S(1)} %get-tuple-element.53), channel_id=1, source_target_pairs={{0,4},{1,5},{2,6},{3,7},{4,0},{5,1},{6,2},{7,3},{8,12},{9,13},{10,... | collective-permute-start | bytes 196616 | tf_op jit(solution)/shard_map/ppermute | solution.py:356
  14.9 6.1 %collective-permute-start.2 = (bf16[64,512]{1,0:T(8,128)(2,1)S(1)}, bf16[64,512]{1,0:T(8,128)(2,1)S(1)}, u32[]{:S(2)}, u32[]{:S(2)}) collective-permute-start(bf16[64,512]{1,0:T(8,128)(2,1)S(1)} %get-tuple-element.54), channel_id=1, source_target_pairs={{0,6},{1,7},{2,4},{3,5},{4,2},{5,3},{6,0},{7,1},{8,14},{9,15},{10,... | collective-permute-start | bytes 196616 | tf_op jit(solution)/shard_map/ppermute | solution.py:356
  21.0 10.7 %collective-permute-start.3 = (bf16[64,512]{1,0:T(8,128)(2,1)S(1)}, bf16[64,512]{1,0:T(8,128)(2,1)S(1)}, u32[]{:S(2)}, u32[]{:S(2)}) collective-permute-start(bf16[64,512]{1,0:T(8,128)(2,1)S(1)} %get-tuple-element.56), channel_id=1, source_target_pairs={{0,8},{8,24},{24,16},{16,0},{1,9},{9,25},{25,17},{17,1},{2,10},{10... | collective-permute-start | bytes 196616 | tf_op jit(solution)/shard_map/ppermute | solution.py:359
  22.6 11.3 %collective-permute-start.4 = (bf16[64,512]{1,0:T(8,128)(2,1)S(1)}, bf16[64,512]{1,0:T(8,128)(2,1)S(1)}, u32[]{:S(2)}, u32[]{:S(2)}) collective-permute-start(bf16[64,512]{1,0:T(8,128)(2,1)S(1)} %get-tuple-element.57), channel_id=1, source_target_pairs={{0,24},{8,16},{24,0},{16,8},{1,25},{9,17},{25,1},{17,9},{2,26},{10... | collective-permute-start | bytes 196616 | tf_op jit(solution)/shard_map/ppermute | solution.py:359
  24.1 9.8 %collective-permute-start.5 = (bf16[64,512]{1,0:T(8,128)(2,1)S(1)}, bf16[64,512]{1,0:T(8,128)(2,1)S(1)}, u32[]{:S(2)}, u32[]{:S(2)}) collective-permute-start(bf16[64,512]{1,0:T(8,128)(2,1)S(1)} %get-tuple-element.58), channel_id=1, source_target_pairs={{0,16},{8,0},{24,8},{16,24},{1,17},{9,1},{25,9},{17,25},{2,18},{10... | collective-permute-start | bytes 196616 | tf_op jit(solution)/shard_map/ppermute | solution.py:359
  29.0 37.3 %collective-permute-start.15 = (bf16[256,3072]{1,0:T(8,128)(2,1)S(1)}, bf16[256,3072]{1,0:T(8,128)(2,1)S(1)}, u32[]{:S(2)}, u32[]{:S(2)}) collective-permute-start(bf16[256,3072]{1,0:T(8,128)(2,1)S(1)} %get-tuple-element.71), channel_id=1, source_target_pairs={{0,16},{8,0},{24,8},{16,24},{1,17},{9,1},{25,9},{17,25},{2,18},{10... | collective-permute-start | bytes 4718600 | tf_op jit(solution)/shard_map/ppermute | solution.py:221
  31.6 37.3 %collective-permute-start.14 = (bf16[256,3072]{1,0:T(8,128)(2,1)S(1)}, bf16[256,3072]{1,0:T(8,128)(2,1)S(1)}, u32[]{:S(2)}, u32[]{:S(2)}) collective-permute-start(bf16[256,3072]{1,0:T(8,128)(2,1)S(1)} %get-tuple-element.71), channel_id=1, source_target_pairs={{0,8},{8,24},{24,16},{16,0},{1,9},{9,25},{25,17},{17,1},{2,10},{10... | collective-permute-start | bytes 4718600 | tf_op jit(solution)/shard_map/ppermute | solution.py:220
  33.9 12.0 %collective-permute-start.8 = (bf16[1,4,64,512]{3,2,1,0:T(8,128)(2,1)S(1)}, bf16[1,4,64,512]{3,2,1,0:T(8,128)(2,1)S(1)}, u32[]{:S(2)}, u32[]{:S(2)}) collective-permute-start(bf16[1,4,64,512]{3,2,1,0:T(8,128)(2,1)S(1)} %bitcast.7), channel_id=1, source_target_pairs={{0,4},{1,5},{2,6},{3,7},{4,0},{5,1},{6,2},{7,3},{8,12},{9,13},{10,... | collective-permute-start | bytes 786440 | tf_op jit(solution)/shard_map/ppermute | solution.py:393
  45.9 12.8 %collective-permute-start.9 = (bf16[2,4,64,512]{3,2,1,0:T(8,128)(2,1)S(1)}, bf16[2,4,64,512]{3,2,1,0:T(8,128)(2,1)S(1)}, u32[]{:S(2)}, u32[]{:S(2)}) collective-permute-start(bf16[2,4,64,512]{3,2,1,0:T(8,128)(2,1)S(1)} %bitcast.4), channel_id=1, source_target_pairs={{0,2},{1,3},{2,0},{3,1},{4,6},{5,7},{6,4},{7,5},{8,10},{9,11},{10,... | collective-permute-start | bytes 1572872 | tf_op jit(solution)/shard_map/ppermute | solution.py:398
  46.6 12.1 %collective-permute-start.10 = (bf16[2,4,64,512]{3,2,1,0:T(8,128)(2,1)S(1)}, bf16[2,4,64,512]{3,2,1,0:T(8,128)(2,1)S(1)}, u32[]{:S(2)}, u32[]{:S(2)}) collective-permute-start(bf16[2,4,64,512]{3,2,1,0:T(8,128)(2,1)S(1)} %bitcast.5), channel_id=1, source_target_pairs={{0,1},{1,0},{2,3},{3,2},{4,5},{5,4},{6,7},{7,6},{8,9},{9,8},{10,11... | collective-permute-start | bytes 1572872 | tf_op jit(solution)/shard_map/ppermute | solution.py:403
  58.7 2.0 %collective-permute-start.11 = (bf16[2,4,64,512]{3,2,1,0:T(8,128)(2,1)S(1)}, bf16[2,4,64,512]{3,2,1,0:T(8,128)(2,1)S(1)}, u32[]{:S(2)}, u32[]{:S(2)}) collective-permute-start(bf16[2,4,64,512]{3,2,1,0:T(8,128)(2,1)S(1)} %collective-permute-done.9.refs_1_), channel_id=1, source_target_pairs={{0,1},{1,0},{2,3},{3,2},{4,5},{5,4},{6,7},{7,6},{8,9},{9,8},{10,11... | collective-permute-start | bytes 1572872 | tf_op jit(solution)/shard_map/ppermute | solution.py:403
  58.7 21.5 %collective-permute-start.12 = (bf16[128,2048]{1,0:T(8,128)(2,1)S(1)}, bf16[128,2048]{1,0:T(8,128)(2,1)S(1)}, u32[]{:S(2)}, u32[]{:S(2)}) collective-permute-start(bf16[128,2048]{1,0:T(8,128)(2,1)S(1)} %get-tuple-element.69), channel_id=1, source_target_pairs={{0,8},{8,24},{24,16},{16,0},{1,9},{9,25},{25,17},{17,1},{2,10},{10... | collective-permute-start | bytes 1572872 | tf_op jit(solution)/shard_map/ppermute | solution.py:258
  58.7 21.5 %collective-permute-start.13 = (bf16[128,2048]{1,0:T(8,128)(2,1)S(1)}, bf16[128,2048]{1,0:T(8,128)(2,1)S(1)}, u32[]{:S(2)}, u32[]{:S(2)}) collective-permute-start(bf16[128,2048]{1,0:T(8,128)(2,1)S(1)} %get-tuple-element.70), channel_id=1, source_target_pairs={{0,16},{8,0},{24,8},{16,24},{1,17},{9,1},{25,9},{17,25},{2,18},{10... | collective-permute-start | bytes 1572872 | tf_op jit(solution)/shard_map/ppermute | solution.py:258
  69.1 19.4 %collective-permute-start.19 = (bf16[256,1024]{1,0:T(8,128)(2,1)S(1)}, bf16[256,1024]{1,0:T(8,128)(2,1)S(1)}, u32[]{:S(2)}, u32[]{:S(2)}) collective-permute-start(bf16[256,1024]{1,0:T(8,128)(2,1)S(1)} %get-tuple-element.81), channel_id=1, source_target_pairs={{0,16},{8,0},{24,8},{16,24},{1,17},{9,1},{25,9},{17,25},{2,18},{10... | collective-permute-start | bytes 1572872 | tf_op jit(solution)/shard_map/ppermute | solution.py:221
  69.4 22.0 %collective-permute-start.18 = (bf16[256,1024]{1,0:T(8,128)(2,1)S(1)}, bf16[256,1024]{1,0:T(8,128)(2,1)S(1)}, u32[]{:S(2)}, u32[]{:S(2)}) collective-permute-start(bf16[256,1024]{1,0:T(8,128)(2,1)S(1)} %get-tuple-element.81), channel_id=1, source_target_pairs={{0,8},{8,24},{24,16},{16,0},{1,9},{9,25},{25,17},{17,1},{2,10},{10... | collective-permute-start | bytes 1572872 | tf_op jit(solution)/shard_map/ppermute | solution.py:220
  80.3 18.5 %collective-permute-start.17 = (bf16[144,1536]{1,0:T(8,128)(2,1)S(1)}, bf16[144,1536]{1,0:T(8,128)(2,1)S(1)}, u32[]{:S(2)}, u32[]{:S(2)}) collective-permute-start(bf16[144,1536]{1,0:T(8,128)(2,1)S(1)} %get-tuple-element.80), channel_id=1, source_target_pairs={{0,16},{8,0},{24,8},{16,24},{1,17},{9,1},{25,9},{17,25},{2,18},{10... | collective-permute-start | bytes 1327112 | tf_op jit(solution)/shard_map/ppermute | solution.py:258
  80.5 18.3 %collective-permute-start.16 = (bf16[112,1536]{1,0:T(8,128)(2,1)S(1)}, bf16[112,1536]{1,0:T(8,128)(2,1)S(1)}, u32[]{:S(2)}, u32[]{:S(2)}) collective-permute-start(bf16[112,1536]{1,0:T(8,128)(2,1)S(1)} %get-tuple-element.79), channel_id=1, source_target_pairs={{0,8},{8,24},{24,16},{16,0},{1,9},{9,25},{25,17},{17,1},{2,10},{10... | collective-permute-start | bytes 1032200 | tf_op jit(solution)/shard_map/ppermute | solution.py:258
  91.5 15.0 %collective-permute-start.20 = (bf16[128,1536]{1,0:T(8,128)(2,1)S(1)}, bf16[128,1536]{1,0:T(8,128)(2,1)S(1)}, u32[]{:S(2)}, u32[]{:S(2)}) collective-permute-start(bf16[128,1536]{1,0:T(8,128)(2,1)S(1)} %get-tuple-element.88), channel_id=1, source_target_pairs={{0,8},{8,24},{24,16},{16,0},{1,9},{9,25},{25,17},{17,1},{2,10},{10... | collective-permute-start | bytes 1179656 | tf_op jit(solution)/shard_map/ppermute | solution.py:258
  91.5 15.0 %collective-permute-start.21 = (bf16[128,1536]{1,0:T(8,128)(2,1)S(1)}, bf16[128,1536]{1,0:T(8,128)(2,1)S(1)}, u32[]{:S(2)}, u32[]{:S(2)}) collective-permute-start(bf16[128,1536]{1,0:T(8,128)(2,1)S(1)} %get-tuple-element.89), channel_id=1, source_target_pairs={{0,16},{8,0},{24,8},{16,24},{1,17},{9,1},{25,9},{17,25},{2,18},{10... | collective-permute-start | bytes 1179656 | tf_op jit(solution)/shard_map/ppermute | solution.py:258
  98.8 10.6 %collective-permute-start.22 = (bf16[128,1024]{1,0:T(8,128)(2,1)S(1)}, bf16[128,1024]{1,0:T(8,128)(2,1)S(1)}, u32[]{:S(2)}, u32[]{:S(2)}) collective-permute-start(bf16[128,1024]{1,0:T(8,128)(2,1)S(1)} %get-tuple-element.93), channel_id=1, source_target_pairs={{0,8},{8,24},{24,16},{16,0},{1,9},{9,25},{25,17},{17,1},{2,10},{10... | collective-permute-start | bytes 786440 | tf_op jit(solution)/shard_map/ppermute | solution.py:258
  100.0 10.0 %collective-permute-start.23 = (bf16[128,1024]{1,0:T(8,128)(2,1)S(1)}, bf16[128,1024]{1,0:T(8,128)(2,1)S(1)}, u32[]{:S(2)}, u32[]{:S(2)}) collective-permute-start(bf16[128,1024]{1,0:T(8,128)(2,1)S(1)} %get-tuple-element.94), channel_id=1, source_target_pairs={{0,16},{8,0},{24,8},{16,24},{1,17},{9,1},{25,9},{17,25},{2,18},{10... | collective-permute-start | bytes 786440 | tf_op jit(solution)/shard_map/ppermute | solution.py:258

commit v5 on v4

--- a/solution.py
+++ b/solution.py
@@ -277,16 +277,12 @@
 def far_kernel(near, weights, *refs):
     pieces, (_, out, token) = refs[:-3], refs[-3:]
     token[...] = jnp.zeros_like(token)
-    rows, width = out.shape
-    step = pl.program_id(0)
+    rows = out.shape[0]
     stacked = jnp.concatenate([piece[...] for piece in pieces], axis=0)
     last = pl.ds(weights.shape[1] - stacked.shape[0], stacked.shape[0])
-    if rows < near.shape[0]:
-        down, across = pl.ds(pl.multiple_of(step * rows, rows), rows), slice(None)
-    else:
-        down, across = slice(None), pl.ds(pl.multiple_of(step * width, width), width)
-    added = jnp.dot(weights[down, last], stacked, preferred_element_type=jnp.float32)
-    out[...] = (near[down, across] + added).astype(out.dtype)
+    here = pl.ds(pl.multiple_of(pl.program_id(0) * rows, rows), rows)
+    added = jnp.dot(weights[here, last], stacked, preferred_element_type=jnp.float32)
+    out[...] = (near[here, :] + added).astype(out.dtype)
 
 
 def piece_specs(pieces, unit):
@@ -311,22 +307,18 @@
     )(weights, *[array for array, _ in pieces], after)
 
 
-def band_chunk(band, near, weights, pieces, begin, columns, unit, after):
+def band_chunk(band, near, weights, pieces, begin, columns, after):
     rows, width = near.shape
     kernel, operands, specs, aliases = far_kernel, [], [], {}
     if band is not None:
         kernel, operands, aliases = far_kernel_onto, [band], {0: 0}
         specs = [pl.BlockSpec(memory_space=pl.ANY)]
     specs += [pl.BlockSpec(memory_space=pltpu.VMEM)] * 2
-    if begin % width == 0:
-        steps, place = 2, begin // width
-        specs += [pl.BlockSpec(memory_space=pltpu.VMEM)] * len(pieces)
-        out_spec = pl.BlockSpec((rows // steps, width), lambda i: (i, place))
-    else:
-        block = block_width(begin, width, unit)
-        steps, place = width // block, begin // block
-        specs += piece_specs([(piece, 0) for piece in pieces], block)
-        out_spec = pl.BlockSpec((rows, block), lambda i: (0, place + i))
+    steps, height = 2, rows // 2
+    specs += [pl.BlockSpec(memory_space=pltpu.VMEM)] * len(pieces)
+    out_spec = pl.BlockSpec(
+        (pl.Element(height), pl.Element(width)), lambda i: (i * height, begin)
+    )
     return pl.pallas_call(
         kernel,
         grid=(steps,),
@@ -382,7 +374,7 @@
 
     def multiply(band, near, index, token):
         begin, far = chunks[index]
-        return band_chunk(band, near, weights, far, begin, columns, unit, token)
+        return band_chunk(band, near, weights, far, begin, columns, token)
 
     token = send_slice(1, token)
     token = send_chunk(0, 0, token)

time: 112 us -> 112 us (level)
  transfers between devices with their start and end apart: 24 -> 24, of which waited for: 13 -> 14; matrix products, arithmetic and copies ran while one was open for 0% -> 0% of each run, Pallas kernels for 23% -> 22%
where the time goes in v5:
time: 112 us
  waiting for transfers between devices  50.7 us (45%)
  starting transfers between devices  28.6 us (26%)
  Pallas kernels  26.8 us (24%)
  local copies, waits for them, and re-layouts  5.57 us (5%)
    pallas_call x4, Pallas kernels, near_chunk(): pl.pallas_call(near_kernel, grid=(width // unit,), in_specs=[pl.BlockSpec...  14.1 us
    ppermute x1, waiting for transfers between devices, shards(): moved = lax.ppermute(held, 'tile', swap(tiles, members))  12.1 us
    pallas_call x4, Pallas kernels, band_chunk(): pl.pallas_call(kernel, grid=(steps,), in_specs=specs + [token_spec()], ou...  9.35 us
    ppermute x1, waiting for transfers between devices, shards(): moved = lax.ppermute(held, 'tile', swap(tiles, bit * members))  9.31 us
    ppermute x8, waiting for transfers between devices, send_far(): lax.ppermute(cut, 'blk', ring_shift(blks, by))  9.11 us
    ppermute x8, starting transfers between devices, send_far(): lax.ppermute(cut, 'blk', ring_shift(blks, by))  8.25 us
    ppermute x3, waiting for transfers between devices, send_slab(): behind.append(lax.ppermute(behind[-1] if behind else piece, 'blk', back))  6.36 us
    ppermute x3, waiting for transfers between devices, shards(): lax.ppermute(blocks[distance], 'tile', swap(tiles, distance * members))  6.06 us
  transfers between devices with their start and end apart: 24, of which 14 were waited for; matrix products, arithmetic and copies ran while one was open for 0% of the time, Pallas kernels for 22%

profile of v5, /device:TPU:0, one launch (start us, length us, event | category | flops | bytes accessed | tf_op | source)
XLA Modules:
  0.0 111.8 jit_solution(3081042499086921622)
XLA Ops:
  0.0 1.3 %slice.3.refs_6_ = bf16[256,2048]{1,0:T(8,128)(2,1)S(1)} slice(bf16[256,6144]{1,0:T(8,128)(2,1)} %refs_1_.9), slice={[0:256], [0:2048]} | slice | bytes 2097152 | tf_op jit(solution)/shard_map/slice | solution.py:342
  1.3 3.0 %collective-permute-start.7 = (bf16[256,2048]{1,0:T(8,128)(2,1)S(1)}, bf16[256,2048]{1,0:T(8,128)(2,1)S(1)}, u32[]{:S(2)}, u32[]{:S(2)}) collective-permute-start(bf16[256,2048]{1,0:T(8,128)(2,1)S(1)} %slice.3.refs_6_), channel_id=1, source_target_pairs={{0,16},{8,0},{24,8},{16,24},{1,17},{9,1},{25,9},{17,25},{2,18},{10... | collective-permute-start | bytes 3145736 | tf_op jit(solution)/shard_map/ppermute | solution.py:221
  4.4 0.9 copy-done.1
  5.3 0.7 copy-done.2
  6.0 0.7 copy-done.3
  6.7 0.7 copy-done.4
  7.3 0.7 copy-done.5
  8.0 0.7 copy-done.6
  8.6 1.6 %shard_map.73 = (bf16[64,512]{1,0:T(8,128)(2,1)S(1)}, bf16[64,512]{1,0:T(8,128)(2,1)S(1)}, bf16[64,512]{1,0:T(8,128)(2,1)S(1)}, bf16[64,512]{1,0:T(8,128)(2,1)S(1)}) custom-call(s32[8]{0:T(128)S(1)} %copy-done.4, s32[8]{0:T(128)S(1)} %copy-done.5, s32[8]{0:T(128)S(1)} %copy-done.6, bf16[256,512]{1,0:T(8,128)(2,1)S(1)} %copy-done.1, f32[1,256]{1,0:T(1,128)S(1)} %bitcast.9, ...), custom_call_target="tpu_custom_call" | custom-call | flops 99999997952 | tf_op jit(solution)/shard_map/pallas_call | solution.py:101
  10.2 2.1 %collective-permute-start = (bf16[64,512]{1,0:T(8,128)(2,1)S(1)}, bf16[64,512]{1,0:T(8,128)(2,1)S(1)}, u32[]{:S(2)}, u32[]{:S(2)}) collective-permute-start(bf16[64,512]{1,0:T(8,128)(2,1)S(1)} %get-tuple-element.52), channel_id=1, source_target_pairs={{0,2},{1,3},{2,0},{3,1},{4,6},{5,7},{6,4},{7,5},{8,10},{9,11},{10,... | collective-permute-start | bytes 196616 | tf_op jit(solution)/shard_map/ppermute | solution.py:348
  12.3 2.6 %collective-permute-start.1 = (bf16[64,512]{1,0:T(8,128)(2,1)S(1)}, bf16[64,512]{1,0:T(8,128)(2,1)S(1)}, u32[]{:S(2)}, u32[]{:S(2)}) collective-permute-start(bf16[64,512]{1,0:T(8,128)(2,1)S(1)} %get-tuple-element.53), channel_id=1, source_target_pairs={{0,4},{1,5},{2,6},{3,7},{4,0},{5,1},{6,2},{7,3},{8,12},{9,13},{10,... | collective-permute-start | bytes 196616 | tf_op jit(solution)/shard_map/ppermute | solution.py:348
  14.9 4.1 %collective-permute-done.1.refs_2_ = bf16[64,512]{1,0:T(8,128)(2,1)S(1)} collective-permute-done((bf16[64,512]{1,0:T(8,128)(2,1)S(1)}, bf16[64,512]{1,0:T(8,128)(2,1)S(1)}, u32[]{:S(2)}, u32[]{:S(2)}) %collective-permute-start.1) | collective-permute-done | bytes 65568 | tf_op jit(solution)/shard_map/ppermute | solution.py:348
  19.0 2.0 %collective-permute-done.2.refs_3_ = bf16[64,512]{1,0:T(8,128)(2,1)S(1)} collective-permute-done((bf16[64,512]{1,0:T(8,128)(2,1)S(1)}, bf16[64,512]{1,0:T(8,128)(2,1)S(1)}, u32[]{:S(2)}, u32[]{:S(2)}) %collective-permute-start.2) | collective-permute-done | bytes 65568 | tf_op jit(solution)/shard_map/ppermute | solution.py:348
  21.0 1.5 %collective-permute-start.3 = (bf16[64,512]{1,0:T(8,128)(2,1)S(1)}, bf16[64,512]{1,0:T(8,128)(2,1)S(1)}, u32[]{:S(2)}, u32[]{:S(2)}) collective-permute-start(bf16[64,512]{1,0:T(8,128)(2,1)S(1)} %get-tuple-element.56), channel_id=1, source_target_pairs={{0,8},{8,24},{24,16},{16,0},{1,9},{9,25},{25,17},{17,1},{2,10},{10... | collective-permute-start | bytes 196616 | tf_op jit(solution)/shard_map/ppermute | solution.py:351
  22.6 1.5 %collective-permute-start.4 = (bf16[64,512]{1,0:T(8,128)(2,1)S(1)}, bf16[64,512]{1,0:T(8,128)(2,1)S(1)}, u32[]{:S(2)}, u32[]{:S(2)}) collective-permute-start(bf16[64,512]{1,0:T(8,128)(2,1)S(1)} %get-tuple-element.57), channel_id=1, source_target_pairs={{0,24},{8,16},{24,0},{16,8},{1,25},{9,17},{25,1},{17,9},{2,26},{10... | collective-permute-start | bytes 196616 | tf_op jit(solution)/shard_map/ppermute | solution.py:351
  24.1 1.5 %collective-permute-start.5 = (bf16[64,512]{1,0:T(8,128)(2,1)S(1)}, bf16[64,512]{1,0:T(8,128)(2,1)S(1)}, u32[]{:S(2)}, u32[]{:S(2)}) collective-permute-start(bf16[64,512]{1,0:T(8,128)(2,1)S(1)} %get-tuple-element.58), channel_id=1, source_target_pairs={{0,16},{8,0},{24,8},{16,24},{1,17},{9,1},{25,9},{17,25},{2,18},{10... | collective-permute-start | bytes 196616 | tf_op jit(solution)/shard_map/ppermute | solution.py:351
  25.5 0.4 shard_map.75
  26.0 3.0 %collective-permute-done.7.behind.refs_3_ = bf16[256,2048]{1,0:T(8,128)(2,1)S(1)} collective-permute-done((bf16[256,2048]{1,0:T(8,128)(2,1)S(1)}, bf16[256,2048]{1,0:T(8,128)(2,1)S(1)}, u32[]{:S(2)}, u32[]{:S(2)}) %collective-permute-start.7) | collective-permute-done | bytes 1048608 | tf_op jit(solution)/shard_map/ppermute | solution.py:221
  29.0 2.6 %collective-permute-start.15 = (bf16[256,3072]{1,0:T(8,128)(2,1)S(1)}, bf16[256,3072]{1,0:T(8,128)(2,1)S(1)}, u32[]{:S(2)}, u32[]{:S(2)}) collective-permute-start(bf16[256,3072]{1,0:T(8,128)(2,1)S(1)} %get-tuple-element.71), channel_id=1, source_target_pairs={{0,16},{8,0},{24,8},{16,24},{1,17},{9,1},{25,9},{17,25},{2,18},{10... | collective-permute-start | bytes 4718600 | tf_op jit(solution)/shard_map/ppermute | solution.py:221
  31.7 2.1 %collective-permute-done.4.refs_2_ = bf16[64,512]{1,0:T(8,128)(2,1)S(1)} collective-permute-done((bf16[64,512]{1,0:T(8,128)(2,1)S(1)}, bf16[64,512]{1,0:T(8,128)(2,1)S(1)}, u32[]{:S(2)}, u32[]{:S(2)}) %collective-permute-start.4) | collective-permute-done | bytes 65568 | tf_op jit(solution)/shard_map/ppermute | solution.py:351
  33.9 2.7 %collective-permute-start.8 = (bf16[1,4,64,512]{3,2,1,0:T(8,128)(2,1)S(1)}, bf16[1,4,64,512]{3,2,1,0:T(8,128)(2,1)S(1)}, u32[]{:S(2)}, u32[]{:S(2)}) collective-permute-start(bf16[1,4,64,512]{3,2,1,0:T(8,128)(2,1)S(1)} %bitcast.7), channel_id=1, source_target_pairs={{0,4},{1,5},{2,6},{3,7},{4,0},{5,1},{6,2},{7,3},{8,12},{9,13},{10,... | collective-permute-start | bytes 786440 | tf_op jit(solution)/shard_map/ppermute | solution.py:385
  36.5 9.3 %collective-permute-done.8.refs_1_ = bf16[1,4,64,512]{3,2,1,0:T(8,128)(2,1)S(1)} collective-permute-done((bf16[1,4,64,512]{3,2,1,0:T(8,128)(2,1)S(1)}, bf16[1,4,64,512]{3,2,1,0:T(8,128)(2,1)S(1)}, u32[]{:S(2)}, u32[]{:S(2)}) %collective-permute-start.8) | collective-permute-done | bytes 262176 | tf_op jit(solution)/shard_map/ppermute | solution.py:385
  45.9 0.7 collective-permute-start.9
  46.6 12.1 %collective-permute-done.9.refs_1_ = bf16[2,4,64,512]{3,2,1,0:T(8,128)(2,1)S(1)} collective-permute-done((bf16[2,4,64,512]{3,2,1,0:T(8,128)(2,1)S(1)}, bf16[2,4,64,512]{3,2,1,0:T(8,128)(2,1)S(1)}, u32[]{:S(2)}, u32[]{:S(2)}) %collective-permute-start.9) | collective-permute-done | bytes 524320 | tf_op jit(solution)/shard_map/ppermute | solution.py:390
  58.7 2.0 %collective-permute-start.13 = (bf16[128,2048]{1,0:T(8,128)(2,1)S(1)}, bf16[128,2048]{1,0:T(8,128)(2,1)S(1)}, u32[]{:S(2)}, u32[]{:S(2)}) collective-permute-start(bf16[128,2048]{1,0:T(8,128)(2,1)S(1)} %get-tuple-element.70), channel_id=1, source_target_pairs={{0,16},{8,0},{24,8},{16,24},{1,17},{9,1},{25,9},{17,25},{2,18},{10... | collective-permute-start | bytes 1572872 | tf_op jit(solution)/shard_map/ppermute | solution.py:258
  60.8 0.8 shard_map.79
  61.6 4.7 %shard_map.80 = (f32[1024,2048]{1,0:T(8,128)S(1)}, bf16[16,128]{1,0:T(8,128)(2,1)S(1)}) custom-call(bf16[1024,1024]{1,0:T(8,128)(2,1)S(1)} %get-tuple-element.66.refs_0_.weights.refs_1_, bf16[256,6144]{1,0:T(8,128)(2,1)S(1)} %copy-done, bf16[256,2048]{1,0:T(8,128)(2,1)S(1)} %collective-permute-done.6.ahead.refs_2_, ...), custom_call_target="tpu_custom_call" | custom-call | flops 1000000 | tf_op jit(solution)/shard_map/pallas_call | solution.py:297
  66.3 2.7 %collective-permute-done.14.refs_1_.refs_2_.ahead = bf16[256,3072]{1,0:T(8,128)(2,1)S(1)} collective-permute-done((bf16[256,3072]{1,0:T(8,128)(2,1)S(1)}, bf16[256,3072]{1,0:T(8,128)(2,1)S(1)}, u32[]{:S(2)}, u32[]{:S(2)}) %collective-permute-start.14) | collective-permute-done | bytes 1572896 | tf_op jit(solution)/shard_map/ppermute | solution.py:220
  69.1 0.3 collective-permute-start.19
  69.4 1.8 %collective-permute-start.18 = (bf16[256,1024]{1,0:T(8,128)(2,1)S(1)}, bf16[256,1024]{1,0:T(8,128)(2,1)S(1)}, u32[]{:S(2)}, u32[]{:S(2)}) collective-permute-start(bf16[256,1024]{1,0:T(8,128)(2,1)S(1)} %get-tuple-element.81), channel_id=1, source_target_pairs={{0,8},{8,24},{24,16},{16,0},{1,9},{9,25},{25,17},{17,1},{2,10},{10... | collective-permute-start | bytes 1572872 | tf_op jit(solution)/shard_map/ppermute | solution.py:220
  71.2 3.5 %shard_map.82 = (f32[1024,1536]{1,0:T(8,128)S(1)}, bf16[16,128]{1,0:T(8,128)(2,1)S(1)}) custom-call(bf16[1024,1024]{1,0:T(8,128)(2,1)S(1)} %get-tuple-element.66.refs_0_.weights.refs_1_, bf16[256,6144]{1,0:T(8,128)(2,1)S(1)} %copy-done, bf16[256,3072]{1,0:T(8,128)(2,1)S(1)} %collective-permute-done.14.refs_1_.refs_2_.ahead, ...), custom_call_target="tpu_custom_call" | custom-call | flops 1000000 | tf_op jit(solution)/shard_map/pallas_call | solution.py:297
  74.8 3.5 %shard_map.83 = (f32[1024,1536]{1,0:T(8,128)S(1)}, bf16[16,128]{1,0:T(8,128)(2,1)S(1)}) custom-call(bf16[1024,1024]{1,0:T(8,128)(2,1)S(1)} %get-tuple-element.66.refs_0_.weights.refs_1_, bf16[256,6144]{1,0:T(8,128)(2,1)S(1)} %copy-done, bf16[256,3072]{1,0:T(8,128)(2,1)S(1)} %collective-permute-done.14.refs_1_.refs_2_.ahead, ...), custom_call_target="tpu_custom_call" | custom-call | flops 1000000 | tf_op jit(solution)/shard_map/pallas_call | solution.py:297
  78.3 1.9 %collective-permute-done.12.refs_1_.refs_0_ = bf16[128,2048]{1,0:T(8,128)(2,1)S(1)} collective-permute-done((bf16[128,2048]{1,0:T(8,128)(2,1)S(1)}, bf16[128,2048]{1,0:T(8,128)(2,1)S(1)}, u32[]{:S(2)}, u32[]{:S(2)}) %collective-permute-start.12) | collective-permute-done | bytes 524320 | tf_op jit(solution)/shard_map/ppermute | solution.py:258
  80.5 1.8 %collective-permute-start.16 = (bf16[112,1536]{1,0:T(8,128)(2,1)S(1)}, bf16[112,1536]{1,0:T(8,128)(2,1)S(1)}, u32[]{:S(2)}, u32[]{:S(2)}) collective-permute-start(bf16[112,1536]{1,0:T(8,128)(2,1)S(1)} %get-tuple-element.79), channel_id=1, source_target_pairs={{0,8},{8,24},{24,16},{16,0},{1,9},{9,25},{25,17},{17,1},{2,10},{10... | collective-permute-start | bytes 1032200 | tf_op jit(solution)/shard_map/ppermute | solution.py:258
  82.3 2.8 %shard_map.85 = (bf16[1024,6144]{1,0:T(8,128)(2,1)}, bf16[16,128]{1,0:T(8,128)(2,1)S(1)}) custom-call(f32[1024,2048]{1,0:T(8,128)S(1)} %get-tuple-element.68.near, bf16[1024,1024]{1,0:T(8,128)(2,1)S(1)} %get-tuple-element.66.refs_0_.weights.refs_1_, bf16[128,2048]{1,0:T(8,128)(2,1)S(1)} %collective-permute-done.12.refs_1_.refs_0_, ...), custom_call_target="tpu_custom_call" | custom-call | flops 1000000 | tf_op jit(solution)/shard_map/pallas_call | solution.py:322
  85.1 3.4 %collective-permute-done.19.refs_2_.refs_3_.behind = bf16[256,1024]{1,0:T(8,128)(2,1)S(1)} collective-permute-done((bf16[256,1024]{1,0:T(8,128)(2,1)S(1)}, bf16[256,1024]{1,0:T(8,128)(2,1)S(1)}, u32[]{:S(2)}, u32[]{:S(2)}) %collective-permute-start.19) | collective-permute-done | bytes 524320 | tf_op jit(solution)/shard_map/ppermute | solution.py:221
  88.5 2.9 %collective-permute-done.18.refs_1_.refs_2_.ahead = bf16[256,1024]{1,0:T(8,128)(2,1)S(1)} collective-permute-done((bf16[256,1024]{1,0:T(8,128)(2,1)S(1)}, bf16[256,1024]{1,0:T(8,128)(2,1)S(1)}, u32[]{:S(2)}, u32[]{:S(2)}) %collective-permute-start.18) | collective-permute-done | bytes 524320 | tf_op jit(solution)/shard_map/ppermute | solution.py:220
  91.5 2.0 %collective-permute-start.21 = (bf16[128,1536]{1,0:T(8,128)(2,1)S(1)}, bf16[128,1536]{1,0:T(8,128)(2,1)S(1)}, u32[]{:S(2)}, u32[]{:S(2)}) collective-permute-start(bf16[128,1536]{1,0:T(8,128)(2,1)S(1)} %get-tuple-element.89), channel_id=1, source_target_pairs={{0,16},{8,0},{24,8},{16,24},{1,17},{9,1},{25,9},{17,25},{2,18},{10... | collective-permute-start | bytes 1179656 | tf_op jit(solution)/shard_map/ppermute | solution.py:258
  93.6 2.4 %shard_map.87 = (f32[1024,1024]{1,0:T(8,128)S(1)}, bf16[16,128]{1,0:T(8,128)(2,1)S(1)}) custom-call(bf16[1024,1024]{1,0:T(8,128)(2,1)S(1)} %get-tuple-element.66.refs_0_.weights.refs_1_, bf16[256,6144]{1,0:T(8,128)(2,1)S(1)} %copy-done, bf16[256,1024]{1,0:T(8,128)(2,1)S(1)} %collective-permute-done.18.refs_1_.refs_2_.ahead, ...), custom_call_target="tpu_custom_call" | custom-call | flops 1000000 | tf_op jit(solution)/shard_map/pallas_call | solution.py:297
  95.9 2.9 %collective-permute-done.16.refs_1_.refs_2_ = bf16[112,1536]{1,0:T(8,128)(2,1)S(1)} collective-permute-done((bf16[112,1536]{1,0:T(8,128)(2,1)S(1)}, bf16[112,1536]{1,0:T(8,128)(2,1)S(1)}, u32[]{:S(2)}, u32[]{:S(2)}) %collective-permute-start.16) | collective-permute-done | bytes 344096 | tf_op jit(solution)/shard_map/ppermute | solution.py:258
  98.8 1.1 %collective-permute-start.22 = (bf16[128,1024]{1,0:T(8,128)(2,1)S(1)}, bf16[128,1024]{1,0:T(8,128)(2,1)S(1)}, u32[]{:S(2)}, u32[]{:S(2)}) collective-permute-start(bf16[128,1024]{1,0:T(8,128)(2,1)S(1)} %get-tuple-element.93), channel_id=1, source_target_pairs={{0,8},{8,24},{24,16},{16,0},{1,9},{9,25},{25,17},{17,1},{2,10},{10... | collective-permute-start | bytes 786440 | tf_op jit(solution)/shard_map/ppermute | solution.py:258
  100.0 1.0 collective-permute-start.23
  100.9 2.3 %shard_map.89 = (bf16[1024,6144]{1,0:T(8,128)(2,1)}, bf16[16,128]{1,0:T(8,128)(2,1)S(1)}) custom-call(bf16[1024,6144]{1,0:T(8,128)(2,1)} %get-tuple-element.77._, f32[1024,1536]{1,0:T(8,128)S(1)} %get-tuple-element.78.refs_0_, bf16[1024,1024]{1,0:T(8,128)(2,1)S(1)} %get-tuple-element.66.refs_0_.weights.refs_1_, ...), custom_call_target="tpu_custom_call", output_to_operand_aliasing={{0}: (0, {})} | custom-call | flops 1000000 | tf_op jit(solution)/shard_map/pallas_call | solution.py:322
  103.3 3.3 %collective-permute-done.20.refs_2_ = bf16[128,1536]{1,0:T(8,128)(2,1)S(1)} collective-permute-done((bf16[128,1536]{1,0:T(8,128)(2,1)S(1)}, bf16[128,1536]{1,0:T(8,128)(2,1)S(1)}, u32[]{:S(2)}, u32[]{:S(2)}) %collective-permute-start.20) | collective-permute-done | bytes 393248 | tf_op jit(solution)/shard_map/ppermute | solution.py:258
  106.5 2.3 %shard_map.90 = (bf16[1024,6144]{1,0:T(8,128)(2,1)}, bf16[16,128]{1,0:T(8,128)(2,1)S(1)}) custom-call(bf16[1024,6144]{1,0:T(8,128)(2,1)} %get-tuple-element.86._, f32[1024,1536]{1,0:T(8,128)S(1)} %get-tuple-element.87.refs_0_, bf16[1024,1024]{1,0:T(8,128)(2,1)S(1)} %get-tuple-element.66.refs_0_.weights.refs_1_, ...), custom_call_target="tpu_custom_call", output_to_operand_aliasing={{0}: (0, {})} | custom-call | flops 1000000 | tf_op jit(solution)/shard_map/pallas_call | solution.py:322
  108.9 0.5 collective-permute-done.22.refs_2_
  109.3 0.6 collective-permute-done.23.refs_3_
  110.0 1.9 %shard_map.91 = (bf16[1024,6144]{1,0:T(8,128)(2,1)}, bf16[16,128]{1,0:T(8,128)(2,1)}) custom-call(bf16[1024,6144]{1,0:T(8,128)(2,1)} %get-tuple-element.91._, f32[1024,1024]{1,0:T(8,128)S(1)} %get-tuple-element.92.refs_0_, bf16[1024,1024]{1,0:T(8,128)(2,1)S(1)} %get-tuple-element.66.refs_0_.weights.refs_1_, ...), custom_call_target="tpu_custom_call", output_to_operand_aliasing={{0}: (0, {})} | custom-call | flops 1000000 | tf_op jit(solution)/shard_map/pallas_call | solution.py:322
  (34 shorter events, 0.9 us)
Async XLA Ops:
  1.3 27.7 %collective-permute-start.7 = (bf16[256,2048]{1,0:T(8,128)(2,1)S(1)}, bf16[256,2048]{1,0:T(8,128)(2,1)S(1)}, u32[]{:S(2)}, u32[]{:S(2)}) collective-permute-start(bf16[256,2048]{1,0:T(8,128)(2,1)S(1)} %slice.3.refs_6_), channel_id=1, source_target_pairs={{0,16},{8,0},{24,8},{16,24},{1,17},{9,1},{25,9},{17,25},{2,18},{10... | collective-permute-start | bytes 3145736 | tf_op jit(solution)/shard_map/ppermute | solution.py:221
  4.3 27.3 %collective-permute-start.6 = (bf16[256,2048]{1,0:T(8,128)(2,1)S(1)}, bf16[256,2048]{1,0:T(8,128)(2,1)S(1)}, u32[]{:S(2)}, u32[]{:S(2)}) collective-permute-start(bf16[256,2048]{1,0:T(8,128)(2,1)S(1)} %slice.3.refs_6_), channel_id=1, source_target_pairs={{0,8},{8,24},{24,16},{16,0},{1,9},{9,25},{25,17},{17,1},{2,10},{10... | collective-permute-start | bytes 3145736 | tf_op jit(solution)/shard_map/ppermute | solution.py:220
  4.4 0.9 copy-start.1
  5.3 0.7 copy-start.2
  6.0 0.7 copy-start.3
  6.7 0.7 copy-start.4
  7.3 0.7 copy-start.5
  8.0 0.7 copy-start.6
  8.6 16.9 %copy-start = (bf16[256,6144]{1,0:T(8,128)(2,1)S(1)}, bf16[256,6144]{1,0:T(8,128)(2,1)}, u32[]{:S(2)}) copy-start(bf16[256,6144]{1,0:T(8,128)(2,1)} %refs_1_.9) | copy-start | bytes 9437188
  10.2 4.7 %collective-permute-start = (bf16[64,512]{1,0:T(8,128)(2,1)S(1)}, bf16[64,512]{1,0:T(8,128)(2,1)S(1)}, u32[]{:S(2)}, u32[]{:S(2)}) collective-permute-start(bf16[64,512]{1,0:T(8,128)(2,1)S(1)} %get-tuple-element.52), channel_id=1, source_target_pairs={{0,2},{1,3},{2,0},{3,1},{4,6},{5,7},{6,4},{7,5},{8,10},{9,11},{10,... | collective-permute-start | bytes 196616 | tf_op jit(solution)/shard_map/ppermute | solution.py:348
  12.3 6.7 %collective-permute-start.1 = (bf16[64,512]{1,0:T(8,128)(2,1)S(1)}, bf16[64,512]{1,0:T(8,128)(2,1)S(1)}, u32[]{:S(2)}, u32[]{:S(2)}) collective-permute-start(bf16[64,512]{1,0:T(8,128)(2,1)S(1)} %get-tuple-element.53), channel_id=1, source_target_pairs={{0,4},{1,5},{2,6},{3,7},{4,0},{5,1},{6,2},{7,3},{8,12},{9,13},{10,... | collective-permute-start | bytes 196616 | tf_op jit(solution)/shard_map/ppermute | solution.py:348
  14.9 6.1 %collective-permute-start.2 = (bf16[64,512]{1,0:T(8,128)(2,1)S(1)}, bf16[64,512]{1,0:T(8,128)(2,1)S(1)}, u32[]{:S(2)}, u32[]{:S(2)}) collective-permute-start(bf16[64,512]{1,0:T(8,128)(2,1)S(1)} %get-tuple-element.54), channel_id=1, source_target_pairs={{0,6},{1,7},{2,4},{3,5},{4,2},{5,3},{6,0},{7,1},{8,14},{9,15},{10,... | collective-permute-start | bytes 196616 | tf_op jit(solution)/shard_map/ppermute | solution.py:348
  21.0 10.7 %collective-permute-start.3 = (bf16[64,512]{1,0:T(8,128)(2,1)S(1)}, bf16[64,512]{1,0:T(8,128)(2,1)S(1)}, u32[]{:S(2)}, u32[]{:S(2)}) collective-permute-start(bf16[64,512]{1,0:T(8,128)(2,1)S(1)} %get-tuple-element.56), channel_id=1, source_target_pairs={{0,8},{8,24},{24,16},{16,0},{1,9},{9,25},{25,17},{17,1},{2,10},{10... | collective-permute-start | bytes 196616 | tf_op jit(solution)/shard_map/ppermute | solution.py:351
  22.6 11.3 %collective-permute-start.4 = (bf16[64,512]{1,0:T(8,128)(2,1)S(1)}, bf16[64,512]{1,0:T(8,128)(2,1)S(1)}, u32[]{:S(2)}, u32[]{:S(2)}) collective-permute-start(bf16[64,512]{1,0:T(8,128)(2,1)S(1)} %get-tuple-element.57), channel_id=1, source_target_pairs={{0,24},{8,16},{24,0},{16,8},{1,25},{9,17},{25,1},{17,9},{2,26},{10... | collective-permute-start | bytes 196616 | tf_op jit(solution)/shard_map/ppermute | solution.py:351
  24.1 9.8 %collective-permute-start.5 = (bf16[64,512]{1,0:T(8,128)(2,1)S(1)}, bf16[64,512]{1,0:T(8,128)(2,1)S(1)}, u32[]{:S(2)}, u32[]{:S(2)}) collective-permute-start(bf16[64,512]{1,0:T(8,128)(2,1)S(1)} %get-tuple-element.58), channel_id=1, source_target_pairs={{0,16},{8,0},{24,8},{16,24},{1,17},{9,1},{25,9},{17,25},{2,18},{10... | collective-permute-start | bytes 196616 | tf_op jit(solution)/shard_map/ppermute | solution.py:351
  29.0 37.3 %collective-permute-start.15 = (bf16[256,3072]{1,0:T(8,128)(2,1)S(1)}, bf16[256,3072]{1,0:T(8,128)(2,1)S(1)}, u32[]{:S(2)}, u32[]{:S(2)}) collective-permute-start(bf16[256,3072]{1,0:T(8,128)(2,1)S(1)} %get-tuple-element.71), channel_id=1, source_target_pairs={{0,16},{8,0},{24,8},{16,24},{1,17},{9,1},{25,9},{17,25},{2,18},{10... | collective-permute-start | bytes 4718600 | tf_op jit(solution)/shard_map/ppermute | solution.py:221
  31.6 37.3 %collective-permute-start.14 = (bf16[256,3072]{1,0:T(8,128)(2,1)S(1)}, bf16[256,3072]{1,0:T(8,128)(2,1)S(1)}, u32[]{:S(2)}, u32[]{:S(2)}) collective-permute-start(bf16[256,3072]{1,0:T(8,128)(2,1)S(1)} %get-tuple-element.71), channel_id=1, source_target_pairs={{0,8},{8,24},{24,16},{16,0},{1,9},{9,25},{25,17},{17,1},{2,10},{10... | collective-permute-start | bytes 4718600 | tf_op jit(solution)/shard_map/ppermute | solution.py:220
  33.9 12.0 %collective-permute-start.8 = (bf16[1,4,64,512]{3,2,1,0:T(8,128)(2,1)S(1)}, bf16[1,4,64,512]{3,2,1,0:T(8,128)(2,1)S(1)}, u32[]{:S(2)}, u32[]{:S(2)}) collective-permute-start(bf16[1,4,64,512]{3,2,1,0:T(8,128)(2,1)S(1)} %bitcast.7), channel_id=1, source_target_pairs={{0,4},{1,5},{2,6},{3,7},{4,0},{5,1},{6,2},{7,3},{8,12},{9,13},{10,... | collective-permute-start | bytes 786440 | tf_op jit(solution)/shard_map/ppermute | solution.py:385
  45.9 12.8 %collective-permute-start.9 = (bf16[2,4,64,512]{3,2,1,0:T(8,128)(2,1)S(1)}, bf16[2,4,64,512]{3,2,1,0:T(8,128)(2,1)S(1)}, u32[]{:S(2)}, u32[]{:S(2)}) collective-permute-start(bf16[2,4,64,512]{3,2,1,0:T(8,128)(2,1)S(1)} %bitcast.4), channel_id=1, source_target_pairs={{0,2},{1,3},{2,0},{3,1},{4,6},{5,7},{6,4},{7,5},{8,10},{9,11},{10,... | collective-permute-start | bytes 1572872 | tf_op jit(solution)/shard_map/ppermute | solution.py:390
  46.6 12.1 %collective-permute-start.10 = (bf16[2,4,64,512]{3,2,1,0:T(8,128)(2,1)S(1)}, bf16[2,4,64,512]{3,2,1,0:T(8,128)(2,1)S(1)}, u32[]{:S(2)}, u32[]{:S(2)}) collective-permute-start(bf16[2,4,64,512]{3,2,1,0:T(8,128)(2,1)S(1)} %bitcast.5), channel_id=1, source_target_pairs={{0,1},{1,0},{2,3},{3,2},{4,5},{5,4},{6,7},{7,6},{8,9},{9,8},{10,11... | collective-permute-start | bytes 1572872 | tf_op jit(solution)/shard_map/ppermute | solution.py:395
  58.7 2.0 %collective-permute-start.11 = (bf16[2,4,64,512]{3,2,1,0:T(8,128)(2,1)S(1)}, bf16[2,4,64,512]{3,2,1,0:T(8,128)(2,1)S(1)}, u32[]{:S(2)}, u32[]{:S(2)}) collective-permute-start(bf16[2,4,64,512]{3,2,1,0:T(8,128)(2,1)S(1)} %collective-permute-done.9.refs_1_), channel_id=1, source_target_pairs={{0,1},{1,0},{2,3},{3,2},{4,5},{5,4},{6,7},{7,6},{8,9},{9,8},{10,11... | collective-permute-start | bytes 1572872 | tf_op jit(solution)/shard_map/ppermute | solution.py:395
  58.7 21.5 %collective-permute-start.12 = (bf16[128,2048]{1,0:T(8,128)(2,1)S(1)}, bf16[128,2048]{1,0:T(8,128)(2,1)S(1)}, u32[]{:S(2)}, u32[]{:S(2)}) collective-permute-start(bf16[128,2048]{1,0:T(8,128)(2,1)S(1)} %get-tuple-element.69), channel_id=1, source_target_pairs={{0,8},{8,24},{24,16},{16,0},{1,9},{9,25},{25,17},{17,1},{2,10},{10... | collective-permute-start | bytes 1572872 | tf_op jit(solution)/shard_map/ppermute | solution.py:258
  58.7 21.5 %collective-permute-start.13 = (bf16[128,2048]{1,0:T(8,128)(2,1)S(1)}, bf16[128,2048]{1,0:T(8,128)(2,1)S(1)}, u32[]{:S(2)}, u32[]{:S(2)}) collective-permute-start(bf16[128,2048]{1,0:T(8,128)(2,1)S(1)} %get-tuple-element.70), channel_id=1, source_target_pairs={{0,16},{8,0},{24,8},{16,24},{1,17},{9,1},{25,9},{17,25},{2,18},{10... | collective-permute-start | bytes 1572872 | tf_op jit(solution)/shard_map/ppermute | solution.py:258
  69.1 19.4 %collective-permute-start.19 = (bf16[256,1024]{1,0:T(8,128)(2,1)S(1)}, bf16[256,1024]{1,0:T(8,128)(2,1)S(1)}, u32[]{:S(2)}, u32[]{:S(2)}) collective-permute-start(bf16[256,1024]{1,0:T(8,128)(2,1)S(1)} %get-tuple-element.81), channel_id=1, source_target_pairs={{0,16},{8,0},{24,8},{16,24},{1,17},{9,1},{25,9},{17,25},{2,18},{10... | collective-permute-start | bytes 1572872 | tf_op jit(solution)/shard_map/ppermute | solution.py:221
  69.4 22.0 %collective-permute-start.18 = (bf16[256,1024]{1,0:T(8,128)(2,1)S(1)}, bf16[256,1024]{1,0:T(8,128)(2,1)S(1)}, u32[]{:S(2)}, u32[]{:S(2)}) collective-permute-start(bf16[256,1024]{1,0:T(8,128)(2,1)S(1)} %get-tuple-element.81), channel_id=1, source_target_pairs={{0,8},{8,24},{24,16},{16,0},{1,9},{9,25},{25,17},{17,1},{2,10},{10... | collective-permute-start | bytes 1572872 | tf_op jit(solution)/shard_map/ppermute | solution.py:220
  80.3 18.5 %collective-permute-start.17 = (bf16[144,1536]{1,0:T(8,128)(2,1)S(1)}, bf16[144,1536]{1,0:T(8,128)(2,1)S(1)}, u32[]{:S(2)}, u32[]{:S(2)}) collective-permute-start(bf16[144,1536]{1,0:T(8,128)(2,1)S(1)} %get-tuple-element.80), channel_id=1, source_target_pairs={{0,16},{8,0},{24,8},{16,24},{1,17},{9,1},{25,9},{17,25},{2,18},{10... | collective-permute-start | bytes 1327112 | tf_op jit(solution)/shard_map/ppermute | solution.py:258
  80.5 18.3 %collective-permute-start.16 = (bf16[112,1536]{1,0:T(8,128)(2,1)S(1)}, bf16[112,1536]{1,0:T(8,128)(2,1)S(1)}, u32[]{:S(2)}, u32[]{:S(2)}) collective-permute-start(bf16[112,1536]{1,0:T(8,128)(2,1)S(1)} %get-tuple-element.79), channel_id=1, source_target_pairs={{0,8},{8,24},{24,16},{16,0},{1,9},{9,25},{25,17},{17,1},{2,10},{10... | collective-permute-start | bytes 1032200 | tf_op jit(solution)/shard_map/ppermute | solution.py:258
  91.5 15.0 %collective-permute-start.20 = (bf16[128,1536]{1,0:T(8,128)(2,1)S(1)}, bf16[128,1536]{1,0:T(8,128)(2,1)S(1)}, u32[]{:S(2)}, u32[]{:S(2)}) collective-permute-start(bf16[128,1536]{1,0:T(8,128)(2,1)S(1)} %get-tuple-element.88), channel_id=1, source_target_pairs={{0,8},{8,24},{24,16},{16,0},{1,9},{9,25},{25,17},{17,1},{2,10},{10... | collective-permute-start | bytes 1179656 | tf_op jit(solution)/shard_map/ppermute | solution.py:258
  91.5 15.0 %collective-permute-start.21 = (bf16[128,1536]{1,0:T(8,128)(2,1)S(1)}, bf16[128,1536]{1,0:T(8,128)(2,1)S(1)}, u32[]{:S(2)}, u32[]{:S(2)}) collective-permute-start(bf16[128,1536]{1,0:T(8,128)(2,1)S(1)} %get-tuple-element.89), channel_id=1, source_target_pairs={{0,16},{8,0},{24,8},{16,24},{1,17},{9,1},{25,9},{17,25},{2,18},{10... | collective-permute-start | bytes 1179656 | tf_op jit(solution)/shard_map/ppermute | solution.py:258
  98.8 10.5 %collective-permute-start.22 = (bf16[128,1024]{1,0:T(8,128)(2,1)S(1)}, bf16[128,1024]{1,0:T(8,128)(2,1)S(1)}, u32[]{:S(2)}, u32[]{:S(2)}) collective-permute-start(bf16[128,1024]{1,0:T(8,128)(2,1)S(1)} %get-tuple-element.93), channel_id=1, source_target_pairs={{0,8},{8,24},{24,16},{16,0},{1,9},{9,25},{25,17},{17,1},{2,10},{10... | collective-permute-start | bytes 786440 | tf_op jit(solution)/shard_map/ppermute | solution.py:258
  100.0 10.0 %collective-permute-start.23 = (bf16[128,1024]{1,0:T(8,128)(2,1)S(1)}, bf16[128,1024]{1,0:T(8,128)(2,1)S(1)}, u32[]{:S(2)}, u32[]{:S(2)}) collective-permute-start(bf16[128,1024]{1,0:T(8,128)(2,1)S(1)} %get-tuple-element.94), channel_id=1, source_target_pairs={{0,16},{8,0},{24,8},{16,24},{1,17},{9,1},{25,9},{17,25},{2,18},{10... | collective-permute-start | bytes 786440 | tf_op jit(solution)/shard_map/ppermute | solution.py:258

commit v6 on v5

--- a/solution.py
+++ b/solution.py
@@ -275,8 +275,11 @@
 
 
 def far_kernel(near, weights, *refs):
-    pieces, (_, out, token) = refs[:-3], refs[-3:]
-    token[...] = jnp.zeros_like(token)
+    if len(refs) == 3:
+        *pieces, out = refs
+    else:
+        *pieces, _, out, token = refs
+        token[...] = jnp.zeros_like(token)
     rows = out.shape[0]
     stacked = jnp.concatenate([piece[...] for piece in pieces], axis=0)
     last = pl.ds(weights.shape[1] - stacked.shape[0], stacked.shape[0])
@@ -322,13 +325,14 @@
     return pl.pallas_call(
         kernel,
         grid=(steps,),
-        in_specs=specs + [token_spec()],
-        out_specs=[out_spec, token_spec()],
-        out_shape=[jax.ShapeDtypeStruct((rows, columns), jnp.bfloat16), token_shape()],
+        in_specs=specs + [token_spec()] * len(after),
+        out_specs=[out_spec] + [token_spec()] * len(after),
+        out_shape=[jax.ShapeDtypeStruct((rows, columns), jnp.bfloat16)]
+        + [token_shape()] * len(after),
         input_output_aliases=aliases,
         compiler_params=pltpu.CompilerParams(vmem_limit_bytes=VMEM_LIMIT),
         cost_estimate=cost(1),
-    )(*operands, near, weights, *pieces, after)
+    )(*operands, near, weights, *pieces, *after)
 
 
 def shards(left_rows, right_rows, row_weight, coupling, assign, orders, offsets):
@@ -372,9 +376,9 @@
         pieces = [(left_rows, begin)] + [(array, offset) for array in ahead + behind[::-1]]
         return near_chunk(weights, pieces, width, block_width(begin, width, unit), token)
 
-    def multiply(band, near, index, token):
+    def multiply(band, near, index, after):
         begin, far = chunks[index]
-        return band_chunk(band, near, weights, far, begin, columns, token)
+        return band_chunk(band, near, weights, far, begin, columns, after)
 
     token = send_slice(1, token)
     token = send_chunk(0, 0, token)
@@ -404,12 +408,13 @@
     nears[1], token = multiply_near(1, 0, token)
     nears[2], token = multiply_near(1, 1, token)
     token = send_chunk(1, 0, token, chunks[0][-1])
-    band, token = multiply(None, nears[0], 0, token)
+    band, token = multiply(None, nears[0], 0, [token])
     token = send_chunk(1, 1, token, [streams[2][0][-1], streams[2][1][-1]])
     nears[3], token = multiply_near(2, 0, token)
     token = send_chunk(2, 0, token, chunks[1][-1])
-    for index in range(1, len(chunks)):
-        band, token = multiply(band, nears[index], index, token)
+    band, _ = multiply(band, nears[1], 1, [token])
+    for index in range(2, len(chunks)):
+        (band,) = multiply(band, nears[index], index, [])
     return band
 
 

time: 112 us -> 112 us (level)
  no operation moved by 1% of the time
where the time goes in v6:
time: 112 us
  waiting for transfers between devices  50.7 us (45%)
  starting transfers between devices  28.6 us (26%)
  Pallas kernels  26.8 us (24%)
  local copies, waits for them, and re-layouts  5.57 us (5%)
    pallas_call x4, Pallas kernels, near_chunk(): pl.pallas_call(near_kernel, grid=(width // unit,), in_specs=[pl.BlockSpec...  14.1 us
    ppermute x1, waiting for transfers between devices, shards(): moved = lax.ppermute(held, 'tile', swap(tiles, members))  12.1 us
    pallas_call x4, Pallas kernels, band_chunk(): pl.pallas_call(kernel, grid=(steps,), in_specs=specs + [token_spec()] * l...  9.33 us
    ppermute x1, waiting for transfers between devices, shards(): moved = lax.ppermute(held, 'tile', swap(tiles, bit * members))  9.31 us
    ppermute x8, waiting for transfers between devices, send_far(): lax.ppermute(cut, 'blk', ring_shift(blks, by))  9.12 us
    ppermute x8, starting transfers between devices, send_far(): lax.ppermute(cut, 'blk', ring_shift(blks, by))  8.25 us
    ppermute x3, waiting for transfers between devices, send_slab(): behind.append(lax.ppermute(behind[-1] if behind else piece, 'blk', back))  6.36 us
    ppermute x3, waiting for transfers between devices, shards(): lax.ppermute(blocks[distance], 'tile', swap(tiles, distance * members))  6.06 us
  transfers between devices with their start and end apart: 24, of which 14 were waited for; matrix products, arithmetic and copies ran while one was open for 0% of the time, Pallas kernels for 22%

profile of v6, /device:TPU:0, one launch (start us, length us, event | category | flops | bytes accessed | tf_op | source)
XLA Modules:
  0.0 111.8 jit_solution(13016966896194105753)
XLA Ops:
  0.0 1.3 %slice.3.refs_6_ = bf16[256,2048]{1,0:T(8,128)(2,1)S(1)} slice(bf16[256,6144]{1,0:T(8,128)(2,1)} %refs_1_.9), slice={[0:256], [0:2048]} | slice | bytes 2097152 | tf_op jit(solution)/shard_map/slice | solution.py:346
  1.3 3.0 %collective-permute-start.7 = (bf16[256,2048]{1,0:T(8,128)(2,1)S(1)}, bf16[256,2048]{1,0:T(8,128)(2,1)S(1)}, u32[]{:S(2)}, u32[]{:S(2)}) collective-permute-start(bf16[256,2048]{1,0:T(8,128)(2,1)S(1)} %slice.3.refs_6_), channel_id=1, source_target_pairs={{0,16},{8,0},{24,8},{16,24},{1,17},{9,1},{25,9},{17,25},{2,18},{10... | collective-permute-start | bytes 3145736 | tf_op jit(solution)/shard_map/ppermute | solution.py:221
  4.4 0.9 copy-done.1
  5.3 0.7 copy-done.2
  6.0 0.7 copy-done.3
  6.7 0.7 copy-done.4
  7.3 0.7 copy-done.5
  8.0 0.7 copy-done.6
  8.6 1.6 %shard_map.73 = (bf16[64,512]{1,0:T(8,128)(2,1)S(1)}, bf16[64,512]{1,0:T(8,128)(2,1)S(1)}, bf16[64,512]{1,0:T(8,128)(2,1)S(1)}, bf16[64,512]{1,0:T(8,128)(2,1)S(1)}) custom-call(s32[8]{0:T(128)S(1)} %copy-done.4, s32[8]{0:T(128)S(1)} %copy-done.5, s32[8]{0:T(128)S(1)} %copy-done.6, bf16[256,512]{1,0:T(8,128)(2,1)S(1)} %copy-done.1, f32[1,256]{1,0:T(1,128)S(1)} %bitcast.9, ...), custom_call_target="tpu_custom_call" | custom-call | flops 99999997952 | tf_op jit(solution)/shard_map/pallas_call | solution.py:101
  10.2 2.1 %collective-permute-start = (bf16[64,512]{1,0:T(8,128)(2,1)S(1)}, bf16[64,512]{1,0:T(8,128)(2,1)S(1)}, u32[]{:S(2)}, u32[]{:S(2)}) collective-permute-start(bf16[64,512]{1,0:T(8,128)(2,1)S(1)} %get-tuple-element.48), channel_id=1, source_target_pairs={{0,2},{1,3},{2,0},{3,1},{4,6},{5,7},{6,4},{7,5},{8,10},{9,11},{10,... | collective-permute-start | bytes 196616 | tf_op jit(solution)/shard_map/ppermute | solution.py:352
  12.3 2.6 %collective-permute-start.1 = (bf16[64,512]{1,0:T(8,128)(2,1)S(1)}, bf16[64,512]{1,0:T(8,128)(2,1)S(1)}, u32[]{:S(2)}, u32[]{:S(2)}) collective-permute-start(bf16[64,512]{1,0:T(8,128)(2,1)S(1)} %get-tuple-element.49), channel_id=1, source_target_pairs={{0,4},{1,5},{2,6},{3,7},{4,0},{5,1},{6,2},{7,3},{8,12},{9,13},{10,... | collective-permute-start | bytes 196616 | tf_op jit(solution)/shard_map/ppermute | solution.py:352
  14.9 4.1 %collective-permute-done.1.refs_2_ = bf16[64,512]{1,0:T(8,128)(2,1)S(1)} collective-permute-done((bf16[64,512]{1,0:T(8,128)(2,1)S(1)}, bf16[64,512]{1,0:T(8,128)(2,1)S(1)}, u32[]{:S(2)}, u32[]{:S(2)}) %collective-permute-start.1) | collective-permute-done | bytes 65568 | tf_op jit(solution)/shard_map/ppermute | solution.py:352
  19.0 2.0 %collective-permute-done.2.refs_3_ = bf16[64,512]{1,0:T(8,128)(2,1)S(1)} collective-permute-done((bf16[64,512]{1,0:T(8,128)(2,1)S(1)}, bf16[64,512]{1,0:T(8,128)(2,1)S(1)}, u32[]{:S(2)}, u32[]{:S(2)}) %collective-permute-start.2) | collective-permute-done | bytes 65568 | tf_op jit(solution)/shard_map/ppermute | solution.py:352
  21.0 1.5 %collective-permute-start.3 = (bf16[64,512]{1,0:T(8,128)(2,1)S(1)}, bf16[64,512]{1,0:T(8,128)(2,1)S(1)}, u32[]{:S(2)}, u32[]{:S(2)}) collective-permute-start(bf16[64,512]{1,0:T(8,128)(2,1)S(1)} %get-tuple-element.52), channel_id=1, source_target_pairs={{0,8},{8,24},{24,16},{16,0},{1,9},{9,25},{25,17},{17,1},{2,10},{10... | collective-permute-start | bytes 196616 | tf_op jit(solution)/shard_map/ppermute | solution.py:355
  22.6 1.5 %collective-permute-start.4 = (bf16[64,512]{1,0:T(8,128)(2,1)S(1)}, bf16[64,512]{1,0:T(8,128)(2,1)S(1)}, u32[]{:S(2)}, u32[]{:S(2)}) collective-permute-start(bf16[64,512]{1,0:T(8,128)(2,1)S(1)} %get-tuple-element.53), channel_id=1, source_target_pairs={{0,24},{8,16},{24,0},{16,8},{1,25},{9,17},{25,1},{17,9},{2,26},{10... | collective-permute-start | bytes 196616 | tf_op jit(solution)/shard_map/ppermute | solution.py:355
  24.1 1.5 %collective-permute-start.5 = (bf16[64,512]{1,0:T(8,128)(2,1)S(1)}, bf16[64,512]{1,0:T(8,128)(2,1)S(1)}, u32[]{:S(2)}, u32[]{:S(2)}) collective-permute-start(bf16[64,512]{1,0:T(8,128)(2,1)S(1)} %get-tuple-element.54), channel_id=1, source_target_pairs={{0,16},{8,0},{24,8},{16,24},{1,17},{9,1},{25,9},{17,25},{2,18},{10... | collective-permute-start | bytes 196616 | tf_op jit(solution)/shard_map/ppermute | solution.py:355
  25.5 0.4 shard_map.75
  26.0 3.0 %collective-permute-done.7.behind.refs_3_ = bf16[256,2048]{1,0:T(8,128)(2,1)S(1)} collective-permute-done((bf16[256,2048]{1,0:T(8,128)(2,1)S(1)}, bf16[256,2048]{1,0:T(8,128)(2,1)S(1)}, u32[]{:S(2)}, u32[]{:S(2)}) %collective-permute-start.7) | collective-permute-done | bytes 1048608 | tf_op jit(solution)/shard_map/ppermute | solution.py:221
  29.0 2.6 %collective-permute-start.15 = (bf16[256,3072]{1,0:T(8,128)(2,1)S(1)}, bf16[256,3072]{1,0:T(8,128)(2,1)S(1)}, u32[]{:S(2)}, u32[]{:S(2)}) collective-permute-start(bf16[256,3072]{1,0:T(8,128)(2,1)S(1)} %get-tuple-element.67), channel_id=1, source_target_pairs={{0,16},{8,0},{24,8},{16,24},{1,17},{9,1},{25,9},{17,25},{2,18},{10... | collective-permute-start | bytes 4718600 | tf_op jit(solution)/shard_map/ppermute | solution.py:221
  31.7 2.1 %collective-permute-done.4.refs_2_ = bf16[64,512]{1,0:T(8,128)(2,1)S(1)} collective-permute-done((bf16[64,512]{1,0:T(8,128)(2,1)S(1)}, bf16[64,512]{1,0:T(8,128)(2,1)S(1)}, u32[]{:S(2)}, u32[]{:S(2)}) %collective-permute-start.4) | collective-permute-done | bytes 65568 | tf_op jit(solution)/shard_map/ppermute | solution.py:355
  33.9 2.7 %collective-permute-start.8 = (bf16[1,4,64,512]{3,2,1,0:T(8,128)(2,1)S(1)}, bf16[1,4,64,512]{3,2,1,0:T(8,128)(2,1)S(1)}, u32[]{:S(2)}, u32[]{:S(2)}) collective-permute-start(bf16[1,4,64,512]{3,2,1,0:T(8,128)(2,1)S(1)} %bitcast.7), channel_id=1, source_target_pairs={{0,4},{1,5},{2,6},{3,7},{4,0},{5,1},{6,2},{7,3},{8,12},{9,13},{10,... | collective-permute-start | bytes 786440 | tf_op jit(solution)/shard_map/ppermute | solution.py:389
  36.5 9.3 %collective-permute-done.8.refs_1_ = bf16[1,4,64,512]{3,2,1,0:T(8,128)(2,1)S(1)} collective-permute-done((bf16[1,4,64,512]{3,2,1,0:T(8,128)(2,1)S(1)}, bf16[1,4,64,512]{3,2,1,0:T(8,128)(2,1)S(1)}, u32[]{:S(2)}, u32[]{:S(2)}) %collective-permute-start.8) | collective-permute-done | bytes 262176 | tf_op jit(solution)/shard_map/ppermute | solution.py:389
  45.9 0.7 collective-permute-start.9
  46.6 12.1 %collective-permute-done.9.refs_1_ = bf16[2,4,64,512]{3,2,1,0:T(8,128)(2,1)S(1)} collective-permute-done((bf16[2,4,64,512]{3,2,1,0:T(8,128)(2,1)S(1)}, bf16[2,4,64,512]{3,2,1,0:T(8,128)(2,1)S(1)}, u32[]{:S(2)}, u32[]{:S(2)}) %collective-permute-start.9) | collective-permute-done | bytes 524320 | tf_op jit(solution)/shard_map/ppermute | solution.py:394
  58.7 2.0 %collective-permute-start.13 = (bf16[128,2048]{1,0:T(8,128)(2,1)S(1)}, bf16[128,2048]{1,0:T(8,128)(2,1)S(1)}, u32[]{:S(2)}, u32[]{:S(2)}) collective-permute-start(bf16[128,2048]{1,0:T(8,128)(2,1)S(1)} %get-tuple-element.66), channel_id=1, source_target_pairs={{0,16},{8,0},{24,8},{16,24},{1,17},{9,1},{25,9},{17,25},{2,18},{10... | collective-permute-start | bytes 1572872 | tf_op jit(solution)/shard_map/ppermute | solution.py:258
  60.8 0.8 shard_map.79
  61.6 4.7 %shard_map.80 = (f32[1024,2048]{1,0:T(8,128)S(1)}, bf16[16,128]{1,0:T(8,128)(2,1)S(1)}) custom-call(bf16[1024,1024]{1,0:T(8,128)(2,1)S(1)} %get-tuple-element.62.refs_0_.weights.refs_1_, bf16[256,6144]{1,0:T(8,128)(2,1)S(1)} %copy-done, bf16[256,2048]{1,0:T(8,128)(2,1)S(1)} %collective-permute-done.6.ahead.refs_2_, ...), custom_call_target="tpu_custom_call" | custom-call | flops 1000000 | tf_op jit(solution)/shard_map/pallas_call | solution.py:300
  66.3 2.7 %collective-permute-done.14.refs_1_.refs_2_.ahead = bf16[256,3072]{1,0:T(8,128)(2,1)S(1)} collective-permute-done((bf16[256,3072]{1,0:T(8,128)(2,1)S(1)}, bf16[256,3072]{1,0:T(8,128)(2,1)S(1)}, u32[]{:S(2)}, u32[]{:S(2)}) %collective-permute-start.14) | collective-permute-done | bytes 1572896 | tf_op jit(solution)/shard_map/ppermute | solution.py:220
  69.1 0.3 collective-permute-start.19
  69.4 1.8 %collective-permute-start.18 = (bf16[256,1024]{1,0:T(8,128)(2,1)S(1)}, bf16[256,1024]{1,0:T(8,128)(2,1)S(1)}, u32[]{:S(2)}, u32[]{:S(2)}) collective-permute-start(bf16[256,1024]{1,0:T(8,128)(2,1)S(1)} %get-tuple-element.77), channel_id=1, source_target_pairs={{0,8},{8,24},{24,16},{16,0},{1,9},{9,25},{25,17},{17,1},{2,10},{10... | collective-permute-start | bytes 1572872 | tf_op jit(solution)/shard_map/ppermute | solution.py:220
  71.2 3.5 %shard_map.82 = (f32[1024,1536]{1,0:T(8,128)S(1)}, bf16[16,128]{1,0:T(8,128)(2,1)S(1)}) custom-call(bf16[1024,1024]{1,0:T(8,128)(2,1)S(1)} %get-tuple-element.62.refs_0_.weights.refs_1_, bf16[256,6144]{1,0:T(8,128)(2,1)S(1)} %copy-done, bf16[256,3072]{1,0:T(8,128)(2,1)S(1)} %collective-permute-done.14.refs_1_.refs_2_.ahead, ...), custom_call_target="tpu_custom_call" | custom-call | flops 1000000 | tf_op jit(solution)/shard_map/pallas_call | solution.py:300
  74.8 3.5 %shard_map.83 = (f32[1024,1536]{1,0:T(8,128)S(1)}, bf16[16,128]{1,0:T(8,128)(2,1)S(1)}) custom-call(bf16[1024,1024]{1,0:T(8,128)(2,1)S(1)} %get-tuple-element.62.refs_0_.weights.refs_1_, bf16[256,6144]{1,0:T(8,128)(2,1)S(1)} %copy-done, bf16[256,3072]{1,0:T(8,128)(2,1)S(1)} %collective-permute-done.14.refs_1_.refs_2_.ahead, ...), custom_call_target="tpu_custom_call" | custom-call | flops 1000000 | tf_op jit(solution)/shard_map/pallas_call | solution.py:300
  78.3 1.9 %collective-permute-done.12.refs_1_.refs_0_ = bf16[128,2048]{1,0:T(8,128)(2,1)S(1)} collective-permute-done((bf16[128,2048]{1,0:T(8,128)(2,1)S(1)}, bf16[128,2048]{1,0:T(8,128)(2,1)S(1)}, u32[]{:S(2)}, u32[]{:S(2)}) %collective-permute-start.12) | collective-permute-done | bytes 524320 | tf_op jit(solution)/shard_map/ppermute | solution.py:258
  80.5 1.8 %collective-permute-start.16 = (bf16[112,1536]{1,0:T(8,128)(2,1)S(1)}, bf16[112,1536]{1,0:T(8,128)(2,1)S(1)}, u32[]{:S(2)}, u32[]{:S(2)}) collective-permute-start(bf16[112,1536]{1,0:T(8,128)(2,1)S(1)} %get-tuple-element.75), channel_id=1, source_target_pairs={{0,8},{8,24},{24,16},{16,0},{1,9},{9,25},{25,17},{17,1},{2,10},{10... | collective-permute-start | bytes 1032200 | tf_op jit(solution)/shard_map/ppermute | solution.py:258
  82.3 2.8 %shard_map.85 = (bf16[1024,6144]{1,0:T(8,128)(2,1)}, bf16[16,128]{1,0:T(8,128)(2,1)S(1)}) custom-call(f32[1024,2048]{1,0:T(8,128)S(1)} %get-tuple-element.64.near, bf16[1024,1024]{1,0:T(8,128)(2,1)S(1)} %get-tuple-element.62.refs_0_.weights.refs_1_, bf16[128,2048]{1,0:T(8,128)(2,1)S(1)} %collective-permute-done.12.refs_1_.refs_0_, ...), custom_call_target="tpu_custom_call" | custom-call | flops 1000000 | tf_op jit(solution)/shard_map/pallas_call | solution.py:325
  85.1 3.4 %collective-permute-done.19.refs_2_.refs_3_.behind = bf16[256,1024]{1,0:T(8,128)(2,1)S(1)} collective-permute-done((bf16[256,1024]{1,0:T(8,128)(2,1)S(1)}, bf16[256,1024]{1,0:T(8,128)(2,1)S(1)}, u32[]{:S(2)}, u32[]{:S(2)}) %collective-permute-start.19) | collective-permute-done | bytes 524320 | tf_op jit(solution)/shard_map/ppermute | solution.py:221
  88.5 2.9 %collective-permute-done.18.refs_1_.refs_2_.ahead = bf16[256,1024]{1,0:T(8,128)(2,1)S(1)} collective-permute-done((bf16[256,1024]{1,0:T(8,128)(2,1)S(1)}, bf16[256,1024]{1,0:T(8,128)(2,1)S(1)}, u32[]{:S(2)}, u32[]{:S(2)}) %collective-permute-start.18) | collective-permute-done | bytes 524320 | tf_op jit(solution)/shard_map/ppermute | solution.py:220
  91.5 2.0 %collective-permute-start.21 = (bf16[128,1536]{1,0:T(8,128)(2,1)S(1)}, bf16[128,1536]{1,0:T(8,128)(2,1)S(1)}, u32[]{:S(2)}, u32[]{:S(2)}) collective-permute-start(bf16[128,1536]{1,0:T(8,128)(2,1)S(1)} %get-tuple-element.85), channel_id=1, source_target_pairs={{0,16},{8,0},{24,8},{16,24},{1,17},{9,1},{25,9},{17,25},{2,18},{10... | collective-permute-start | bytes 1179656 | tf_op jit(solution)/shard_map/ppermute | solution.py:258
  93.6 2.4 %shard_map.87 = (f32[1024,1024]{1,0:T(8,128)S(1)}, bf16[16,128]{1,0:T(8,128)(2,1)S(1)}) custom-call(bf16[1024,1024]{1,0:T(8,128)(2,1)S(1)} %get-tuple-element.62.refs_0_.weights.refs_1_, bf16[256,6144]{1,0:T(8,128)(2,1)S(1)} %copy-done, bf16[256,1024]{1,0:T(8,128)(2,1)S(1)} %collective-permute-done.18.refs_1_.refs_2_.ahead, ...), custom_call_target="tpu_custom_call" | custom-call | flops 1000000 | tf_op jit(solution)/shard_map/pallas_call | solution.py:300
  95.9 2.9 %collective-permute-done.16.refs_1_.refs_2_ = bf16[112,1536]{1,0:T(8,128)(2,1)S(1)} collective-permute-done((bf16[112,1536]{1,0:T(8,128)(2,1)S(1)}, bf16[112,1536]{1,0:T(8,128)(2,1)S(1)}, u32[]{:S(2)}, u32[]{:S(2)}) %collective-permute-start.16) | collective-permute-done | bytes 344096 | tf_op jit(solution)/shard_map/ppermute | solution.py:258
  98.8 1.1 %collective-permute-start.22 = (bf16[128,1024]{1,0:T(8,128)(2,1)S(1)}, bf16[128,1024]{1,0:T(8,128)(2,1)S(1)}, u32[]{:S(2)}, u32[]{:S(2)}) collective-permute-start(bf16[128,1024]{1,0:T(8,128)(2,1)S(1)} %get-tuple-element.87), channel_id=1, source_target_pairs={{0,8},{8,24},{24,16},{16,0},{1,9},{9,25},{25,17},{17,1},{2,10},{10... | collective-permute-start | bytes 786440 | tf_op jit(solution)/shard_map/ppermute | solution.py:258
  100.0 1.0 collective-permute-start.23
  100.9 2.3 %shard_map.89 = (bf16[1024,6144]{1,0:T(8,128)(2,1)}, bf16[16,128]{1,0:T(8,128)(2,1)}) custom-call(bf16[1024,6144]{1,0:T(8,128)(2,1)} %get-tuple-element.73._, f32[1024,1536]{1,0:T(8,128)S(1)} %get-tuple-element.74.refs_0_, bf16[1024,1024]{1,0:T(8,128)(2,1)S(1)} %get-tuple-element.62.refs_0_.weights.refs_1_, ...), custom_call_target="tpu_custom_call", output_to_operand_aliasing={{0}: (0, {})} | custom-call | flops 1000000 | tf_op jit(solution)/shard_map/pallas_call | solution.py:325
  103.3 3.3 %collective-permute-done.20.refs_2_ = bf16[128,1536]{1,0:T(8,128)(2,1)S(1)} collective-permute-done((bf16[128,1536]{1,0:T(8,128)(2,1)S(1)}, bf16[128,1536]{1,0:T(8,128)(2,1)S(1)}, u32[]{:S(2)}, u32[]{:S(2)}) %collective-permute-start.20) | collective-permute-done | bytes 393248 | tf_op jit(solution)/shard_map/ppermute | solution.py:258
  106.5 2.3 %shard_map.90._ = bf16[1024,6144]{1,0:T(8,128)(2,1)} custom-call(bf16[1024,6144]{1,0:T(8,128)(2,1)} %get-tuple-element.82._, f32[1024,1536]{1,0:T(8,128)S(1)} %get-tuple-element.83.refs_0_, bf16[1024,1024]{1,0:T(8,128)(2,1)S(1)} %get-tuple-element.62.refs_0_.weights.refs_1_, ...), custom_call_target="tpu_custom_call", output_to_operand_aliasing={{}: (0, {})} | custom-call | flops 1000000 | tf_op jit(solution)/shard_map/pallas_call | solution.py:325
  108.9 0.5 collective-permute-done.22.refs_2_
  109.3 0.6 collective-permute-done.23.refs_3_
  110.0 1.9 %shard_map.91 = bf16[1024,6144]{1,0:T(8,128)(2,1)} custom-call(bf16[1024,6144]{1,0:T(8,128)(2,1)} %shard_map.90._, f32[1024,1024]{1,0:T(8,128)S(1)} %get-tuple-element.86.refs_0_, bf16[1024,1024]{1,0:T(8,128)(2,1)S(1)} %get-tuple-element.62.refs_0_.weights.refs_1_, ...), custom_call_target="tpu_custom_call", output_to_operand_aliasing={{}: (0, {})} | custom-call | flops 1000000 | tf_op jit(solution)/shard_map/pallas_call | solution.py:325
  (34 shorter events, 0.9 us)
Async XLA Ops:
  1.3 27.7 %collective-permute-start.7 = (bf16[256,2048]{1,0:T(8,128)(2,1)S(1)}, bf16[256,2048]{1,0:T(8,128)(2,1)S(1)}, u32[]{:S(2)}, u32[]{:S(2)}) collective-permute-start(bf16[256,2048]{1,0:T(8,128)(2,1)S(1)} %slice.3.refs_6_), channel_id=1, source_target_pairs={{0,16},{8,0},{24,8},{16,24},{1,17},{9,1},{25,9},{17,25},{2,18},{10... | collective-permute-start | bytes 3145736 | tf_op jit(solution)/shard_map/ppermute | solution.py:221
  4.3 27.3 %collective-permute-start.6 = (bf16[256,2048]{1,0:T(8,128)(2,1)S(1)}, bf16[256,2048]{1,0:T(8,128)(2,1)S(1)}, u32[]{:S(2)}, u32[]{:S(2)}) collective-permute-start(bf16[256,2048]{1,0:T(8,128)(2,1)S(1)} %slice.3.refs_6_), channel_id=1, source_target_pairs={{0,8},{8,24},{24,16},{16,0},{1,9},{9,25},{25,17},{17,1},{2,10},{10... | collective-permute-start | bytes 3145736 | tf_op jit(solution)/shard_map/ppermute | solution.py:220
  4.4 0.9 copy-start.1
  5.3 0.7 copy-start.2
  6.0 0.7 copy-start.3
  6.7 0.7 copy-start.4
  7.3 0.7 copy-start.5
  8.0 0.7 copy-start.6
  8.6 16.9 %copy-start = (bf16[256,6144]{1,0:T(8,128)(2,1)S(1)}, bf16[256,6144]{1,0:T(8,128)(2,1)}, u32[]{:S(2)}) copy-start(bf16[256,6144]{1,0:T(8,128)(2,1)} %refs_1_.9) | copy-start | bytes 9437188
  10.2 4.7 %collective-permute-start = (bf16[64,512]{1,0:T(8,128)(2,1)S(1)}, bf16[64,512]{1,0:T(8,128)(2,1)S(1)}, u32[]{:S(2)}, u32[]{:S(2)}) collective-permute-start(bf16[64,512]{1,0:T(8,128)(2,1)S(1)} %get-tuple-element.48), channel_id=1, source_target_pairs={{0,2},{1,3},{2,0},{3,1},{4,6},{5,7},{6,4},{7,5},{8,10},{9,11},{10,... | collective-permute-start | bytes 196616 | tf_op jit(solution)/shard_map/ppermute | solution.py:352
  12.3 6.7 %collective-permute-start.1 = (bf16[64,512]{1,0:T(8,128)(2,1)S(1)}, bf16[64,512]{1,0:T(8,128)(2,1)S(1)}, u32[]{:S(2)}, u32[]{:S(2)}) collective-permute-start(bf16[64,512]{1,0:T(8,128)(2,1)S(1)} %get-tuple-element.49), channel_id=1, source_target_pairs={{0,4},{1,5},{2,6},{3,7},{4,0},{5,1},{6,2},{7,3},{8,12},{9,13},{10,... | collective-permute-start | bytes 196616 | tf_op jit(solution)/shard_map/ppermute | solution.py:352
  14.9 6.1 %collective-permute-start.2 = (bf16[64,512]{1,0:T(8,128)(2,1)S(1)}, bf16[64,512]{1,0:T(8,128)(2,1)S(1)}, u32[]{:S(2)}, u32[]{:S(2)}) collective-permute-start(bf16[64,512]{1,0:T(8,128)(2,1)S(1)} %get-tuple-element.50), channel_id=1, source_target_pairs={{0,6},{1,7},{2,4},{3,5},{4,2},{5,3},{6,0},{7,1},{8,14},{9,15},{10,... | collective-permute-start | bytes 196616 | tf_op jit(solution)/shard_map/ppermute | solution.py:352
  21.0 10.7 %collective-permute-start.3 = (bf16[64,512]{1,0:T(8,128)(2,1)S(1)}, bf16[64,512]{1,0:T(8,128)(2,1)S(1)}, u32[]{:S(2)}, u32[]{:S(2)}) collective-permute-start(bf16[64,512]{1,0:T(8,128)(2,1)S(1)} %get-tuple-element.52), channel_id=1, source_target_pairs={{0,8},{8,24},{24,16},{16,0},{1,9},{9,25},{25,17},{17,1},{2,10},{10... | collective-permute-start | bytes 196616 | tf_op jit(solution)/shard_map/ppermute | solution.py:355
  22.6 11.3 %collective-permute-start.4 = (bf16[64,512]{1,0:T(8,128)(2,1)S(1)}, bf16[64,512]{1,0:T(8,128)(2,1)S(1)}, u32[]{:S(2)}, u32[]{:S(2)}) collective-permute-start(bf16[64,512]{1,0:T(8,128)(2,1)S(1)} %get-tuple-element.53), channel_id=1, source_target_pairs={{0,24},{8,16},{24,0},{16,8},{1,25},{9,17},{25,1},{17,9},{2,26},{10... | collective-permute-start | bytes 196616 | tf_op jit(solution)/shard_map/ppermute | solution.py:355
  24.1 9.8 %collective-permute-start.5 = (bf16[64,512]{1,0:T(8,128)(2,1)S(1)}, bf16[64,512]{1,0:T(8,128)(2,1)S(1)}, u32[]{:S(2)}, u32[]{:S(2)}) collective-permute-start(bf16[64,512]{1,0:T(8,128)(2,1)S(1)} %get-tuple-element.54), channel_id=1, source_target_pairs={{0,16},{8,0},{24,8},{16,24},{1,17},{9,1},{25,9},{17,25},{2,18},{10... | collective-permute-start | bytes 196616 | tf_op jit(solution)/shard_map/ppermute | solution.py:355
  29.0 37.3 %collective-permute-start.15 = (bf16[256,3072]{1,0:T(8,128)(2,1)S(1)}, bf16[256,3072]{1,0:T(8,128)(2,1)S(1)}, u32[]{:S(2)}, u32[]{:S(2)}) collective-permute-start(bf16[256,3072]{1,0:T(8,128)(2,1)S(1)} %get-tuple-element.67), channel_id=1, source_target_pairs={{0,16},{8,0},{24,8},{16,24},{1,17},{9,1},{25,9},{17,25},{2,18},{10... | collective-permute-start | bytes 4718600 | tf_op jit(solution)/shard_map/ppermute | solution.py:221
  31.6 37.3 %collective-permute-start.14 = (bf16[256,3072]{1,0:T(8,128)(2,1)S(1)}, bf16[256,3072]{1,0:T(8,128)(2,1)S(1)}, u32[]{:S(2)}, u32[]{:S(2)}) collective-permute-start(bf16[256,3072]{1,0:T(8,128)(2,1)S(1)} %get-tuple-element.67), channel_id=1, source_target_pairs={{0,8},{8,24},{24,16},{16,0},{1,9},{9,25},{25,17},{17,1},{2,10},{10... | collective-permute-start | bytes 4718600 | tf_op jit(solution)/shard_map/ppermute | solution.py:220
  33.9 12.0 %collective-permute-start.8 = (bf16[1,4,64,512]{3,2,1,0:T(8,128)(2,1)S(1)}, bf16[1,4,64,512]{3,2,1,0:T(8,128)(2,1)S(1)}, u32[]{:S(2)}, u32[]{:S(2)}) collective-permute-start(bf16[1,4,64,512]{3,2,1,0:T(8,128)(2,1)S(1)} %bitcast.7), channel_id=1, source_target_pairs={{0,4},{1,5},{2,6},{3,7},{4,0},{5,1},{6,2},{7,3},{8,12},{9,13},{10,... | collective-permute-start | bytes 786440 | tf_op jit(solution)/shard_map/ppermute | solution.py:389
  45.9 12.8 %collective-permute-start.9 = (bf16[2,4,64,512]{3,2,1,0:T(8,128)(2,1)S(1)}, bf16[2,4,64,512]{3,2,1,0:T(8,128)(2,1)S(1)}, u32[]{:S(2)}, u32[]{:S(2)}) collective-permute-start(bf16[2,4,64,512]{3,2,1,0:T(8,128)(2,1)S(1)} %bitcast.4), channel_id=1, source_target_pairs={{0,2},{1,3},{2,0},{3,1},{4,6},{5,7},{6,4},{7,5},{8,10},{9,11},{10,... | collective-permute-start | bytes 1572872 | tf_op jit(solution)/shard_map/ppermute | solution.py:394
  46.6 12.1 %collective-permute-start.10 = (bf16[2,4,64,512]{3,2,1,0:T(8,128)(2,1)S(1)}, bf16[2,4,64,512]{3,2,1,0:T(8,128)(2,1)S(1)}, u32[]{:S(2)}, u32[]{:S(2)}) collective-permute-start(bf16[2,4,64,512]{3,2,1,0:T(8,128)(2,1)S(1)} %bitcast.5), channel_id=1, source_target_pairs={{0,1},{1,0},{2,3},{3,2},{4,5},{5,4},{6,7},{7,6},{8,9},{9,8},{10,11... | collective-permute-start | bytes 1572872 | tf_op jit(solution)/shard_map/ppermute | solution.py:399
  58.7 2.0 %collective-permute-start.11 = (bf16[2,4,64,512]{3,2,1,0:T(8,128)(2,1)S(1)}, bf16[2,4,64,512]{3,2,1,0:T(8,128)(2,1)S(1)}, u32[]{:S(2)}, u32[]{:S(2)}) collective-permute-start(bf16[2,4,64,512]{3,2,1,0:T(8,128)(2,1)S(1)} %collective-permute-done.9.refs_1_), channel_id=1, source_target_pairs={{0,1},{1,0},{2,3},{3,2},{4,5},{5,4},{6,7},{7,6},{8,9},{9,8},{10,11... | collective-permute-start | bytes 1572872 | tf_op jit(solution)/shard_map/ppermute | solution.py:399
  58.7 21.5 %collective-permute-start.12 = (bf16[128,2048]{1,0:T(8,128)(2,1)S(1)}, bf16[128,2048]{1,0:T(8,128)(2,1)S(1)}, u32[]{:S(2)}, u32[]{:S(2)}) collective-permute-start(bf16[128,2048]{1,0:T(8,128)(2,1)S(1)} %get-tuple-element.65), channel_id=1, source_target_pairs={{0,8},{8,24},{24,16},{16,0},{1,9},{9,25},{25,17},{17,1},{2,10},{10... | collective-permute-start | bytes 1572872 | tf_op jit(solution)/shard_map/ppermute | solution.py:258
  58.7 21.5 %collective-permute-start.13 = (bf16[128,2048]{1,0:T(8,128)(2,1)S(1)}, bf16[128,2048]{1,0:T(8,128)(2,1)S(1)}, u32[]{:S(2)}, u32[]{:S(2)}) collective-permute-start(bf16[128,2048]{1,0:T(8,128)(2,1)S(1)} %get-tuple-element.66), channel_id=1, source_target_pairs={{0,16},{8,0},{24,8},{16,24},{1,17},{9,1},{25,9},{17,25},{2,18},{10... | collective-permute-start | bytes 1572872 | tf_op jit(solution)/shard_map/ppermute | solution.py:258
  69.1 19.4 %collective-permute-start.19 = (bf16[256,1024]{1,0:T(8,128)(2,1)S(1)}, bf16[256,1024]{1,0:T(8,128)(2,1)S(1)}, u32[]{:S(2)}, u32[]{:S(2)}) collective-permute-start(bf16[256,1024]{1,0:T(8,128)(2,1)S(1)} %get-tuple-element.77), channel_id=1, source_target_pairs={{0,16},{8,0},{24,8},{16,24},{1,17},{9,1},{25,9},{17,25},{2,18},{10... | collective-permute-start | bytes 1572872 | tf_op jit(solution)/shard_map/ppermute | solution.py:221
  69.4 22.0 %collective-permute-start.18 = (bf16[256,1024]{1,0:T(8,128)(2,1)S(1)}, bf16[256,1024]{1,0:T(8,128)(2,1)S(1)}, u32[]{:S(2)}, u32[]{:S(2)}) collective-permute-start(bf16[256,1024]{1,0:T(8,128)(2,1)S(1)} %get-tuple-element.77), channel_id=1, source_target_pairs={{0,8},{8,24},{24,16},{16,0},{1,9},{9,25},{25,17},{17,1},{2,10},{10... | collective-permute-start | bytes 1572872 | tf_op jit(solution)/shard_map/ppermute | solution.py:220
  80.3 18.5 %collective-permute-start.17 = (bf16[144,1536]{1,0:T(8,128)(2,1)S(1)}, bf16[144,1536]{1,0:T(8,128)(2,1)S(1)}, u32[]{:S(2)}, u32[]{:S(2)}) collective-permute-start(bf16[144,1536]{1,0:T(8,128)(2,1)S(1)} %get-tuple-element.76), channel_id=1, source_target_pairs={{0,16},{8,0},{24,8},{16,24},{1,17},{9,1},{25,9},{17,25},{2,18},{10... | collective-permute-start | bytes 1327112 | tf_op jit(solution)/shard_map/ppermute | solution.py:258
  80.5 18.3 %collective-permute-start.16 = (bf16[112,1536]{1,0:T(8,128)(2,1)S(1)}, bf16[112,1536]{1,0:T(8,128)(2,1)S(1)}, u32[]{:S(2)}, u32[]{:S(2)}) collective-permute-start(bf16[112,1536]{1,0:T(8,128)(2,1)S(1)} %get-tuple-element.75), channel_id=1, source_target_pairs={{0,8},{8,24},{24,16},{16,0},{1,9},{9,25},{25,17},{17,1},{2,10},{10... | collective-permute-start | bytes 1032200 | tf_op jit(solution)/shard_map/ppermute | solution.py:258
  91.5 15.0 %collective-permute-start.20 = (bf16[128,1536]{1,0:T(8,128)(2,1)S(1)}, bf16[128,1536]{1,0:T(8,128)(2,1)S(1)}, u32[]{:S(2)}, u32[]{:S(2)}) collective-permute-start(bf16[128,1536]{1,0:T(8,128)(2,1)S(1)} %get-tuple-element.84), channel_id=1, source_target_pairs={{0,8},{8,24},{24,16},{16,0},{1,9},{9,25},{25,17},{17,1},{2,10},{10... | collective-permute-start | bytes 1179656 | tf_op jit(solution)/shard_map/ppermute | solution.py:258
  91.5 15.0 %collective-permute-start.21 = (bf16[128,1536]{1,0:T(8,128)(2,1)S(1)}, bf16[128,1536]{1,0:T(8,128)(2,1)S(1)}, u32[]{:S(2)}, u32[]{:S(2)}) collective-permute-start(bf16[128,1536]{1,0:T(8,128)(2,1)S(1)} %get-tuple-element.85), channel_id=1, source_target_pairs={{0,16},{8,0},{24,8},{16,24},{1,17},{9,1},{25,9},{17,25},{2,18},{10... | collective-permute-start | bytes 1179656 | tf_op jit(solution)/shard_map/ppermute | solution.py:258
  98.8 10.5 %collective-permute-start.22 = (bf16[128,1024]{1,0:T(8,128)(2,1)S(1)}, bf16[128,1024]{1,0:T(8,128)(2,1)S(1)}, u32[]{:S(2)}, u32[]{:S(2)}) collective-permute-start(bf16[128,1024]{1,0:T(8,128)(2,1)S(1)} %get-tuple-element.87), channel_id=1, source_target_pairs={{0,8},{8,24},{24,16},{16,0},{1,9},{9,25},{25,17},{17,1},{2,10},{10... | collective-permute-start | bytes 786440 | tf_op jit(solution)/shard_map/ppermute | solution.py:258
  100.0 10.0 %collective-permute-start.23 = (bf16[128,1024]{1,0:T(8,128)(2,1)S(1)}, bf16[128,1024]{1,0:T(8,128)(2,1)S(1)}, u32[]{:S(2)}, u32[]{:S(2)}) collective-permute-start(bf16[128,1024]{1,0:T(8,128)(2,1)S(1)} %get-tuple-element.88), channel_id=1, source_target_pairs={{0,16},{8,0},{24,8},{16,24},{1,17},{9,1},{25,9},{17,25},{2,18},{10... | collective-permute-start | bytes 786440 | tf_op jit(solution)/shard_map/ppermute | solution.py:258

commit v7 on v5

--- a/solution.py
+++ b/solution.py
@@ -8,7 +8,7 @@
 from jax.sharding import PartitionSpec as P
 
 UNITS = 24
-SENDS = ((8,), (6, 6), (4,))
+SENDS = ((8,), (7, 5), (4,))
 SHIFT = (0, 16, 0, 0)
 LANES = 128
 VMEM_LIMIT = 16 * 1024 * 1024

time: 112 us -> 112 us (level)
  Pallas kernels: 26.8 us -> 28.6 us
  waiting for transfers between devices: 50.7 us -> 49.1 us
    ppermute x8, waiting for transfers between devices: 9.11 us -> 7.5 us  [send_far(): lax.ppermute(cut, 'blk', ring_shift(blks, by))]
    pallas_call x4, Pallas kernels: 14.1 us -> 15.6 us  [near_chunk(): pl.pallas_call(near_kernel, grid=(width // unit,), in_specs=[pl.BlockSpec...]
  transfers between devices with their start and end apart: 24 -> 24, of which waited for: 14 -> 15; matrix products, arithmetic and copies ran while one was open for 0% -> 0% of each run, Pallas kernels for 22% -> 24%
where the time goes in v7:
time: 112 us
  waiting for transfers between devices  49.1 us (44%)
  starting transfers between devices  28.6 us (26%)
  Pallas kernels  28.6 us (26%)
  local copies, waits for them, and re-layouts  5.57 us (5%)
    pallas_call x4, Pallas kernels, near_chunk(): pl.pallas_call(near_kernel, grid=(width // unit,), in_specs=[pl.BlockSpec...  15.6 us
    ppermute x1, waiting for transfers between devices, shards(): moved = lax.ppermute(held, 'tile', swap(tiles, members))  12.1 us
    pallas_call x4, Pallas kernels, band_chunk(): pl.pallas_call(kernel, grid=(steps,), in_specs=specs + [token_spec()], ou...  9.34 us
    ppermute x1, waiting for transfers between devices, shards(): moved = lax.ppermute(held, 'tile', swap(tiles, bit * members))  9.31 us
    ppermute x8, starting transfers between devices, send_far(): lax.ppermute(cut, 'blk', ring_shift(blks, by))  8.25 us
    ppermute x8, waiting for transfers between devices, send_far(): lax.ppermute(cut, 'blk', ring_shift(blks, by))  7.5 us
    ppermute x3, waiting for transfers between devices, send_slab(): behind.append(lax.ppermute(behind[-1] if behind else piece, 'blk', back))  6.35 us
    ppermute x3, waiting for transfers between devices, shards(): lax.ppermute(blocks[distance], 'tile', swap(tiles, distance * members))  6.06 us
  transfers between devices with their start and end apart: 24, of which 15 were waited for; matrix products, arithmetic and copies ran while one was open for 0% of the time, Pallas kernels for 24%

profile of v7, /device:TPU:0, one launch (start us, length us, event | category | flops | bytes accessed | tf_op | source)
XLA Modules:
  0.0 112.0 jit_solution(12820475413371358005)
XLA Ops:
  0.0 1.3 %slice.3.refs_6_ = bf16[256,2048]{1,0:T(8,128)(2,1)S(1)} slice(bf16[256,6144]{1,0:T(8,128)(2,1)} %refs_1_.9), slice={[0:256], [0:2048]} | slice | bytes 2097152 | tf_op jit(solution)/shard_map/slice | solution.py:342
  1.3 3.0 %collective-permute-start.7 = (bf16[256,2048]{1,0:T(8,128)(2,1)S(1)}, bf16[256,2048]{1,0:T(8,128)(2,1)S(1)}, u32[]{:S(2)}, u32[]{:S(2)}) collective-permute-start(bf16[256,2048]{1,0:T(8,128)(2,1)S(1)} %slice.3.refs_6_), channel_id=1, source_target_pairs={{0,16},{8,0},{24,8},{16,24},{1,17},{9,1},{25,9},{17,25},{2,18},{10... | collective-permute-start | bytes 3145736 | tf_op jit(solution)/shard_map/ppermute | solution.py:221
  4.4 0.9 copy-done.1
  5.3 0.7 copy-done.2
  6.0 0.7 copy-done.3
  6.7 0.7 copy-done.4
  7.3 0.7 copy-done.5
  8.0 0.7 copy-done.6
  8.6 1.6 %shard_map.73 = (bf16[64,512]{1,0:T(8,128)(2,1)S(1)}, bf16[64,512]{1,0:T(8,128)(2,1)S(1)}, bf16[64,512]{1,0:T(8,128)(2,1)S(1)}, bf16[64,512]{1,0:T(8,128)(2,1)S(1)}) custom-call(s32[8]{0:T(128)S(1)} %copy-done.4, s32[8]{0:T(128)S(1)} %copy-done.5, s32[8]{0:T(128)S(1)} %copy-done.6, bf16[256,512]{1,0:T(8,128)(2,1)S(1)} %copy-done.1, f32[1,256]{1,0:T(1,128)S(1)} %bitcast.9, ...), custom_call_target="tpu_custom_call" | custom-call | flops 99999997952 | tf_op jit(solution)/shard_map/pallas_call | solution.py:101
  10.2 2.1 %collective-permute-start = (bf16[64,512]{1,0:T(8,128)(2,1)S(1)}, bf16[64,512]{1,0:T(8,128)(2,1)S(1)}, u32[]{:S(2)}, u32[]{:S(2)}) collective-permute-start(bf16[64,512]{1,0:T(8,128)(2,1)S(1)} %get-tuple-element.52), channel_id=1, source_target_pairs={{0,2},{1,3},{2,0},{3,1},{4,6},{5,7},{6,4},{7,5},{8,10},{9,11},{10,... | collective-permute-start | bytes 196616 | tf_op jit(solution)/shard_map/ppermute | solution.py:348
  12.3 2.6 %collective-permute-start.1 = (bf16[64,512]{1,0:T(8,128)(2,1)S(1)}, bf16[64,512]{1,0:T(8,128)(2,1)S(1)}, u32[]{:S(2)}, u32[]{:S(2)}) collective-permute-start(bf16[64,512]{1,0:T(8,128)(2,1)S(1)} %get-tuple-element.53), channel_id=1, source_target_pairs={{0,4},{1,5},{2,6},{3,7},{4,0},{5,1},{6,2},{7,3},{8,12},{9,13},{10,... | collective-permute-start | bytes 196616 | tf_op jit(solution)/shard_map/ppermute | solution.py:348
  14.9 4.1 %collective-permute-done.1.refs_2_ = bf16[64,512]{1,0:T(8,128)(2,1)S(1)} collective-permute-done((bf16[64,512]{1,0:T(8,128)(2,1)S(1)}, bf16[64,512]{1,0:T(8,128)(2,1)S(1)}, u32[]{:S(2)}, u32[]{:S(2)}) %collective-permute-start.1) | collective-permute-done | bytes 65568 | tf_op jit(solution)/shard_map/ppermute | solution.py:348
  19.0 2.0 %collective-permute-done.2.refs_3_ = bf16[64,512]{1,0:T(8,128)(2,1)S(1)} collective-permute-done((bf16[64,512]{1,0:T(8,128)(2,1)S(1)}, bf16[64,512]{1,0:T(8,128)(2,1)S(1)}, u32[]{:S(2)}, u32[]{:S(2)}) %collective-permute-start.2) | collective-permute-done | bytes 65568 | tf_op jit(solution)/shard_map/ppermute | solution.py:348
  21.0 1.5 %collective-permute-start.3 = (bf16[64,512]{1,0:T(8,128)(2,1)S(1)}, bf16[64,512]{1,0:T(8,128)(2,1)S(1)}, u32[]{:S(2)}, u32[]{:S(2)}) collective-permute-start(bf16[64,512]{1,0:T(8,128)(2,1)S(1)} %get-tuple-element.56), channel_id=1, source_target_pairs={{0,8},{8,24},{24,16},{16,0},{1,9},{9,25},{25,17},{17,1},{2,10},{10... | collective-permute-start | bytes 196616 | tf_op jit(solution)/shard_map/ppermute | solution.py:351
  22.6 1.5 %collective-permute-start.4 = (bf16[64,512]{1,0:T(8,128)(2,1)S(1)}, bf16[64,512]{1,0:T(8,128)(2,1)S(1)}, u32[]{:S(2)}, u32[]{:S(2)}) collective-permute-start(bf16[64,512]{1,0:T(8,128)(2,1)S(1)} %get-tuple-element.57), channel_id=1, source_target_pairs={{0,24},{8,16},{24,0},{16,8},{1,25},{9,17},{25,1},{17,9},{2,26},{10... | collective-permute-start | bytes 196616 | tf_op jit(solution)/shard_map/ppermute | solution.py:351
  24.1 1.5 %collective-permute-start.5 = (bf16[64,512]{1,0:T(8,128)(2,1)S(1)}, bf16[64,512]{1,0:T(8,128)(2,1)S(1)}, u32[]{:S(2)}, u32[]{:S(2)}) collective-permute-start(bf16[64,512]{1,0:T(8,128)(2,1)S(1)} %get-tuple-element.58), channel_id=1, source_target_pairs={{0,16},{8,0},{24,8},{16,24},{1,17},{9,1},{25,9},{17,25},{2,18},{10... | collective-permute-start | bytes 196616 | tf_op jit(solution)/shard_map/ppermute | solution.py:351
  25.5 0.4 shard_map.75
  26.0 3.0 %collective-permute-done.7.behind.refs_3_ = bf16[256,2048]{1,0:T(8,128)(2,1)S(1)} collective-permute-done((bf16[256,2048]{1,0:T(8,128)(2,1)S(1)}, bf16[256,2048]{1,0:T(8,128)(2,1)S(1)}, u32[]{:S(2)}, u32[]{:S(2)}) %collective-permute-start.7) | collective-permute-done | bytes 1048608 | tf_op jit(solution)/shard_map/ppermute | solution.py:221
  29.0 2.6 %collective-permute-start.15 = (bf16[256,3072]{1,0:T(8,128)(2,1)S(1)}, bf16[256,3072]{1,0:T(8,128)(2,1)S(1)}, u32[]{:S(2)}, u32[]{:S(2)}) collective-permute-start(bf16[256,3072]{1,0:T(8,128)(2,1)S(1)} %get-tuple-element.71), channel_id=1, source_target_pairs={{0,16},{8,0},{24,8},{16,24},{1,17},{9,1},{25,9},{17,25},{2,18},{10... | collective-permute-start | bytes 4718600 | tf_op jit(solution)/shard_map/ppermute | solution.py:221
  31.7 2.1 %collective-permute-done.4.refs_2_ = bf16[64,512]{1,0:T(8,128)(2,1)S(1)} collective-permute-done((bf16[64,512]{1,0:T(8,128)(2,1)S(1)}, bf16[64,512]{1,0:T(8,128)(2,1)S(1)}, u32[]{:S(2)}, u32[]{:S(2)}) %collective-permute-start.4) | collective-permute-done | bytes 65568 | tf_op jit(solution)/shard_map/ppermute | solution.py:351
  33.9 2.7 %collective-permute-start.8 = (bf16[1,4,64,512]{3,2,1,0:T(8,128)(2,1)S(1)}, bf16[1,4,64,512]{3,2,1,0:T(8,128)(2,1)S(1)}, u32[]{:S(2)}, u32[]{:S(2)}) collective-permute-start(bf16[1,4,64,512]{3,2,1,0:T(8,128)(2,1)S(1)} %bitcast.7), channel_id=1, source_target_pairs={{0,4},{1,5},{2,6},{3,7},{4,0},{5,1},{6,2},{7,3},{8,12},{9,13},{10,... | collective-permute-start | bytes 786440 | tf_op jit(solution)/shard_map/ppermute | solution.py:385
  36.5 9.3 %collective-permute-done.8.refs_1_ = bf16[1,4,64,512]{3,2,1,0:T(8,128)(2,1)S(1)} collective-permute-done((bf16[1,4,64,512]{3,2,1,0:T(8,128)(2,1)S(1)}, bf16[1,4,64,512]{3,2,1,0:T(8,128)(2,1)S(1)}, u32[]{:S(2)}, u32[]{:S(2)}) %collective-permute-start.8) | collective-permute-done | bytes 262176 | tf_op jit(solution)/shard_map/ppermute | solution.py:385
  45.9 0.7 collective-permute-start.9
  46.6 12.1 %collective-permute-done.9.refs_1_ = bf16[2,4,64,512]{3,2,1,0:T(8,128)(2,1)S(1)} collective-permute-done((bf16[2,4,64,512]{3,2,1,0:T(8,128)(2,1)S(1)}, bf16[2,4,64,512]{3,2,1,0:T(8,128)(2,1)S(1)}, u32[]{:S(2)}, u32[]{:S(2)}) %collective-permute-start.9) | collective-permute-done | bytes 524320 | tf_op jit(solution)/shard_map/ppermute | solution.py:390
  58.7 2.0 %collective-permute-start.13 = (bf16[128,2048]{1,0:T(8,128)(2,1)S(1)}, bf16[128,2048]{1,0:T(8,128)(2,1)S(1)}, u32[]{:S(2)}, u32[]{:S(2)}) collective-permute-start(bf16[128,2048]{1,0:T(8,128)(2,1)S(1)} %get-tuple-element.70), channel_id=1, source_target_pairs={{0,16},{8,0},{24,8},{16,24},{1,17},{9,1},{25,9},{17,25},{2,18},{10... | collective-permute-start | bytes 1572872 | tf_op jit(solution)/shard_map/ppermute | solution.py:258
  60.8 0.8 shard_map.79
  61.6 4.7 %shard_map.80 = (f32[1024,2048]{1,0:T(8,128)S(1)}, bf16[16,128]{1,0:T(8,128)(2,1)S(1)}) custom-call(bf16[1024,1024]{1,0:T(8,128)(2,1)S(1)} %get-tuple-element.66.refs_0_.weights.refs_1_, bf16[256,6144]{1,0:T(8,128)(2,1)S(1)} %copy-done, bf16[256,2048]{1,0:T(8,128)(2,1)S(1)} %collective-permute-done.6.ahead.refs_2_, ...), custom_call_target="tpu_custom_call" | custom-call | flops 1000000 | tf_op jit(solution)/shard_map/pallas_call | solution.py:297
  66.3 2.7 %collective-permute-done.14.refs_1_.refs_2_.ahead = bf16[256,3072]{1,0:T(8,128)(2,1)S(1)} collective-permute-done((bf16[256,3072]{1,0:T(8,128)(2,1)S(1)}, bf16[256,3072]{1,0:T(8,128)(2,1)S(1)}, u32[]{:S(2)}, u32[]{:S(2)}) %collective-permute-start.14) | collective-permute-done | bytes 1572896 | tf_op jit(solution)/shard_map/ppermute | solution.py:220
  69.4 1.8 %collective-permute-start.18 = (bf16[256,1024]{1,0:T(8,128)(2,1)S(1)}, bf16[256,1024]{1,0:T(8,128)(2,1)S(1)}, u32[]{:S(2)}, u32[]{:S(2)}) collective-permute-start(bf16[256,1024]{1,0:T(8,128)(2,1)S(1)} %get-tuple-element.81), channel_id=1, source_target_pairs={{0,8},{8,24},{24,16},{16,0},{1,9},{9,25},{25,17},{17,1},{2,10},{10... | collective-permute-start | bytes 1572872 | tf_op jit(solution)/shard_map/ppermute | solution.py:220
  71.2 4.9 %shard_map.82 = (f32[1024,1792]{1,0:T(8,128)S(1)}, bf16[16,128]{1,0:T(8,128)(2,1)S(1)}) custom-call(bf16[1024,1024]{1,0:T(8,128)(2,1)S(1)} %get-tuple-element.66.refs_0_.weights.refs_1_, bf16[256,6144]{1,0:T(8,128)(2,1)S(1)} %copy-done, bf16[256,3072]{1,0:T(8,128)(2,1)S(1)} %collective-permute-done.14.refs_1_.refs_2_.ahead, ...), custom_call_target="tpu_custom_call" | custom-call | flops 1000000 | tf_op jit(solution)/shard_map/pallas_call | solution.py:297
  76.2 3.6 %shard_map.83 = (f32[1024,1280]{1,0:T(8,128)S(1)}, bf16[16,128]{1,0:T(8,128)(2,1)S(1)}) custom-call(bf16[1024,1024]{1,0:T(8,128)(2,1)S(1)} %get-tuple-element.66.refs_0_.weights.refs_1_, bf16[256,6144]{1,0:T(8,128)(2,1)S(1)} %copy-done, bf16[256,3072]{1,0:T(8,128)(2,1)S(1)} %collective-permute-done.14.refs_1_.refs_2_.ahead, ...), custom_call_target="tpu_custom_call" | custom-call | flops 1000000 | tf_op jit(solution)/shard_map/pallas_call | solution.py:297
  79.8 0.4 collective-permute-done.12.refs_1_.refs_0_
  80.5 1.8 %collective-permute-start.16 = (bf16[112,1792]{1,0:T(8,128)(2,1)S(1)}, bf16[112,1792]{1,0:T(8,128)(2,1)S(1)}, u32[]{:S(2)}, u32[]{:S(2)}) collective-permute-start(bf16[112,1792]{1,0:T(8,128)(2,1)S(1)} %get-tuple-element.79), channel_id=1, source_target_pairs={{0,8},{8,24},{24,16},{16,0},{1,9},{9,25},{25,17},{17,1},{2,10},{10... | collective-permute-start | bytes 1204232 | tf_op jit(solution)/shard_map/ppermute | solution.py:258
  82.3 2.8 %shard_map.85 = (bf16[1024,6144]{1,0:T(8,128)(2,1)}, bf16[16,128]{1,0:T(8,128)(2,1)S(1)}) custom-call(f32[1024,2048]{1,0:T(8,128)S(1)} %get-tuple-element.68.near, bf16[1024,1024]{1,0:T(8,128)(2,1)S(1)} %get-tuple-element.66.refs_0_.weights.refs_1_, bf16[128,2048]{1,0:T(8,128)(2,1)S(1)} %collective-permute-done.12.refs_1_.refs_0_, ...), custom_call_target="tpu_custom_call" | custom-call | flops 1000000 | tf_op jit(solution)/shard_map/pallas_call | solution.py:322
  85.1 3.4 %collective-permute-done.19.refs_2_.refs_3_.behind = bf16[256,1024]{1,0:T(8,128)(2,1)S(1)} collective-permute-done((bf16[256,1024]{1,0:T(8,128)(2,1)S(1)}, bf16[256,1024]{1,0:T(8,128)(2,1)S(1)}, u32[]{:S(2)}, u32[]{:S(2)}) %collective-permute-start.19) | collective-permute-done | bytes 524320 | tf_op jit(solution)/shard_map/ppermute | solution.py:221
  88.5 2.9 %collective-permute-done.18.refs_1_.refs_2_.ahead = bf16[256,1024]{1,0:T(8,128)(2,1)S(1)} collective-permute-done((bf16[256,1024]{1,0:T(8,128)(2,1)S(1)}, bf16[256,1024]{1,0:T(8,128)(2,1)S(1)}, u32[]{:S(2)}, u32[]{:S(2)}) %collective-permute-start.18) | collective-permute-done | bytes 524320 | tf_op jit(solution)/shard_map/ppermute | solution.py:220
  91.4 0.4 shard_map.86
  91.9 2.0 %collective-permute-start.21 = (bf16[128,1280]{1,0:T(8,128)(2,1)S(1)}, bf16[128,1280]{1,0:T(8,128)(2,1)S(1)}, u32[]{:S(2)}, u32[]{:S(2)}) collective-permute-start(bf16[128,1280]{1,0:T(8,128)(2,1)S(1)} %get-tuple-element.89), channel_id=1, source_target_pairs={{0,16},{8,0},{24,8},{16,24},{1,17},{9,1},{25,9},{17,25},{2,18},{10... | collective-permute-start | bytes 983048 | tf_op jit(solution)/shard_map/ppermute | solution.py:258
  93.9 2.4 %shard_map.87 = (f32[1024,1024]{1,0:T(8,128)S(1)}, bf16[16,128]{1,0:T(8,128)(2,1)S(1)}) custom-call(bf16[1024,1024]{1,0:T(8,128)(2,1)S(1)} %get-tuple-element.66.refs_0_.weights.refs_1_, bf16[256,6144]{1,0:T(8,128)(2,1)S(1)} %copy-done, bf16[256,1024]{1,0:T(8,128)(2,1)S(1)} %collective-permute-done.18.refs_1_.refs_2_.ahead, ...), custom_call_target="tpu_custom_call" | custom-call | flops 1000000 | tf_op jit(solution)/shard_map/pallas_call | solution.py:297
  96.3 3.7 %collective-permute-done.16.refs_1_.refs_2_ = bf16[112,1792]{1,0:T(8,128)(2,1)S(1)} collective-permute-done((bf16[112,1792]{1,0:T(8,128)(2,1)S(1)}, bf16[112,1792]{1,0:T(8,128)(2,1)S(1)}, u32[]{:S(2)}, u32[]{:S(2)}) %collective-permute-start.16) | collective-permute-done | bytes 401440 | tf_op jit(solution)/shard_map/ppermute | solution.py:258
  100.1 1.5 %collective-permute-start.22 = (bf16[128,1024]{1,0:T(8,128)(2,1)S(1)}, bf16[128,1024]{1,0:T(8,128)(2,1)S(1)}, u32[]{:S(2)}, u32[]{:S(2)}) collective-permute-start(bf16[128,1024]{1,0:T(8,128)(2,1)S(1)} %get-tuple-element.93), channel_id=1, source_target_pairs={{0,8},{8,24},{24,16},{16,0},{1,9},{9,25},{25,17},{17,1},{2,10},{10... | collective-permute-start | bytes 786440 | tf_op jit(solution)/shard_map/ppermute | solution.py:258
  101.5 0.6 collective-permute-start.23
  102.2 2.6 %shard_map.89 = (bf16[1024,6144]{1,0:T(8,128)(2,1)}, bf16[16,128]{1,0:T(8,128)(2,1)S(1)}) custom-call(bf16[1024,6144]{1,0:T(8,128)(2,1)} %get-tuple-element.77._, f32[1024,1792]{1,0:T(8,128)S(1)} %get-tuple-element.78.refs_0_, bf16[1024,1024]{1,0:T(8,128)(2,1)S(1)} %get-tuple-element.66.refs_0_.weights.refs_1_, ...), custom_call_target="tpu_custom_call", output_to_operand_aliasing={{0}: (0, {})} | custom-call | flops 1000000 | tf_op jit(solution)/shard_map/pallas_call | solution.py:322
  104.7 1.6 %collective-permute-done.20.refs_2_ = bf16[128,1280]{1,0:T(8,128)(2,1)S(1)} collective-permute-done((bf16[128,1280]{1,0:T(8,128)(2,1)S(1)}, bf16[128,1280]{1,0:T(8,128)(2,1)S(1)}, u32[]{:S(2)}, u32[]{:S(2)}) %collective-permute-start.20) | collective-permute-done | bytes 327712 | tf_op jit(solution)/shard_map/ppermute | solution.py:258
  106.6 2.1 %shard_map.90 = (bf16[1024,6144]{1,0:T(8,128)(2,1)}, bf16[16,128]{1,0:T(8,128)(2,1)S(1)}) custom-call(bf16[1024,6144]{1,0:T(8,128)(2,1)} %get-tuple-element.86._, f32[1024,1280]{1,0:T(8,128)S(1)} %get-tuple-element.87.refs_0_, bf16[1024,1024]{1,0:T(8,128)(2,1)S(1)} %get-tuple-element.66.refs_0_.weights.refs_1_, ...), custom_call_target="tpu_custom_call", output_to_operand_aliasing={{0}: (0, {})} | custom-call | flops 1000000 | tf_op jit(solution)/shard_map/pallas_call | solution.py:322
  108.7 0.5 collective-permute-done.22.refs_2_
  109.2 1.0 collective-permute-done.23.refs_3_
  110.1 1.9 %shard_map.91 = (bf16[1024,6144]{1,0:T(8,128)(2,1)}, bf16[16,128]{1,0:T(8,128)(2,1)}) custom-call(bf16[1024,6144]{1,0:T(8,128)(2,1)} %get-tuple-element.91._, f32[1024,1024]{1,0:T(8,128)S(1)} %get-tuple-element.92.refs_0_, bf16[1024,1024]{1,0:T(8,128)(2,1)S(1)} %get-tuple-element.66.refs_0_.weights.refs_1_, ...), custom_call_target="tpu_custom_call", output_to_operand_aliasing={{0}: (0, {})} | custom-call | flops 1000000 | tf_op jit(solution)/shard_map/pallas_call | solution.py:322
  (34 shorter events, 1.4 us)
Async XLA Ops:
  1.3 27.7 %collective-permute-start.7 = (bf16[256,2048]{1,0:T(8,128)(2,1)S(1)}, bf16[256,2048]{1,0:T(8,128)(2,1)S(1)}, u32[]{:S(2)}, u32[]{:S(2)}) collective-permute-start(bf16[256,2048]{1,0:T(8,128)(2,1)S(1)} %slice.3.refs_6_), channel_id=1, source_target_pairs={{0,16},{8,0},{24,8},{16,24},{1,17},{9,1},{25,9},{17,25},{2,18},{10... | collective-permute-start | bytes 3145736 | tf_op jit(solution)/shard_map/ppermute | solution.py:221
  4.3 27.3 %collective-permute-start.6 = (bf16[256,2048]{1,0:T(8,128)(2,1)S(1)}, bf16[256,2048]{1,0:T(8,128)(2,1)S(1)}, u32[]{:S(2)}, u32[]{:S(2)}) collective-permute-start(bf16[256,2048]{1,0:T(8,128)(2,1)S(1)} %slice.3.refs_6_), channel_id=1, source_target_pairs={{0,8},{8,24},{24,16},{16,0},{1,9},{9,25},{25,17},{17,1},{2,10},{10... | collective-permute-start | bytes 3145736 | tf_op jit(solution)/shard_map/ppermute | solution.py:220
  4.4 0.9 copy-start.1
  5.3 0.7 copy-start.2
  6.0 0.7 copy-start.3
  6.7 0.7 copy-start.4
  7.3 0.7 copy-start.5
  8.0 0.7 copy-start.6
  8.6 16.9 %copy-start = (bf16[256,6144]{1,0:T(8,128)(2,1)S(1)}, bf16[256,6144]{1,0:T(8,128)(2,1)}, u32[]{:S(2)}) copy-start(bf16[256,6144]{1,0:T(8,128)(2,1)} %refs_1_.9) | copy-start | bytes 9437188
  10.2 4.7 %collective-permute-start = (bf16[64,512]{1,0:T(8,128)(2,1)S(1)}, bf16[64,512]{1,0:T(8,128)(2,1)S(1)}, u32[]{:S(2)}, u32[]{:S(2)}) collective-permute-start(bf16[64,512]{1,0:T(8,128)(2,1)S(1)} %get-tuple-element.52), channel_id=1, source_target_pairs={{0,2},{1,3},{2,0},{3,1},{4,6},{5,7},{6,4},{7,5},{8,10},{9,11},{10,... | collective-permute-start | bytes 196616 | tf_op jit(solution)/shard_map/ppermute | solution.py:348
  12.3 6.7 %collective-permute-start.1 = (bf16[64,512]{1,0:T(8,128)(2,1)S(1)}, bf16[64,512]{1,0:T(8,128)(2,1)S(1)}, u32[]{:S(2)}, u32[]{:S(2)}) collective-permute-start(bf16[64,512]{1,0:T(8,128)(2,1)S(1)} %get-tuple-element.53), channel_id=1, source_target_pairs={{0,4},{1,5},{2,6},{3,7},{4,0},{5,1},{6,2},{7,3},{8,12},{9,13},{10,... | collective-permute-start | bytes 196616 | tf_op jit(solution)/shard_map/ppermute | solution.py:348
  14.9 6.1 %collective-permute-start.2 = (bf16[64,512]{1,0:T(8,128)(2,1)S(1)}, bf16[64,512]{1,0:T(8,128)(2,1)S(1)}, u32[]{:S(2)}, u32[]{:S(2)}) collective-permute-start(bf16[64,512]{1,0:T(8,128)(2,1)S(1)} %get-tuple-element.54), channel_id=1, source_target_pairs={{0,6},{1,7},{2,4},{3,5},{4,2},{5,3},{6,0},{7,1},{8,14},{9,15},{10,... | collective-permute-start | bytes 196616 | tf_op jit(solution)/shard_map/ppermute | solution.py:348
  21.0 10.7 %collective-permute-start.3 = (bf16[64,512]{1,0:T(8,128)(2,1)S(1)}, bf16[64,512]{1,0:T(8,128)(2,1)S(1)}, u32[]{:S(2)}, u32[]{:S(2)}) collective-permute-start(bf16[64,512]{1,0:T(8,128)(2,1)S(1)} %get-tuple-element.56), channel_id=1, source_target_pairs={{0,8},{8,24},{24,16},{16,0},{1,9},{9,25},{25,17},{17,1},{2,10},{10... | collective-permute-start | bytes 196616 | tf_op jit(solution)/shard_map/ppermute | solution.py:351
  22.6 11.3 %collective-permute-start.4 = (bf16[64,512]{1,0:T(8,128)(2,1)S(1)}, bf16[64,512]{1,0:T(8,128)(2,1)S(1)}, u32[]{:S(2)}, u32[]{:S(2)}) collective-permute-start(bf16[64,512]{1,0:T(8,128)(2,1)S(1)} %get-tuple-element.57), channel_id=1, source_target_pairs={{0,24},{8,16},{24,0},{16,8},{1,25},{9,17},{25,1},{17,9},{2,26},{10... | collective-permute-start | bytes 196616 | tf_op jit(solution)/shard_map/ppermute | solution.py:351
  24.1 9.8 %collective-permute-start.5 = (bf16[64,512]{1,0:T(8,128)(2,1)S(1)}, bf16[64,512]{1,0:T(8,128)(2,1)S(1)}, u32[]{:S(2)}, u32[]{:S(2)}) collective-permute-start(bf16[64,512]{1,0:T(8,128)(2,1)S(1)} %get-tuple-element.58), channel_id=1, source_target_pairs={{0,16},{8,0},{24,8},{16,24},{1,17},{9,1},{25,9},{17,25},{2,18},{10... | collective-permute-start | bytes 196616 | tf_op jit(solution)/shard_map/ppermute | solution.py:351
  29.0 37.3 %collective-permute-start.15 = (bf16[256,3072]{1,0:T(8,128)(2,1)S(1)}, bf16[256,3072]{1,0:T(8,128)(2,1)S(1)}, u32[]{:S(2)}, u32[]{:S(2)}) collective-permute-start(bf16[256,3072]{1,0:T(8,128)(2,1)S(1)} %get-tuple-element.71), channel_id=1, source_target_pairs={{0,16},{8,0},{24,8},{16,24},{1,17},{9,1},{25,9},{17,25},{2,18},{10... | collective-permute-start | bytes 4718600 | tf_op jit(solution)/shard_map/ppermute | solution.py:221
  31.6 37.3 %collective-permute-start.14 = (bf16[256,3072]{1,0:T(8,128)(2,1)S(1)}, bf16[256,3072]{1,0:T(8,128)(2,1)S(1)}, u32[]{:S(2)}, u32[]{:S(2)}) collective-permute-start(bf16[256,3072]{1,0:T(8,128)(2,1)S(1)} %get-tuple-element.71), channel_id=1, source_target_pairs={{0,8},{8,24},{24,16},{16,0},{1,9},{9,25},{25,17},{17,1},{2,10},{10... | collective-permute-start | bytes 4718600 | tf_op jit(solution)/shard_map/ppermute | solution.py:220
  33.9 12.0 %collective-permute-start.8 = (bf16[1,4,64,512]{3,2,1,0:T(8,128)(2,1)S(1)}, bf16[1,4,64,512]{3,2,1,0:T(8,128)(2,1)S(1)}, u32[]{:S(2)}, u32[]{:S(2)}) collective-permute-start(bf16[1,4,64,512]{3,2,1,0:T(8,128)(2,1)S(1)} %bitcast.7), channel_id=1, source_target_pairs={{0,4},{1,5},{2,6},{3,7},{4,0},{5,1},{6,2},{7,3},{8,12},{9,13},{10,... | collective-permute-start | bytes 786440 | tf_op jit(solution)/shard_map/ppermute | solution.py:385
  45.9 12.8 %collective-permute-start.9 = (bf16[2,4,64,512]{3,2,1,0:T(8,128)(2,1)S(1)}, bf16[2,4,64,512]{3,2,1,0:T(8,128)(2,1)S(1)}, u32[]{:S(2)}, u32[]{:S(2)}) collective-permute-start(bf16[2,4,64,512]{3,2,1,0:T(8,128)(2,1)S(1)} %bitcast.4), channel_id=1, source_target_pairs={{0,2},{1,3},{2,0},{3,1},{4,6},{5,7},{6,4},{7,5},{8,10},{9,11},{10,... | collective-permute-start | bytes 1572872 | tf_op jit(solution)/shard_map/ppermute | solution.py:390
  46.6 12.1 %collective-permute-start.10 = (bf16[2,4,64,512]{3,2,1,0:T(8,128)(2,1)S(1)}, bf16[2,4,64,512]{3,2,1,0:T(8,128)(2,1)S(1)}, u32[]{:S(2)}, u32[]{:S(2)}) collective-permute-start(bf16[2,4,64,512]{3,2,1,0:T(8,128)(2,1)S(1)} %bitcast.5), channel_id=1, source_target_pairs={{0,1},{1,0},{2,3},{3,2},{4,5},{5,4},{6,7},{7,6},{8,9},{9,8},{10,11... | collective-permute-start | bytes 1572872 | tf_op jit(solution)/shard_map/ppermute | solution.py:395
  58.7 2.0 %collective-permute-start.11 = (bf16[2,4,64,512]{3,2,1,0:T(8,128)(2,1)S(1)}, bf16[2,4,64,512]{3,2,1,0:T(8,128)(2,1)S(1)}, u32[]{:S(2)}, u32[]{:S(2)}) collective-permute-start(bf16[2,4,64,512]{3,2,1,0:T(8,128)(2,1)S(1)} %collective-permute-done.9.refs_1_), channel_id=1, source_target_pairs={{0,1},{1,0},{2,3},{3,2},{4,5},{5,4},{6,7},{7,6},{8,9},{9,8},{10,11... | collective-permute-start | bytes 1572872 | tf_op jit(solution)/shard_map/ppermute | solution.py:395
  58.7 21.5 %collective-permute-start.12 = (bf16[128,2048]{1,0:T(8,128)(2,1)S(1)}, bf16[128,2048]{1,0:T(8,128)(2,1)S(1)}, u32[]{:S(2)}, u32[]{:S(2)}) collective-permute-start(bf16[128,2048]{1,0:T(8,128)(2,1)S(1)} %get-tuple-element.69), channel_id=1, source_target_pairs={{0,8},{8,24},{24,16},{16,0},{1,9},{9,25},{25,17},{17,1},{2,10},{10... | collective-permute-start | bytes 1572872 | tf_op jit(solution)/shard_map/ppermute | solution.py:258
  58.7 21.5 %collective-permute-start.13 = (bf16[128,2048]{1,0:T(8,128)(2,1)S(1)}, bf16[128,2048]{1,0:T(8,128)(2,1)S(1)}, u32[]{:S(2)}, u32[]{:S(2)}) collective-permute-start(bf16[128,2048]{1,0:T(8,128)(2,1)S(1)} %get-tuple-element.70), channel_id=1, source_target_pairs={{0,16},{8,0},{24,8},{16,24},{1,17},{9,1},{25,9},{17,25},{2,18},{10... | collective-permute-start | bytes 1572872 | tf_op jit(solution)/shard_map/ppermute | solution.py:258
  69.1 19.4 %collective-permute-start.19 = (bf16[256,1024]{1,0:T(8,128)(2,1)S(1)}, bf16[256,1024]{1,0:T(8,128)(2,1)S(1)}, u32[]{:S(2)}, u32[]{:S(2)}) collective-permute-start(bf16[256,1024]{1,0:T(8,128)(2,1)S(1)} %get-tuple-element.81), channel_id=1, source_target_pairs={{0,16},{8,0},{24,8},{16,24},{1,17},{9,1},{25,9},{17,25},{2,18},{10... | collective-permute-start | bytes 1572872 | tf_op jit(solution)/shard_map/ppermute | solution.py:221
  69.4 22.0 %collective-permute-start.18 = (bf16[256,1024]{1,0:T(8,128)(2,1)S(1)}, bf16[256,1024]{1,0:T(8,128)(2,1)S(1)}, u32[]{:S(2)}, u32[]{:S(2)}) collective-permute-start(bf16[256,1024]{1,0:T(8,128)(2,1)S(1)} %get-tuple-element.81), channel_id=1, source_target_pairs={{0,8},{8,24},{24,16},{16,0},{1,9},{9,25},{25,17},{17,1},{2,10},{10... | collective-permute-start | bytes 1572872 | tf_op jit(solution)/shard_map/ppermute | solution.py:220
  80.3 19.8 %collective-permute-start.17 = (bf16[144,1792]{1,0:T(8,128)(2,1)S(1)}, bf16[144,1792]{1,0:T(8,128)(2,1)S(1)}, u32[]{:S(2)}, u32[]{:S(2)}) collective-permute-start(bf16[144,1792]{1,0:T(8,128)(2,1)S(1)} %get-tuple-element.80), channel_id=1, source_target_pairs={{0,16},{8,0},{24,8},{16,24},{1,17},{9,1},{25,9},{17,25},{2,18},{10... | collective-permute-start | bytes 1548296 | tf_op jit(solution)/shard_map/ppermute | solution.py:258
  80.5 19.5 %collective-permute-start.16 = (bf16[112,1792]{1,0:T(8,128)(2,1)S(1)}, bf16[112,1792]{1,0:T(8,128)(2,1)S(1)}, u32[]{:S(2)}, u32[]{:S(2)}) collective-permute-start(bf16[112,1792]{1,0:T(8,128)(2,1)S(1)} %get-tuple-element.79), channel_id=1, source_target_pairs={{0,8},{8,24},{24,16},{16,0},{1,9},{9,25},{25,17},{17,1},{2,10},{10... | collective-permute-start | bytes 1204232 | tf_op jit(solution)/shard_map/ppermute | solution.py:258
  91.8 14.5 %collective-permute-start.20 = (bf16[128,1280]{1,0:T(8,128)(2,1)S(1)}, bf16[128,1280]{1,0:T(8,128)(2,1)S(1)}, u32[]{:S(2)}, u32[]{:S(2)}) collective-permute-start(bf16[128,1280]{1,0:T(8,128)(2,1)S(1)} %get-tuple-element.88), channel_id=1, source_target_pairs={{0,8},{8,24},{24,16},{16,0},{1,9},{9,25},{25,17},{17,1},{2,10},{10... | collective-permute-start | bytes 983048 | tf_op jit(solution)/shard_map/ppermute | solution.py:258
  91.9 14.7 %collective-permute-start.21 = (bf16[128,1280]{1,0:T(8,128)(2,1)S(1)}, bf16[128,1280]{1,0:T(8,128)(2,1)S(1)}, u32[]{:S(2)}, u32[]{:S(2)}) collective-permute-start(bf16[128,1280]{1,0:T(8,128)(2,1)S(1)} %get-tuple-element.89), channel_id=1, source_target_pairs={{0,16},{8,0},{24,8},{16,24},{1,17},{9,1},{25,9},{17,25},{2,18},{10... | collective-permute-start | bytes 983048 | tf_op jit(solution)/shard_map/ppermute | solution.py:258
  100.1 9.1 %collective-permute-start.22 = (bf16[128,1024]{1,0:T(8,128)(2,1)S(1)}, bf16[128,1024]{1,0:T(8,128)(2,1)S(1)}, u32[]{:S(2)}, u32[]{:S(2)}) collective-permute-start(bf16[128,1024]{1,0:T(8,128)(2,1)S(1)} %get-tuple-element.93), channel_id=1, source_target_pairs={{0,8},{8,24},{24,16},{16,0},{1,9},{9,25},{25,17},{17,1},{2,10},{10... | collective-permute-start | bytes 786440 | tf_op jit(solution)/shard_map/ppermute | solution.py:258
  101.5 8.6 %collective-permute-start.23 = (bf16[128,1024]{1,0:T(8,128)(2,1)S(1)}, bf16[128,1024]{1,0:T(8,128)(2,1)S(1)}, u32[]{:S(2)}, u32[]{:S(2)}) collective-permute-start(bf16[128,1024]{1,0:T(8,128)(2,1)S(1)} %get-tuple-element.94), channel_id=1, source_target_pairs={{0,16},{8,0},{24,8},{16,24},{1,17},{9,1},{25,9},{17,25},{2,18},{10... | collective-permute-start | bytes 786440 | tf_op jit(solution)/shard_map/ppermute | solution.py:258
